TPU v7x, 32 devices: a whole 2x2x4 slice. The times are simulated.
32 devices in a mesh: db: 8 (over z, y), section: 2 (over core), mp: 2 (over x).
Axes of the slice: x: 2, y: 2, z: 4, core: 2. Of those that a mesh axis runs over, the one named last changes fastest.
Arguments:
- hidden_in: bfloat16 [4096, 4096], P('db', 'mp'), may hold values from -24 to 24
- database: bfloat16 [32, 128, 896], P('db'), may hold values from -8.5 to 8.5
- neighbour_ids: int32 [64, 2], replicated, may hold values from 0 to 31, as said below
- enc_gain: float32 [896], replicated, may hold values from 0.1 to 1.9
- enc_up: bfloat16 [896, 2048], P(None, ('section', 'mp')), may hold values from -0.1875 to 0.1875
- enc_down: bfloat16 [2048, 896], P(('section', 'mp')), may hold values from -0.125 to 0.125
- dec_gain: float32 [2, 4096], P('section'), may hold values from 0.1 to 1.9
- w_query: bfloat16 [2, 4096, 2048], P('section', None, 'mp'), may hold values from -0.06328125 to 0.06328125
- w_key: bfloat16 [2, 896, 2048], P('section', None, 'mp'), may hold values from -0.135301004 to 0.135301004
- w_value: bfloat16 [2, 896, 2048], P('section', None, 'mp'), may hold values from -0.1875 to 0.1875
- w_out: bfloat16 [2, 2048, 4096], P('section', 'mp'), may hold values from -0.125 to 0.125
Outputs:
- hidden_out: bfloat16 [4096, 4096], P(('db', 'section'), 'mp')
Inputs may be any that keep to these rules, and one draw needn't show every extreme that they name: `neighbour_ids`: block id b is held by db index b // 4. The 16 ids in the rows of one db index name at most 2 blocks of any one holder, and in every draw one holder is named exactly 2 times by every db index.
All inputs are finite; a program needn't handle non-finite values.
Results may differ from a plain program's by a relative error of at most 0.015.
Values may be sent and summed in bfloat16 or wider, within the bound.
A program may use at most 128 MiB of HBM per device.

v0:
```python
import jax
import jax.numpy as jnp
from jax import lax
from jax.sharding import PartitionSpec as P

HD = 128
E = 896
NEIGH = 2
QBLOCK = 64
NBLOCK = 128


def from_behind(block, axis, distance):
    devices = range(lax.axis_size(axis))
    route = [(i - distance, i) for i in devices if i - distance in devices]
    return lax.ppermute(block, axis, route)


def rms_scale(rows_in, gain_vec):
    return (
        rows_in * lax.rsqrt(jnp.mean(rows_in * rows_in, axis=-1, keepdims=True) + 1e-06) * gain_vec
    )


def encoder_terms(floats, enc_gain, enc_up, enc_down):
    normed = rms_scale(floats, enc_gain).astype(jnp.bfloat16)
    inner_act = jax.nn.gelu(
        jnp.dot(normed, enc_up, preferred_element_type=jnp.float32), approximate=True
    ).astype(jnp.bfloat16)
    return jnp.dot(inner_act, enc_down, preferred_element_type=jnp.float32)


def cross_layer(state_rows, blocks, gain_vec, query_w, key_w, value_w, out_w):
    block_count = blocks.shape[0]
    whole_rows = lax.all_gather(state_rows, "mp", axis=1, tiled=True)
    floats = whole_rows.astype(jnp.float32)
    normed = rms_scale(floats, gain_vec).astype(jnp.bfloat16)
    queries = (jnp.dot(normed, query_w, preferred_element_type=jnp.float32) * HD ** (-0.5)).astype(
        jnp.bfloat16
    )
    flat_rows = blocks.reshape(-1, E)
    key_rows = jnp.dot(flat_rows, key_w, preferred_element_type=jnp.float32).astype(jnp.bfloat16)
    value_rows = jnp.dot(flat_rows, value_w, preferred_element_type=jnp.float32).astype(
        jnp.bfloat16
    )
    head_count = query_w.shape[1] // HD
    query_four = queries.reshape(block_count, QBLOCK, head_count, HD)
    key_four = key_rows.reshape(block_count, NEIGH * NBLOCK, head_count, HD)
    value_four = value_rows.reshape(block_count, NEIGH * NBLOCK, head_count, HD)
    scores = jnp.einsum("cqhd,ckhd->chqk", query_four, key_four, preferred_element_type=jnp.float32)
    soft_weights = jax.nn.softmax(scores, axis=-1).astype(jnp.bfloat16)
    context = jnp.einsum(
        "chqk,ckhd->cqhd", soft_weights, value_four, preferred_element_type=jnp.float32
    )
    context = context.astype(jnp.bfloat16).reshape(block_count * QBLOCK, head_count * HD)
    partial_out = jnp.dot(context, out_w, preferred_element_type=jnp.float32)
    head_share = lax.psum_scatter(partial_out, "mp", scatter_dimension=1, tiled=True)
    return (state_rows.astype(jnp.float32) + head_share).astype(jnp.bfloat16)


def body(
    hidden_in,
    database,
    neighbour_ids,
    enc_gain,
    enc_up,
    enc_down,
    dec_gain,
    w_query,
    w_key,
    w_value,
    w_out,
):
    db_count = lax.axis_size("db")
    db_index = lax.axis_index("db")
    blocks_held = database.shape[0]
    request = neighbour_ids.shape[0] // db_count * NEIGH
    capacity = max(2, (request + db_count - 1) // db_count)
    id_table = neighbour_ids.reshape(db_count, request)
    owners = id_table // blocks_held
    within = id_table % blocks_held
    places = jnp.arange(request)
    same_owner = owners[:, :, None] == owners[:, None, :]
    earlier = places[None, :, None] > places[None, None, :]
    rank_in = jnp.sum((same_owner & earlier).astype(jnp.int32), axis=-1)
    slot_ids = jnp.arange(capacity)
    matches = (owners[:, None, :] == db_index) & (rank_in[:, None, :] == slot_ids[None, :, None])
    send_local = jnp.sum(matches.astype(jnp.int32) * within[:, None, :], axis=-1)
    my_owner = lax.dynamic_index_in_dim(owners, db_index, 0, keepdims=False)
    my_rank = lax.dynamic_index_in_dim(rank_in, db_index, 0, keepdims=False)
    slot_pick = my_owner * capacity + my_rank
    payload = database[send_local]
    received = lax.all_to_all(payload, "db", split_axis=0, concat_axis=0, tiled=True)
    fetched = received.reshape(db_count * capacity, NBLOCK, E)[slot_pick]
    fetched_floats = fetched.reshape(-1, E).astype(jnp.float32)
    fetched_terms = lax.psum(
        encoder_terms(fetched_floats, enc_gain, enc_up, enc_down), ("section", "mp")
    )
    encoded = (fetched_floats + fetched_terms).astype(jnp.bfloat16)
    query_blocks = request // NEIGH
    enc_blocks = encoded.reshape(query_blocks, NEIGH * NBLOCK, E)
    segments = lax.axis_size("section")
    segment_index = lax.axis_index("section")
    micro_tokens = hidden_in.shape[0] // segments
    micro_blocks = micro_tokens // QBLOCK
    arrived = jnp.zeros((micro_tokens, hidden_in.shape[1]), jnp.bfloat16)
    finished = []
    for turn_id in range(2 * segments - 1):
        start_row = min(turn_id, segments - 1) * micro_tokens
        entering = hidden_in[start_row : start_row + micro_tokens]
        current = jnp.where(segment_index == 0, entering, arrived)
        micro_pick = jnp.clip(turn_id - segment_index, 0, segments - 1)
        neighbours = lax.dynamic_slice_in_dim(
            enc_blocks, micro_pick * micro_blocks, micro_blocks, 0
        )
        leaving = cross_layer(
            current, neighbours, dec_gain[0], w_query[0], w_key[0], w_value[0], w_out[0]
        )
        if turn_id >= segments - 1:
            finished.append(leaving)
        if turn_id < 2 * segments - 2:
            arrived = from_behind(leaving, "section", 1)
    result = finished[segments - 1]
    moved_rows = from_behind(finished[0], "section", 0 - (segments - 1))
    result = jnp.where(segment_index == 0, moved_rows, result)
    return result


def solution(mesh):
    in_specs = (
        P("db", "mp"),
        P("db", None, None),
        P(),
        P(),
        P(None, ("section", "mp")),
        P(("section", "mp"), None),
        P("section", None),
        P("section", None, "mp"),
        P("section", None, "mp"),
        P("section", None, "mp"),
        P("section", "mp", None),
    )
    out_specs = P(("db", "section"), "mp")
    return jax.shard_map(body, mesh=mesh, in_specs=in_specs, out_specs=out_specs, check_vma=False)
```

profile of v0, /device:TPU:0, one launch (start us, length us, event | category | flops | bytes accessed | tf_op | source)
XLA Modules:
  0.0 599.1 jit_solution(4454183093159074193)
XLA Ops:
  7.4 0.9 copy.37
  9.0 4.0 gather_fusion
  13.0 7.3 %all-to-all-start = ((bf16[8,2,128,896]{3,2,1,0:T(8,128)(2,1)}), bf16[8,2,128,896]{3,2,1,0:T(8,128)(2,1)}, u32[]{:S(2)}, u32[]{:S(2)}) async-start(bf16[8,2,128,896]{3,2,1,0:T(8,128)(2,1)} %bitcast.145), calls=%async_computation | async-start | bytes 7340032 | tf_op jit(solution)/shard_map/all_to_all | solution.py:93
  20.3 2.3 slice_select_fusion
  22.7 79.6 %all-to-all-done = bf16[8,2,128,896]{3,2,1,0:T(8,128)(2,1)} async-done(((bf16[8,2,128,896]{3,2,1,0:T(8,128)(2,1)}), bf16[8,2,128,896]{3,2,1,0:T(8,128)(2,1)}, u32[]{:S(2)}, u32[]{:S(2)}) %all-to-all-start) | async-done | bytes 3670048 | tf_op jit(solution)/shard_map/all_to_all | solution.py:93
  102.3 4.8 gather_fusion.1
  107.1 3.0 fusion.15
  110.3 2.7 fusion.17
  113.0 10.4 %fusion.36 = f32[2048,896]{1,0:T(8,128)} fusion(bf16[512,896]{1,0:T(8,128)(2,1)S(1)} %copy-done.21, bf16[2048,896]{1,0:T(8,128)(2,1)} %fusion.17, bf16[896,512]{1,0:T(8,128)(2,1)} %param.15), kind=kOutput, calls=%fused_computation.48 | convolution fusion | flops 3767533568 | bytes 12845056 | tf_op jit(solution)/shard_map/dot_general | solution.py:30
  123.7 2.2 fusion.19
  126.0 7.1 %fusion.108 = bf16[32,8,8,128]{3,1,2,0:T(8,128)(2,1)S(1)} fusion(bf16[1,4096,1024]{2,1,0:T(8,128)(2,1)} %param.18, bf16[256,4096]{1,0:T(8,128)(2,1)S(1)} %copy-done.11, f32[4096]{0:T(1024)S(1)} %bitcast.164, f32[256]{0:T(256)S(1)} %add_rsqrt_fusion.2), kind=kOutput, calls=%fused_computation.101 | convolution fusion | flops 2152202240 | bytes 11027456 | tf_op jit(solution)/shard_map/dot_general | solution.py:38
  133.2 125.8 %all-reduce.2.cloned.1.call-done = f32[2048,896]{1,0:T(8,128)} async-done(((f32[2048,896]{1,0:T(8,128)}), f32[2048,896]{1,0:T(8,128)}) %all-reduce.2.cloned.1.call-update) | async-done | bytes 7340048 | tf_op jit(solution)/shard_map/psum | solution.py:96
  259.0 4.8 fusion.18
  263.9 2.3 constant_dynamic-slice_fusion.4
  266.2 2.3 convert_bitcast_fusion.4
  268.6 0.6 copy.52
  269.2 0.8 fusion.51
  270.1 1.3 copy-done.8
  271.4 0.6 fusion.158
  272.0 0.9 copy-done.18
  272.9 2.3 convert_bitcast_fusion.5
  275.2 2.0 copy.53
  277.2 6.5 %fusion.129 = bf16[4,64,8,128]{3,1,2,0:T(8,128)(2,1)S(1)} fusion(bf16[4,256,8,128]{3,2,1,0:T(8,128)(2,1)} %bitcast.157, f32[4,8,64]{2,1,0:T(8,128)S(1)} %fusion.158, f32[4,8,64,256]{3,2,1,0:T(8,128)} %copy-done.8), kind=kOutput, calls=%fused_computation.106 | convolution fusion | flops 136055040 | bytes 4726784 | tf_op jit(solution)/shard_map/chqk,ckhd->cqhd/dot_general | solution.py:52
  284.1 7.6 %fusion.7 = f32[256,4096]{1,0:T(8,128)} fusion(bf16[1,1024,4096]{2,1,0:T(8,128)(2,1)} %param.21, bf16[32,8,8,128]{3,2,1,0:T(8,128)(2,1)S(1)} %bitcast.152), kind=kOutput, calls=%fused_computation.9 | convolution fusion | flops 2147483648 | bytes 13107200 | tf_op jit(solution)/shard_map/dot_general | solution.py:56
  291.8 54.7 %reduce-scatter.4.cloned.1.call-done = f32[256,2048]{1,0:T(8,128)} async-done(((f32[256,4096]{1,0:T(8,128)}), f32[256,2048]{1,0:T(8,128)}) %reduce-scatter.4.cloned.1.call-update) | async-done | bytes 2097168 | tf_op jit(solution)/shard_map/reduce_scatter | solution.py:57
  346.4 2.3 add_convert_fusion.2
  348.7 1.8 collective-permute-start
  350.6 2.2 collective-permute-done
  352.8 1.1 broadcast_select_fusion.1
  354.4 3.8 convert_bitcast_fusion.2
  358.2 2.0 copy.56
  360.2 0.9 copy-done.19
  361.1 2.3 convert_bitcast_fusion.3
  363.4 1.9 copy.57
  365.3 21.9 %all-gather.6.cloned.1.call-done = bf16[256,4096]{1,0:T(8,128)(2,1)} async-done(((bf16[256,2048]{1,0:T(8,128)(2,1)}), bf16[256,4096]{1,0:T(8,128)(2,1)}) %all-gather.6.cloned.1.call-update) | async-done | bytes 2097168 | tf_op jit(solution)/shard_map/all_gather | solution.py:35
  387.2 2.2 fusion.22
  389.5 5.9 fusion.113
  395.5 0.8 fusion.47
  396.4 1.3 copy-done.9
  397.7 0.6 fusion.159
  398.3 6.5 %fusion.126 = bf16[4,64,8,128]{3,1,2,0:T(8,128)(2,1)S(1)} fusion(bf16[4,256,8,128]{3,2,1,0:T(8,128)(2,1)} %bitcast.155, f32[4,8,64]{2,1,0:T(8,128)S(1)} %fusion.159, f32[4,8,64,256]{3,2,1,0:T(8,128)} %copy-done.9), kind=kOutput, calls=%fused_computation.105 | convolution fusion | flops 136055040 | bytes 4726784 | tf_op jit(solution)/shard_map/chqk,ckhd->cqhd/dot_general | solution.py:52
  405.2 7.6 %fusion.5 = f32[256,4096]{1,0:T(8,128)} fusion(bf16[1,1024,4096]{2,1,0:T(8,128)(2,1)} %param.21, bf16[32,8,8,128]{3,2,1,0:T(8,128)(2,1)S(1)} %bitcast.153), kind=kOutput, calls=%fused_computation.7 | convolution fusion | flops 2147483648 | bytes 13107200 | tf_op jit(solution)/shard_map/dot_general | solution.py:56
  412.9 54.4 %reduce-scatter.6.cloned.1.call-done = f32[256,2048]{1,0:T(8,128)} async-done(((f32[256,4096]{1,0:T(8,128)}), f32[256,2048]{1,0:T(8,128)}) %reduce-scatter.6.cloned.1.call-update) | async-done | bytes 2097168 | tf_op jit(solution)/shard_map/reduce_scatter | solution.py:57
  467.4 2.0 add_convert_fusion.1
  469.4 1.8 collective-permute-start.2
  471.2 2.2 collective-permute-done.2
  473.4 1.2 broadcast_select_fusion
  474.9 3.8 convert_bitcast_fusion
  478.7 2.0 copy.60
  480.7 0.9 copy-done.20
  481.6 2.3 convert_bitcast_fusion.1
  483.9 1.9 copy.61
  485.8 22.1 %all-gather.8.cloned.1.call-done = bf16[256,4096]{1,0:T(8,128)(2,1)} async-done(((bf16[256,2048]{1,0:T(8,128)(2,1)}), bf16[256,4096]{1,0:T(8,128)(2,1)}) %all-gather.8.cloned.1.call-update) | async-done | bytes 2097168 | tf_op jit(solution)/shard_map/all_gather | solution.py:35
  507.9 2.2 fusion.25
  510.2 5.9 fusion.118
  516.2 0.8 fusion.43
  517.1 1.3 copy-done.10
  518.5 0.6 fusion.160
  519.1 6.5 %fusion.123 = bf16[4,64,8,128]{3,1,2,0:T(8,128)(2,1)S(1)} fusion(bf16[4,256,8,128]{3,2,1,0:T(8,128)(2,1)} %bitcast.156, f32[4,8,64]{2,1,0:T(8,128)S(1)} %fusion.160, f32[4,8,64,256]{3,2,1,0:T(8,128)} %copy-done.10), kind=kOutput, calls=%fused_computation.104 | convolution fusion | flops 136055040 | bytes 4726784 | tf_op jit(solution)/shard_map/chqk,ckhd->cqhd/dot_general | solution.py:52
  526.0 7.6 %fusion.3 = f32[256,4096]{1,0:T(8,128)} fusion(bf16[1,1024,4096]{2,1,0:T(8,128)(2,1)} %param.21, bf16[32,8,8,128]{3,2,1,0:T(8,128)(2,1)S(1)} %bitcast.154), kind=kOutput, calls=%fused_computation.5 | convolution fusion | flops 2147483648 | bytes 13107200 | tf_op jit(solution)/shard_map/dot_general | solution.py:56
  533.6 1.4 collective-permute-start.1
  535.1 3.6 collective-permute-done.1
  538.7 49.4 %reduce-scatter.8.cloned.1.call-done = f32[256,2048]{1,0:T(8,128)} async-done(((f32[256,4096]{1,0:T(8,128)}), f32[256,2048]{1,0:T(8,128)}) %reduce-scatter.8.cloned.1.call-update) | async-done | bytes 2097168 | tf_op jit(solution)/shard_map/reduce_scatter | solution.py:57
  588.1 3.4 fusion.132
  (77 shorter events, 3.5 us)
Async XLA Ops:
  7.4 258.8 %copy-start = (bf16[1,896,1024]{2,1,0:T(8,128)(2,1)S(1)}, bf16[1,896,1024]{2,1,0:T(8,128)(2,1)}, u32[]{:S(2)}) copy-start(bf16[1,896,1024]{2,1,0:T(8,128)(2,1)} %param.19) | copy-start | bytes 5505028
  13.0 89.3 %all-to-all-start = ((bf16[8,2,128,896]{3,2,1,0:T(8,128)(2,1)}), bf16[8,2,128,896]{3,2,1,0:T(8,128)(2,1)}, u32[]{:S(2)}, u32[]{:S(2)}) async-start(bf16[8,2,128,896]{3,2,1,0:T(8,128)(2,1)} %bitcast.145), calls=%async_computation | async-start | bytes 7340032 | tf_op jit(solution)/shard_map/all_to_all | solution.py:93
  20.3 103.4 %all-gather.4.cloned.1.call-start = ((), (), s32[]{:S(2)}) async-start(), calls=%async_computation.5 | async-start | bytes 3145728 | tf_op jit(solution)/shard_map/all_gather | solution.py:35
  22.6 236.4 %all-reduce.2.cloned.1.call-start = ((), (), s32[]{:S(2)}) async-start(), calls=%async_computation.4 | async-start | bytes 14680064 | tf_op jit(solution)/shard_map/psum | solution.py:96
  107.1 3.1 copy-start.1
  107.1 3.1 copy-start.17
  110.3 2.7 copy-start.21
  123.5 2.5 copy-start.22
  123.5 223.0 %reduce-scatter.4.cloned.1.call-start = ((), (), s32[]{:S(2)}) async-start(), calls=%async_computation.6 | async-start | bytes 6291456 | tf_op jit(solution)/shard_map/reduce_scatter | solution.py:57
  123.7 2.3 copy-start.11
  270.1 1.3 copy-start.8
  271.4 1.5 copy-start.18
  291.7 95.5 %all-gather.6.cloned.1.call-start = ((), (), s32[]{:S(2)}) async-start(), calls=%async_computation.7 | async-start | bytes 3145728 | tf_op jit(solution)/shard_map/all_gather | solution.py:35
  346.4 6.3 %copy-start.4 = (bf16[512,2048]{1,0:T(8,128)(2,1)S(1)}, bf16[512,2048]{1,0:T(8,128)(2,1)}, u32[]{:S(2)}) copy-start(bf16[512,2048]{1,0:T(8,128)(2,1)} %param.11) | copy-start | bytes 6291460
  348.7 4.0 collective-permute-start
  353.9 113.5 %reduce-scatter.6.cloned.1.call-start = ((), (), s32[]{:S(2)}) async-start(), calls=%async_computation.8 | async-start | bytes 6291456 | tf_op jit(solution)/shard_map/reduce_scatter | solution.py:57
  358.2 2.0 copy-start.15
  358.2 2.9 copy-start.19
  387.2 2.2 copy-start.13
  389.5 6.0 %copy-start.6 = (bf16[128,8,8,128]{3,2,1,0:T(8,128)(2,1)S(1)}, bf16[128,8,8,128]{3,2,1,0:T(8,128)(2,1)}, u32[]{:S(2)}) copy-start(bf16[128,8,8,128]{3,2,1,0:T(8,128)(2,1)} %copy.56) | copy-start | bytes 6291460
  396.4 1.4 copy-start.9
  412.9 54.5 %copy-start.3 = (bf16[256,2048]{1,0:T(8,128)(2,1)S(1)}, bf16[256,2048]{1,0:T(8,128)(2,1)}, u32[]{:S(2)}) copy-start(bf16[256,2048]{1,0:T(8,128)(2,1)} %broadcast_select_fusion.1) | copy-start | bytes 3145732
  412.9 95.1 %all-gather.8.cloned.1.call-start = ((), (), s32[]{:S(2)}) async-start(), calls=%async_computation.9 | async-start | bytes 3145728 | tf_op jit(solution)/shard_map/all_gather | solution.py:35
  467.4 6.1 %copy-start.5 = (bf16[512,2048]{1,0:T(8,128)(2,1)S(1)}, bf16[512,2048]{1,0:T(8,128)(2,1)}, u32[]{:S(2)}) copy-start(bf16[512,2048]{1,0:T(8,128)(2,1)} %param.11) | copy-start | bytes 6291460
  469.4 4.0 copy-start.16
  469.4 4.0 collective-permute-start.2
  474.6 113.4 %reduce-scatter.8.cloned.1.call-start = ((), (), s32[]{:S(2)}) async-start(), calls=%async_computation.10 | async-start | bytes 6291456 | tf_op jit(solution)/shard_map/reduce_scatter | solution.py:57
  478.7 2.0 copy-start.14
  478.7 2.9 copy-start.20
  507.9 2.2 copy-start.12
  510.2 6.0 %copy-start.7 = (bf16[128,8,8,128]{3,2,1,0:T(8,128)(2,1)S(1)}, bf16[128,8,8,128]{3,2,1,0:T(8,128)(2,1)}, u32[]{:S(2)}) copy-start(bf16[128,8,8,128]{3,2,1,0:T(8,128)(2,1)} %copy.60) | copy-start | bytes 6291460
  517.1 1.4 copy-start.10
  533.6 54.5 %copy-start.2 = (bf16[256,2048]{1,0:T(8,128)(2,1)S(1)}, bf16[256,2048]{1,0:T(8,128)(2,1)}, u32[]{:S(2)}) copy-start(bf16[256,2048]{1,0:T(8,128)(2,1)} %broadcast_select_fusion) | copy-start | bytes 3145732
  533.6 5.0 collective-permute-start.1
Sparse Core Ops, SparseCore 0:
  22.7 34.4 all-gather.3
  291.9 54.5 reduce-scatter.3
  354.0 33.1 all-gather.5
  413.0 54.3 reduce-scatter.5
  474.8 33.1 all-gather.7
  533.7 54.2 reduce-scatter.7
Sparse Core Ops, SparseCore 1:
  123.5 135.4 all-reduce.1
where the time goes:
time: 606 us; the launch traced here: 599 us
  waiting for transfers between devices  416 us (69%)
  matrix products  91.4 us (15%)
  other arithmetic  31.8 us (5%)
  local copies, waits for them, and re-layouts  30.8 us (5%)
  between operations  15.6 us (3%)
  starting transfers between devices  13.4 us (2%)
    reduce_scatter x3, waiting for transfers between devices, cross_layer(): lax.psum_scatter(partial_out, 'mp', scatter_dimension=1, tiled=True)  158 us
    psum x1, waiting for transfers between devices, body(): lax.psum(encoder_terms(fetched_floats, enc_gain, enc_up, enc_down), ('sec...  126 us
    all_to_all x1, waiting for transfers between devices, body(): lax.all_to_all(payload, 'db', split_axis=0, concat_axis=0, tiled=True)  79.6 us
    all_gather x3, waiting for transfers between devices, cross_layer(): whole_rows = lax.all_gather(state_rows, 'mp', axis=1, tiled=True)  44 us
    dot_general x3, matrix products, cross_layer(): partial_out = jnp.dot(context, out_w, preferred_element_type=jnp.float32)  22.9 us
    dot_general x3, matrix products, cross_layer(): jnp.einsum('chqk,ckhd->cqhd', soft_weights, value_four, preferred_element...  19.5 us
    dot_general x3, matrix products, cross_layer(): jnp.dot(normed, query_w, preferred_element_type=jnp.float32) * HD ** (-0.5)  19 us
    unnamed x56, local copies, waits for them, and re-layouts  18.4 us
  transfers between devices with their start and end apart: 11, of which 10 were waited for; matrix products, arithmetic and copies ran while one was open for 9% of the time, Pallas kernels for 0%

commit v1 on v0

v1 whole, which is shorter than its diff:
```python
import jax
import jax.numpy as jnp
from jax import lax
from jax.sharding import PartitionSpec as P

HD = 128
E = 896
NEIGH = 2
QBLOCK = 64
NBLOCK = 128
CHUNKS = 2
F32 = jnp.float32
BF16 = jnp.bfloat16


def swap(block, axis):
    return lax.ppermute(block, axis, [(0, 1), (1, 0)])


def rms_scale(rows_in, gain_vec):
    return (
        rows_in * lax.rsqrt(jnp.mean(rows_in * rows_in, axis=-1, keepdims=True) + 1e-06) * gain_vec
    )


def mm(a, b):
    return jnp.dot(a, b, preferred_element_type=F32)


def encode_half(database, enc_gain, enc_up, enc_down):
    section = lax.axis_index("section")
    held = database.shape[0]
    floats = database.reshape(-1, E).astype(F32)
    normed = rms_scale(floats, enc_gain).astype(BF16)
    inner = jax.nn.gelu(mm(normed, enc_up), approximate=True).astype(BF16)
    terms = mm(inner, enc_down).reshape(held, 2, NBLOCK // 2, E)
    mine = lax.dynamic_index_in_dim(terms, section, 1, keepdims=False)
    theirs = lax.dynamic_index_in_dim(terms, 1 - section, 1, keepdims=False)
    mine = mine + swap(theirs, "section")
    mine = mine + swap(mine.astype(BF16), "mp").astype(F32)
    rows = lax.dynamic_index_in_dim(
        database.reshape(held, 2, NBLOCK // 2, E), section, 1, keepdims=False
    )
    return (rows.astype(F32) + mine).astype(BF16)


def fetch(encoded, neighbour_ids):
    section = lax.axis_index("section")
    db_count = lax.axis_size("db")
    db_index = lax.axis_index("db")
    blocks_held = encoded.shape[0]
    request = neighbour_ids.shape[0] // db_count * NEIGH
    capacity = max(2, (request + db_count - 1) // db_count)
    id_table = neighbour_ids.reshape(db_count, request)
    owners = id_table // blocks_held
    within = id_table % blocks_held
    places = jnp.arange(request)
    same_owner = owners[:, :, None] == owners[:, None, :]
    earlier = places[None, :, None] > places[None, None, :]
    rank_in = jnp.sum((same_owner & earlier).astype(jnp.int32), axis=-1)
    slot_ids = jnp.arange(capacity)
    matches = (owners[:, None, :] == db_index) & (rank_in[:, None, :] == slot_ids[None, :, None])
    send_local = jnp.sum(matches.astype(jnp.int32) * within[:, None, :], axis=-1)
    my_owner = lax.dynamic_index_in_dim(owners, db_index, 0, keepdims=False)
    my_rank = lax.dynamic_index_in_dim(rank_in, db_index, 0, keepdims=False)
    slot_pick = (my_owner * capacity + my_rank).reshape(2, request // 2)
    mine = lax.dynamic_index_in_dim(slot_pick, section, 0, keepdims=False)
    theirs = lax.dynamic_index_in_dim(slot_pick, 1 - section, 0, keepdims=False)
    payload = encoded[send_local]
    received = lax.all_to_all(payload, "db", split_axis=0, concat_axis=0, tiled=True)
    received = received.reshape(db_count * capacity, NBLOCK // 2, E)
    return jnp.stack([received[mine], swap(received[theirs], "section")])


def attend(queries, key_rows, value_rows):
    blocks = key_rows.shape[1]
    heads = queries.shape[1] // HD
    q = queries.reshape(blocks, QBLOCK, heads, HD)
    k = key_rows.reshape(2, blocks, NBLOCK, heads, HD)
    v = value_rows.reshape(2, blocks, NBLOCK, heads, HD)
    k = jnp.concatenate([k[0], k[1]], axis=1)
    v = jnp.concatenate([v[0], v[1]], axis=1)
    scores = jnp.einsum("cqhd,ckhd->chqk", q, k, preferred_element_type=F32)
    probs = jax.nn.softmax(scores, axis=-1).astype(BF16)
    context = jnp.einsum("chqk,ckhd->cqhd", probs, v, preferred_element_type=F32)
    return context.astype(BF16).reshape(blocks * QBLOCK, heads * HD)


def body(
    hidden_in,
    database,
    neighbour_ids,
    enc_gain,
    enc_up,
    enc_down,
    dec_gain,
    w_query,
    w_key,
    w_value,
    w_out,
):
    section = lax.axis_index("section")
    mp = lax.axis_index("mp")
    tokens = hidden_in.shape[0] // 2
    blocks = tokens // QBLOCK
    width = hidden_in.shape[1]

    encoded = encode_half(database, enc_gain, enc_up, enc_down)
    entering = lax.dynamic_slice_in_dim(hidden_in, section * tokens, tokens, 0)
    state = lax.all_gather(entering, "mp", axis=1, tiled=True)
    gains = lax.all_gather(dec_gain, "section", axis=0, tiled=True)
    wq = lax.all_gather(w_query, "section", axis=0, tiled=True)
    wk = lax.all_gather(w_key, "section", axis=0, tiled=True)
    wv = lax.all_gather(w_value, "section", axis=0, tiled=True)
    wo = lax.all_gather(w_out, "section", axis=0, tiled=True)

    neighbours = fetch(encoded, neighbour_ids).reshape(-1, E)

    def project(layer):
        k = mm(neighbours, wk[layer]).astype(BF16).reshape(2, blocks, NBLOCK, -1)
        v = mm(neighbours, wv[layer]).astype(BF16).reshape(2, blocks, NBLOCK, -1)
        return k, v

    def query(rows, layer):
        normed = rms_scale(rows.astype(F32), gains[layer]).astype(BF16)
        return (mm(normed, wq[layer]) * HD ** (-0.5)).astype(BF16)

    q0 = query(state, 0)
    k0, v0 = project(0)
    k1, v1 = project(1)
    piece = tokens // CHUNKS
    pb = blocks // CHUNKS
    results = []
    for i in range(CHUNKS):
        span = slice(i * piece, (i + 1) * piece)
        bspan = slice(i * pb, (i + 1) * pb)
        context = attend(q0[span], k0[:, bspan], v0[:, bspan])
        terms = mm(context, wo[0])
        arrived = swap(terms.astype(BF16), "mp")
        mid = (state[span].astype(F32) + terms + arrived.astype(F32)).astype(BF16)
        q1 = query(mid, 1)
        context = attend(q1, k1[:, bspan], v1[:, bspan])
        away = lax.dynamic_slice_in_dim(wo[1], (1 - mp) * width, width, 1)
        home = lax.dynamic_slice_in_dim(wo[1], mp * width, width, 1)
        arrived = swap(mm(context, away).astype(BF16), "mp")
        mine = lax.dynamic_slice_in_dim(mid, mp * width, width, 1)
        results.append(
            (mine.astype(F32) + mm(context, home) + arrived.astype(F32)).astype(BF16)
        )
    return jnp.concatenate(results, axis=0)


def solution(mesh):
    in_specs = (
        P("db", "mp"),
        P("db", None, None),
        P(),
        P(),
        P(None, ("section", "mp")),
        P(("section", "mp"), None),
        P("section", None),
        P("section", None, "mp"),
        P("section", None, "mp"),
        P("section", None, "mp"),
        P("section", "mp", None),
    )
    out_specs = P(("db", "section"), "mp")
    return jax.shard_map(body, mesh=mesh, in_specs=in_specs, out_specs=out_specs, check_vma=False)
```

time: 606 us -> 260 us (0.43)
  waiting for transfers between devices: 416 us -> 79.2 us
  local copies, waits for them, and re-layouts: 30.8 us -> 51.9 us
  other arithmetic: 31.8 us -> 13.4 us
  matrix products: 91.4 us -> 85 us
    reduce_scatter x3 -> x0, waiting for transfers between devices: 158 us -> none  [cross_layer(): lax.psum_scatter(partial_out, 'mp', scatter_dimension=1, tiled=True)]
    psum x1 -> x0, waiting for transfers between devices: 126 us -> none  [body(): lax.psum(encoder_terms(fetched_floats, enc_gain, enc_up, enc_down), ('sec...]
    all_gather x3 -> x5, waiting for transfers between devices: 44 us -> 0.92 us  [the longest x1 0.9 us: body(): wo = lax.all_gather(w_out, 'section', axis=0, tiled=True)]
    all_to_all x1, waiting for transfers between devices: 79.6 us -> 40.1 us  [fetch(): lax.all_to_all(payload, 'db', split_axis=0, concat_axis=0, tiled=True)]
    ppermute x3 -> x7, waiting for transfers between devices: 8 us -> 35.8 us  [swap(): return lax.ppermute(block, axis, [(0, 1), (1, 0)])]
    squeeze x0 -> x17, local copies, waits for them, and re-layouts: none -> 17 us  [the longest x8 8.24 us: attend(): v = jnp.concatenate([v[0], v[1]], axis=1)]
    dot_general x19 -> x18, matrix products: 91.4 us -> 76.5 us  [the longest x14 69.1 us: mm(): return jnp.dot(a, b, preferred_element_type=F32)]
    slice x0 -> x6, local copies, waits for them, and re-layouts: none -> 13 us  [the longest x1 7.86 us: body(): home = lax.dynamic_slice_in_dim(wo[1], mp * width, width, 1)]
  transfers between devices with their start and end apart: 11 -> 13, of which waited for: 10 -> 6; matrix products, arithmetic and copies ran while one was open for 9% -> 46% of each run, Pallas kernels for 0% -> 0%
where the time goes in v1:
time: 260 us; the launch traced here: 259 us
  matrix products  85 us (33%)
  waiting for transfers between devices  79.2 us (30%)
  local copies, waits for them, and re-layouts  51.9 us (20%)
  starting transfers between devices  14 us (5%)
  between operations  13.7 us (5%)
  other arithmetic  13.4 us (5%)
    dot_general x14, matrix products, mm(): return jnp.dot(a, b, preferred_element_type=F32)  69.1 us
    all_to_all x1, waiting for transfers between devices, fetch(): lax.all_to_all(payload, 'db', split_axis=0, concat_axis=0, tiled=True)  40.1 us
    ppermute x7, waiting for transfers between devices, swap(): return lax.ppermute(block, axis, [(0, 1), (1, 0)])  35.8 us
    unnamed x68, local copies, waits for them, and re-layouts  15.4 us
    sub x4, matrix products, attend(): probs = jax.nn.softmax(scores, axis=-1).astype(BF16)  8.44 us
    squeeze x8, local copies, waits for them, and re-layouts, attend(): v = jnp.concatenate([v[0], v[1]], axis=1)  8.24 us
    slice x1, local copies, waits for them, and re-layouts, body(): home = lax.dynamic_slice_in_dim(wo[1], mp * width, width, 1)  7.86 us
    squeeze x8, local copies, waits for them, and re-layouts, attend(): k = jnp.concatenate([k[0], k[1]], axis=1)  7.46 us
  transfers between devices with their start and end apart: 13, of which 6 were waited for; matrix products, arithmetic and copies ran while one was open for 46% of the time, Pallas kernels for 0%

profile of v1, /device:TPU:0, one launch (start us, length us, event | category | flops | bytes accessed | tf_op | source)
XLA Modules:
  0.0 259.1 jit_solution(9605519387165217540)
XLA Ops:
  6.5 1.6 copy-done
  8.1 1.1 constant_dynamic-slice_fusion.4
  13.2 3.8 %fusion.108 = f32[512,896]{1,0:T(8,128)} fusion(bf16[512,896]{1,0:T(8,128)(2,1)S(1)} %copy-done.22, bf16[512,896]{1,0:T(8,128)(2,1)S(1)} %fusion.40, bf16[896,512]{1,0:T(8,128)(2,1)} %param.15), kind=kOutput, calls=%fused_computation.137 | convolution fusion | flops 941883392 | bytes 4587520 | tf_op jit(solution)/shard_map/dot_general | solution.py:27
  17.0 1.3 dynamic-slice_bitcast_fusion
  19.0 1.9 collective-permute-done
  20.9 1.3 fusion.118
  22.3 2.9 %collective-permute-start.1 = (bf16[4,64,896]{2,1,0:T(8,128)(2,1)S(1)}, bf16[4,64,896]{2,1,0:T(8,128)(2,1)S(1)}, u32[]{:S(2)}, u32[]{:S(2)}) collective-permute-start(bf16[4,64,896]{2,1,0:T(8,128)(2,1)S(1)} %fusion.118), channel_id=1, source_target_pairs={{0,1},{1,0},{2,3},{3,2},{4,5},{5,4},{6,7},{7,6},{8,9},{9,8},{10,11... | collective-permute-start | bytes 1376264 | tf_op jit(solution)/shard_map/ppermute | solution.py:17
  25.7 20.4 %collective-permute-done.1 = bf16[4,64,896]{2,1,0:T(8,128)(2,1)S(1)} collective-permute-done((bf16[4,64,896]{2,1,0:T(8,128)(2,1)S(1)}, bf16[4,64,896]{2,1,0:T(8,128)(2,1)S(1)}, u32[]{:S(2)}, u32[]{:S(2)}) %collective-permute-start.1) | collective-permute-done | bytes 458784 | tf_op jit(solution)/shard_map/ppermute | solution.py:17
  46.1 1.4 fusion.107
  47.4 2.0 gather_fusion
  49.4 6.4 %all-to-all-start = ((bf16[8,2,64,896]{3,2,1,0:T(8,128)(2,1)}), bf16[8,2,64,896]{3,2,1,0:T(8,128)(2,1)S(1)}, u32[]{:S(2)}, u32[]{:S(2)}) async-start(bf16[8,2,64,896]{3,2,1,0:T(8,128)(2,1)} %bitcast.191), calls=%async_computation | async-start | bytes 3670016 | tf_op jit(solution)/shard_map/all_to_all | solution.py:70
  55.9 2.0 all-gather
  58.0 40.1 %all-to-all-done = bf16[8,2,64,896]{3,2,1,0:T(8,128)(2,1)S(1)} async-done(((bf16[8,2,64,896]{3,2,1,0:T(8,128)(2,1)}), bf16[8,2,64,896]{3,2,1,0:T(8,128)(2,1)S(1)}, u32[]{:S(2)}, u32[]{:S(2)}) %all-to-all-start) | async-done | bytes 1835040 | tf_op jit(solution)/shard_map/all_to_all | solution.py:70
  98.0 1.6 gather_fusion.2
  99.7 2.6 fusion.9
  103.0 2.8 %pad_maximum_fusion = bf16[2,8,64,896]{3,2,1,0:T(8,128)(2,1)} fusion(bf16[1,8,64,896]{3,2,1,0:T(8,128)(2,1)} %bitcast.15, bf16[1,8,64,896]{3,2,1,0:T(8,128)(2,1)S(1)} %bitcast.196), kind=kLoop, calls=%fused_computation.56 | loop fusion | flops 917504 | bytes 3670016 | tf_op jit(solution)/shard_map/stack | solution.py:72
  105.8 5.1 %convolution_convert_fusion.2 = bf16[1024,1024]{1,0:T(8,128)(2,1)S(1)} fusion(bf16[1024,896]{1,0:T(8,128)(2,1)} %bitcast.221, bf16[2,896,1024]{2,1,0:T(8,128)(2,1)} %all-gather.13.cloned.1.call-done), kind=kOutput, calls=%fused_computation.50 | convolution fusion | flops 1880096768 | bytes 5767168 | tf_op jit(solution)/shard_map/dot_general | solution.py:27
  110.9 1.2 fusion.213
  112.1 1.4 copy.152
  113.5 1.0 copy.130
  114.8 1.0 copy.131
  115.9 4.4 %convolution_convert_fusion.3 = bf16[1024,1024]{1,0:T(8,128)(2,1)S(1)} fusion(bf16[1024,896]{1,0:T(8,128)(2,1)} %bitcast.222, bf16[2,896,1024]{2,1,0:T(8,128)(2,1)} %all-gather.9.cloned.1.call-done), kind=kOutput, calls=%fused_computation.51 | convolution fusion | flops 1880096768 | bytes 5767168 | tf_op jit(solution)/shard_map/dot_general | solution.py:27
  120.3 1.4 fusion.214
  121.7 1.4 copy.154
  123.0 1.0 copy.126
  124.3 1.0 copy.127
  127.5 1.0 copy.106
  128.8 1.0 copy.107
  129.8 7.1 %convolution_convert_fusion = bf16[1024,1024]{1,0:T(8,128)(2,1)} fusion(bf16[1024,896]{1,0:T(8,128)(2,1)} %bitcast.223, bf16[2,896,1024]{2,1,0:T(8,128)(2,1)} %all-gather.13.cloned.1.call-done), kind=kOutput, calls=%fused_computation.48 | convolution fusion | flops 1880096768 | bytes 5767168 | tf_op jit(solution)/shard_map/dot_general | solution.py:27
  136.9 7.6 %fusion.52 = bf16[256,1024]{1,0:T(8,128)(2,1)S(1)} fusion(bf16[2,4096,1024]{2,1,0:T(8,128)(2,1)} %all-gather.11.cloned.1.call-done, bf16[256,4096]{1,0:T(8,128)(2,1)S(1)} %copy-done.2, f32[4096]{0:T(1024)S(1)} %bitcast.234, f32[256]{0:T(256)S(1)} %add_rsqrt_fusion), kind=kOutput, calls=%fused_computation.71 | convolution fusion | flops 2152202240 | bytes 11027456 | tf_op jit(solution)/shard_map/dot_general | solution.py:27
  144.6 2.8 %fusion.224 = (f32[2,8,64]{2,1,0:T(8,128)S(1)}, f32[2,8,64,256]{3,2,1,0:T(8,128)}) fusion(bf16[2,128,8,128]{3,1,2,0:T(8,128)(2,1)} %copy.131, bf16[2,128,8,128]{3,1,2,0:T(8,128)(2,1)} %copy.130, bf16[2,64,8,128]{3,2,1,0:T(8,128)(2,1)S(1)} %bitcast.226), kind=kOutput, calls=%fused_computation.232 | convolution fusion | flops 69730560 | bytes 2363392 | tf_op jit(solution)/shard_map/sub | solution.py:84
  147.4 2.1 fusion.61
  150.6 6.4 %fusion.229 = (bf16[128,4096]{1,0:T(8,128)(2,1)}, f32[128,4096]{1,0:T(8,128)}) fusion(bf16[2,1024,4096]{2,1,0:T(8,128)(2,1)} %all-gather.15.cloned.1.call-done, bf16[16,8,8,128]{3,2,1,0:T(8,128)(2,1)S(1)} %bitcast.225), kind=kOutput, calls=%fused_computation.233 | convolution fusion | flops 1074266112 | bytes 11796480 | tf_op jit(solution)/shard_map/dot_general | solution.py:27
  156.9 1.7 collective-permute-start.5
  158.7 2.6 %fusion.218 = (f32[2,8,64]{2,1,0:T(8,128)S(1)}, f32[2,8,64,256]{3,2,1,0:T(8,128)}) fusion(bf16[2,128,8,128]{3,1,2,0:T(8,128)(2,1)} %copy.111, bf16[2,128,8,128]{3,1,2,0:T(8,128)(2,1)S(1)} %copy.110, bf16[2,64,8,128]{3,2,1,0:T(8,128)(2,1)S(1)} %bitcast.227), kind=kOutput, calls=%fused_computation.230 | convolution fusion | flops 69730560 | bytes 2363392 | tf_op jit(solution)/shard_map/sub | solution.py:84
  161.3 1.9 fusion.59
  163.4 6.5 %fusion.223 = (bf16[128,4096]{1,0:T(8,128)(2,1)}, f32[128,4096]{1,0:T(8,128)}) fusion(bf16[2,1024,4096]{2,1,0:T(8,128)(2,1)} %all-gather.15.cloned.1.call-done, bf16[16,8,8,128]{3,2,1,0:T(8,128)(2,1)S(1)} %bitcast.230), kind=kOutput, calls=%fused_computation.231 | convolution fusion | flops 1074266112 | bytes 11796480 | tf_op jit(solution)/shard_map/dot_general | solution.py:27
  170.2 1.2 fusion.215
  171.4 1.3 copy.148
  173.7 1.3 copy.149
  176.1 4.4 %convolution_convert_fusion.1 = bf16[1024,1024]{1,0:T(8,128)(2,1)S(1)} fusion(bf16[1024,896]{1,0:T(8,128)(2,1)} %bitcast.224, bf16[2,896,1024]{2,1,0:T(8,128)(2,1)} %all-gather.9.cloned.1.call-done), kind=kOutput, calls=%fused_computation.49 | convolution fusion | flops 1880096768 | bytes 5767168 | tf_op jit(solution)/shard_map/dot_general | solution.py:27
  180.4 1.3 fusion.216
  181.8 1.3 copy.150
  184.1 1.3 copy.151
  185.4 1.1 copy.117
  186.5 1.3 copy.156
  189.1 1.0 copy.141
  190.1 1.3 copy.158
  193.8 7.9 %slice.193 = bf16[1,1024,4096]{2,1,0:T(8,128)(2,1)} slice(bf16[2,1024,4096]{2,1,0:T(8,128)(2,1)} %all-gather.15.cloned.1.call-done), slice={[1:2], [0:1024], [0:4096]} | slice | bytes 16777216 | tf_op jit(solution)/shard_map/slice | solution.py:144
  201.6 3.4 %collective-permute-done.3 = bf16[128,4096]{1,0:T(8,128)(2,1)} collective-permute-done((bf16[128,4096]{1,0:T(8,128)(2,1)}, bf16[128,4096]{1,0:T(8,128)(2,1)}, u32[]{:S(2)}, u32[]{:S(2)}) %collective-permute-start.3) | collective-permute-done | bytes 1048608 | tf_op jit(solution)/shard_map/ppermute | solution.py:17
  205.1 3.2 %fusion.30 = (f32[128]{0:T(128)S(1)}, bf16[128,4096]{1,0:T(8,128)(2,1)S(1)}, f32[128]{0:T(128)S(1)}, bf16[128,4096]{1,0:T(8,128)(2,1)S(1)}) fusion(bf16[128,4096]{1,0:T(8,128)(2,1)} %collective-permute-done.3, f32[128,4096]{1,0:T(8,128)} %get-tuple-element.38, bf16[256,4096]{1,0:T(8,128)(2,1)S(1)} %copy-done.2, bf16[128,4096]{1,0:T(8,128)(2,1)} %collective-permute-done.5, ...), kind=kLoop, calls=%fused_computation.38 | loop fusion | flops 8388352 | bytes 10486784 | tf_op jit(solution)/shard_map/reduce_sum | solution.py:22
  208.4 5.4 %fusion.63 = bf16[16,8,8,128]{3,1,2,0:T(8,128)(2,1)S(1)} fusion(bf16[2,4096,1024]{2,1,0:T(8,128)(2,1)} %all-gather.11.cloned.1.call-done, bf16[128,4096]{1,0:T(8,128)(2,1)S(1)} %get-tuple-element.6, f32[4096]{0:T(1024)S(1)} %bitcast.232, f32[128]{0:T(128)S(1)} %get-tuple-element.48), kind=kOutput, calls=%fused_computation.84 | convolution fusion | flops 1076101120 | bytes 9716224 | tf_op jit(solution)/shard_map/dot_general | solution.py:27
  213.8 1.5 fusion.235
  215.4 1.6 fusion.60
  217.2 3.7 %fusion.24 = bf16[128,2048]{1,0:T(8,128)(2,1)} fusion(bf16[1,1024,4096]{2,1,0:T(8,128)(2,1)} %slice.193, s32[]{:T(128)S(6)} %select_n.97, bf16[16,8,8,128]{3,2,1,0:T(8,128)(2,1)S(1)} %bitcast.197), kind=kOutput, calls=%fused_computation.36 | convolution fusion | flops 537133056 | bytes 4980740 | tf_op jit(solution)/shard_map/dot_general | solution.py:27
  220.9 1.7 collective-permute-start.4
  222.6 4.8 %fusion.64 = bf16[16,8,8,128]{3,1,2,0:T(8,128)(2,1)S(1)} fusion(bf16[2,4096,1024]{2,1,0:T(8,128)(2,1)} %all-gather.11.cloned.1.call-done, bf16[128,4096]{1,0:T(8,128)(2,1)S(1)} %get-tuple-element.12, f32[128]{0:T(128)S(1)} %get-tuple-element.47, f32[4096]{0:T(1024)S(1)} %bitcast.233), kind=kOutput, calls=%fused_computation.85 | convolution fusion | flops 1076101120 | bytes 9716224 | tf_op jit(solution)/shard_map/dot_general | solution.py:27
  227.5 1.5 fusion.230
  229.1 1.9 fusion.62
  231.1 3.8 %fusion.27 = bf16[128,2048]{1,0:T(8,128)(2,1)} fusion(bf16[1,1024,4096]{2,1,0:T(8,128)(2,1)} %slice.193, s32[]{:T(128)S(6)} %select_n.97, bf16[16,8,8,128]{3,2,1,0:T(8,128)(2,1)S(1)} %bitcast.199), kind=kOutput, calls=%fused_computation.37 | convolution fusion | flops 537133056 | bytes 4980740 | tf_op jit(solution)/shard_map/dot_general | solution.py:27
  235.2 3.0 %add_convert_fusion.3 = bf16[128,2048]{1,0:T(8,128)(2,1)S(1)} fusion(bf16[128,2048]{1,0:T(8,128)(2,1)S(1)} %collective-permute-done.4, bf16[128,4096]{1,0:T(8,128)(2,1)S(1)} %copy-done.5, s32[]{:T(128)S(6)} %select_n.96, bf16[1,1024,4096]{2,1,0:T(8,128)(2,1)} %slice.193, bf16[16,8,8,128]{3,2,1,0:T(8,128)(2,1)S(1)} %bitcast.198), kind=kOutput, calls=%fused_computation.127 | convolution fusion | flops 538181632 | bytes 6030336 | tf_op jit(solution)/shard_map/dot_general | solution.py:27
  238.2 10.1 %collective-permute-done.6 = bf16[128,2048]{1,0:T(8,128)(2,1)} collective-permute-done((bf16[128,2048]{1,0:T(8,128)(2,1)}, bf16[128,2048]{1,0:T(8,128)(2,1)}, u32[]{:S(2)}, u32[]{:S(2)}) %collective-permute-start.6) | collective-permute-done | bytes 524320 | tf_op jit(solution)/shard_map/ppermute | solution.py:17
  248.3 3.3 %add_convert_fusion.2 = bf16[128,2048]{1,0:T(8,128)(2,1)S(1)} fusion(bf16[128,2048]{1,0:T(8,128)(2,1)} %collective-permute-done.6, bf16[128,4096]{1,0:T(8,128)(2,1)S(1)} %get-tuple-element.12, s32[]{:T(128)S(6)} %select_n.96, bf16[1,1024,4096]{2,1,0:T(8,128)(2,1)} %slice.193, bf16[16,8,8,128]{3,2,1,0:T(8,128)(2,1)S(1)} %bitcast.200), kind=kOutput, calls=%fused_computation.123 | convolution fusion | flops 538181632 | bytes 6030336 | tf_op jit(solution)/shard_map/dot_general | solution.py:27
  251.5 1.0 pad_maximum_fusion.1
  (115 shorter events, 18.1 us)
Async XLA Ops:
  6.5 1.6 copy-start
  6.5 93.1 %all-gather.7.cloned.1.call-start = ((), (), s32[]{:S(2)}) async-start(), calls=%async_computation.1 | async-start | bytes 3145728 | tf_op jit(solution)/shard_map/all_gather | solution.py:110
  9.2 96.6 %all-gather.13.cloned.1.call-start = ((), (), s32[]{:S(2)}) async-start(), calls=%async_computation.4 | async-start | bytes 5505024 | tf_op jit(solution)/shard_map/all_gather | solution.py:113
  10.0 105.9 %all-gather.9.cloned.1.call-start = ((), (), s32[]{:S(2)}) async-start(), calls=%async_computation.2 | async-start | bytes 5505024 | tf_op jit(solution)/shard_map/all_gather | solution.py:114
  10.7 126.2 %all-gather.11.cloned.1.call-start = ((), (), s32[]{:S(2)}) async-start(), calls=%async_computation.3 | async-start | bytes 25165824 | tf_op jit(solution)/shard_map/all_gather | solution.py:112
  11.3 1.2 copy-start.3
  11.3 1.4 copy-start.20
  11.3 139.3 %all-gather.15.cloned.1.call-start = ((), (), s32[]{:S(2)}) async-start(), calls=%async_computation.5 | async-start | bytes 25165824 | tf_op jit(solution)/shard_map/all_gather | solution.py:115
  11.9 1.3 copy-start.22
  13.2 5.6 %copy-start.21 = (s32[64,2]{0,1:T(2,128)S(1)}, s32[64,2]{0,1:T(2,128)}, u32[]{:S(2)}) copy-start(s32[64,2]{0,1:T(2,128)} %param.13) | copy-start | bytes 1540
  18.3 2.6 %collective-permute-start = (f32[4,64,896]{2,1,0:T(8,128)S(1)}, f32[4,64,896]{2,1,0:T(8,128)S(1)}, u32[]{:S(2)}, u32[]{:S(2)}) collective-permute-start(f32[4,64,896]{2,1,0:T(8,128)S(1)} %dynamic-slice_bitcast_fusion), channel_id=1, source_target_pairs={{0,2},{2,0},{1,3},{3,1},{4,6},{6,4},{5,7},{7,5},{8,10},{10,8},{9,1... | collective-permute-start | bytes 2752520 | tf_op jit(solution)/shard_map/ppermute | solution.py:17
  22.3 23.8 %collective-permute-start.1 = (bf16[4,64,896]{2,1,0:T(8,128)(2,1)S(1)}, bf16[4,64,896]{2,1,0:T(8,128)(2,1)S(1)}, u32[]{:S(2)}, u32[]{:S(2)}) collective-permute-start(bf16[4,64,896]{2,1,0:T(8,128)(2,1)S(1)} %fusion.118), channel_id=1, source_target_pairs={{0,1},{1,0},{2,3},{3,2},{4,5},{5,4},{6,7},{7,6},{8,9},{9,8},{10,11... | collective-permute-start | bytes 1376264 | tf_op jit(solution)/shard_map/ppermute | solution.py:17
  49.4 6.5 %copy-start.19 = (f32[1,4096]{1,0:T(1,128)S(1)}, f32[1,4096]{1,0:T(1,128)}, u32[]{:S(2)}) copy-start(f32[1,4096]{1,0:T(1,128)} %param.17) | copy-start | bytes 49156
  49.4 48.6 %all-to-all-start = ((bf16[8,2,64,896]{3,2,1,0:T(8,128)(2,1)}), bf16[8,2,64,896]{3,2,1,0:T(8,128)(2,1)S(1)}, u32[]{:S(2)}, u32[]{:S(2)}) async-start(bf16[8,2,64,896]{3,2,1,0:T(8,128)(2,1)} %bitcast.191), calls=%async_computation | async-start | bytes 3670016 | tf_op jit(solution)/shard_map/all_to_all | solution.py:70
  99.6 3.4 %collective-permute-start.2 = (bf16[8,64,896]{2,1,0:T(8,128)(2,1)}, bf16[8,64,896]{2,1,0:T(8,128)(2,1)}, u32[]{:S(2)}, u32[]{:S(2)}) collective-permute-start(bf16[8,64,896]{2,1,0:T(8,128)(2,1)} %gather_fusion.2), channel_id=1, source_target_pairs={{0,2},{2,0},{1,3},{3,1},{4,6},{6,4},{5,7},{7,5},{8,10},{10,8},{9,1... | collective-permute-start | bytes 2752520 | tf_op jit(solution)/shard_map/ppermute | solution.py:17
  112.1 2.4 copy-start.11
  121.7 2.4 copy-start.12
  125.4 1.9 copy-start.10
  125.9 2.6 %copy-start.8 = (bf16[1,2,128,1024]{3,2,1,0:T(8,128)(2,1)S(1)}, bf16[1,2,128,1024]{3,2,1,0:T(8,128)(2,1)}, u32[]{:S(2)}) copy-start(bf16[1,2,128,1024]{3,2,1,0:T(8,128)(2,1)} %get-tuple-element.19) | copy-start | bytes 1572868
  129.8 7.1 %copy-start.2 = (bf16[256,4096]{1,0:T(8,128)(2,1)S(1)}, bf16[256,4096]{1,0:T(8,128)(2,1)}, u32[]{:S(2)}) copy-start(bf16[256,4096]{1,0:T(8,128)(2,1)} %all-gather.7.cloned.1.call-done) | copy-start | bytes 6291460
  156.9 44.7 %collective-permute-start.5 = (bf16[128,4096]{1,0:T(8,128)(2,1)}, bf16[128,4096]{1,0:T(8,128)(2,1)}, u32[]{:S(2)}, u32[]{:S(2)}) collective-permute-start(bf16[128,4096]{1,0:T(8,128)(2,1)} %get-tuple-element.41), channel_id=1, source_target_pairs={{0,1},{1,0},{2,3},{3,2},{4,5},{5,4},{6,7},{7,6},{8,9},{9,8},{10,11... | collective-permute-start | bytes 3145736 | tf_op jit(solution)/shard_map/ppermute | solution.py:17
  163.4 6.8 %copy-start.6 = (bf16[1024,1024]{1,0:T(8,128)(2,1)S(1)}, bf16[1024,1024]{1,0:T(8,128)(2,1)}, u32[]{:S(2)}) copy-start(bf16[1024,1024]{1,0:T(8,128)(2,1)} %convolution_convert_fusion) | copy-start | bytes 6291460
  169.8 35.2 %collective-permute-start.3 = (bf16[128,4096]{1,0:T(8,128)(2,1)}, bf16[128,4096]{1,0:T(8,128)(2,1)}, u32[]{:S(2)}, u32[]{:S(2)}) collective-permute-start(bf16[128,4096]{1,0:T(8,128)(2,1)} %get-tuple-element.37), channel_id=1, source_target_pairs={{0,1},{1,0},{2,3},{3,2},{4,5},{5,4},{6,7},{7,6},{8,9},{9,8},{10,11... | collective-permute-start | bytes 3145736 | tf_op jit(solution)/shard_map/ppermute | solution.py:17
  189.1 3.4 %copy-start.9 = (bf16[1,2,128,1024]{3,2,1,0:T(8,128)(2,1)S(1)}, bf16[1,2,128,1024]{3,2,1,0:T(8,128)(2,1)}, u32[]{:S(2)}) copy-start(bf16[1,2,128,1024]{3,2,1,0:T(8,128)(2,1)} %get-tuple-element.28) | copy-start | bytes 1572868
  193.8 11.3 %copy-start.7 = (f32[128,4096]{1,0:T(8,128)S(1)}, f32[128,4096]{1,0:T(8,128)}, u32[]{:S(2)}) copy-start(f32[128,4096]{1,0:T(8,128)} %get-tuple-element.42) | copy-start | bytes 6291460
  208.3 5.4 %copy-start.4 = (bf16[128,4096]{1,0:T(8,128)(2,1)}, bf16[128,4096]{1,0:T(8,128)(2,1)S(1)}, u32[]{:S(2)}) copy-start(bf16[128,4096]{1,0:T(8,128)(2,1)S(1)} %get-tuple-element.6) | copy-start | bytes 3145732
  208.3 5.5 %copy-start.14 = (bf16[2,128,8,128]{3,1,2,0:T(8,128)(2,1)S(1)}, bf16[2,128,8,128]{3,1,2,0:T(8,128)(2,1)}, u32[]{:S(2)}) copy-start(bf16[2,128,8,128]{3,1,2,0:T(8,128)(2,1)} %copy.120) | copy-start | bytes 1572868
  208.3 5.5 %copy-start.16 = (bf16[2,128,8,128]{3,1,2,0:T(8,128)(2,1)S(1)}, bf16[2,128,8,128]{3,1,2,0:T(8,128)(2,1)}, u32[]{:S(2)}) copy-start(bf16[2,128,8,128]{3,1,2,0:T(8,128)(2,1)} %copy.121) | copy-start | bytes 1572868
  213.8 1.6 copy-start.17
  213.8 1.6 copy-start.18
  220.9 14.3 %collective-permute-start.4 = (bf16[128,2048]{1,0:T(8,128)(2,1)}, bf16[128,2048]{1,0:T(8,128)(2,1)S(1)}, u32[]{:S(2)}, u32[]{:S(2)}) collective-permute-start(bf16[128,2048]{1,0:T(8,128)(2,1)} %fusion.24), channel_id=1, source_target_pairs={{0,1},{1,0},{2,3},{3,2},{4,5},{5,4},{6,7},{7,6},{8,9},{9,8},{10,11... | collective-permute-start | bytes 1572872 | tf_op jit(solution)/shard_map/ppermute | solution.py:17
  222.6 4.9 %copy-start.13 = (bf16[2,128,8,128]{3,1,2,0:T(8,128)(2,1)S(1)}, bf16[2,128,8,128]{3,1,2,0:T(8,128)(2,1)}, u32[]{:S(2)}) copy-start(bf16[2,128,8,128]{3,1,2,0:T(8,128)(2,1)} %copy.140) | copy-start | bytes 1572868
  222.6 4.9 %copy-start.15 = (bf16[2,128,8,128]{3,1,2,0:T(8,128)(2,1)S(1)}, bf16[2,128,8,128]{3,1,2,0:T(8,128)(2,1)}, u32[]{:S(2)}) copy-start(bf16[2,128,8,128]{3,1,2,0:T(8,128)(2,1)} %copy.141) | copy-start | bytes 1572868
  231.1 4.1 %copy-start.5 = (bf16[128,4096]{1,0:T(8,128)(2,1)S(1)}, bf16[128,4096]{1,0:T(8,128)(2,1)}, u32[]{:S(2)}) copy-start(bf16[128,4096]{1,0:T(8,128)(2,1)} %copy-done.4) | copy-start | bytes 3145732
  234.9 13.4 %collective-permute-start.6 = (bf16[128,2048]{1,0:T(8,128)(2,1)}, bf16[128,2048]{1,0:T(8,128)(2,1)}, u32[]{:S(2)}, u32[]{:S(2)}) collective-permute-start(bf16[128,2048]{1,0:T(8,128)(2,1)} %fusion.27), channel_id=1, source_target_pairs={{0,1},{1,0},{2,3},{3,2},{4,5},{5,4},{6,7},{7,6},{8,9},{9,8},{10,11... | collective-permute-start | bytes 1572872 | tf_op jit(solution)/shard_map/ppermute | solution.py:17
  248.3 4.3 %copy-start.1 = (bf16[512,2048]{1,0:T(8,128)(2,1)S(1)}, bf16[512,2048]{1,0:T(8,128)(2,1)}, u32[]{:S(2)}) copy-start(bf16[512,2048]{1,0:T(8,128)(2,1)} %param.11) | copy-start | bytes 6291460
Sparse Core Ops, SparseCore 0:
  9.4 45.6 all-gather.6
  56.6 12.9 all-gather.12
  71.1 14.0 all-gather.8
  86.6 31.2 all-gather.10
  119.3 31.2 all-gather.14

commit v2 on v1

--- a/solution.py
+++ b/solution.py
@@ -1,6 +1,10 @@
+import functools
+
 import jax
 import jax.numpy as jnp
 from jax import lax
+from jax.experimental import pallas as pl
+from jax.experimental.pallas import tpu as pltpu
 from jax.sharding import PartitionSpec as P
 
 HD = 128
@@ -44,7 +48,7 @@
     return (rows.astype(F32) + mine).astype(BF16)
 
 
-def fetch(encoded, neighbour_ids):
+def fetch(encoded, neighbour_ids, fill):
     section = lax.axis_index("section")
     db_count = lax.axis_size("db")
     db_index = lax.axis_index("db")
@@ -68,22 +72,189 @@
     theirs = lax.dynamic_index_in_dim(slot_pick, 1 - section, 0, keepdims=False)
     payload = encoded[send_local]
     received = lax.all_to_all(payload, "db", split_axis=0, concat_axis=0, tiled=True)
+    received, fill = lax.optimization_barrier((received, fill))
     received = received.reshape(db_count * capacity, NBLOCK // 2, E)
-    return jnp.stack([received[mine], swap(received[theirs], "section")])
-
-
-def attend(queries, key_rows, value_rows):
-    blocks = key_rows.shape[1]
-    heads = queries.shape[1] // HD
-    q = queries.reshape(blocks, QBLOCK, heads, HD)
-    k = key_rows.reshape(2, blocks, NBLOCK, heads, HD)
-    v = value_rows.reshape(2, blocks, NBLOCK, heads, HD)
-    k = jnp.concatenate([k[0], k[1]], axis=1)
-    v = jnp.concatenate([v[0], v[1]], axis=1)
-    scores = jnp.einsum("cqhd,ckhd->chqk", q, k, preferred_element_type=F32)
-    probs = jax.nn.softmax(scores, axis=-1).astype(BF16)
-    context = jnp.einsum("chqk,ckhd->cqhd", probs, v, preferred_element_type=F32)
-    return context.astype(BF16).reshape(blocks * QBLOCK, heads * HD)
+    moved = swap(received[theirs], "section")
+    return received[mine].reshape(-1, E), moved.reshape(-1, E), fill
+
+
+def kv_kernel(rows, wk, wv, k, v):
+    k[...] = mm(rows[...], wk[0]).astype(BF16)
+    v[...] = mm(rows[...], wv[0]).astype(BF16)
+
+
+def keys_values(rows, wk, wv, layer):
+    count, out = rows.shape[0], wk.shape[2]
+    tile = 256
+    weight = pl.BlockSpec((1, E, out), lambda i: (layer, 0, 0))
+    made = pl.BlockSpec((tile, out), lambda i: (i, 0))
+    k, v = pl.pallas_call(
+        kv_kernel,
+        grid=(count // tile,),
+        in_specs=[pl.BlockSpec((tile, E), lambda i: (i, 0)), weight, weight],
+        out_specs=[made, made],
+        out_shape=[jax.ShapeDtypeStruct((count, out), BF16)] * 2,
+        compiler_params=pltpu.CompilerParams(vmem_limit_bytes=40 << 20),
+        cost_estimate=pl.CostEstimate(
+            flops=4 * count * E * out,
+            bytes_accessed=4 * E * out + 2 * count * E + 4 * count * out,
+            transcendentals=0,
+        ),
+    )(rows, wk, wv)
+    shape = (count // NBLOCK, NBLOCK, out)
+    return k.reshape(shape), v.reshape(shape)
+
+
+def attend_heads(q, ks, vs, block, heads):
+    made = []
+    for h in range(heads):
+        cols = slice(h * HD, (h + 1) * HD)
+        k = jnp.concatenate([ref[block, :, cols] for ref in ks], axis=0)
+        v = jnp.concatenate([ref[block, :, cols] for ref in vs], axis=0)
+        scores = lax.dot_general(
+            q[:, cols], k, (((1,), (1,)), ((), ())), preferred_element_type=F32
+        )
+        e = jnp.exp(scores - jnp.max(scores, axis=-1, keepdims=True))
+        probs = (e / jnp.sum(e, axis=-1, keepdims=True)).astype(BF16)
+        made.append(mm(probs, v).astype(BF16))
+    return jnp.concatenate(made, axis=1)
+
+
+def first_kernel(blocks, heads, q, ka, kb, va, vb, wo, state, send, base, ctx):
+    @pl.when(pl.program_id(0) == 0)
+    def _():
+        for b in range(blocks):
+            rows = slice(b * QBLOCK, (b + 1) * QBLOCK)
+            ctx[rows, :] = attend_heads(q[rows, :], (ka, kb), (va, vb), b, heads)
+
+    terms = mm(ctx[...], wo[0])
+    send[...] = terms.astype(BF16)
+    base[...] = state[...].astype(F32) + terms
+
+
+def first_layer(q, kv, wo, state, part, piece):
+    ka, kb, va, vb = kv
+    blocks = piece // QBLOCK
+    inner, width = wo.shape[1], wo.shape[2]
+    tile = 512
+    around = pl.BlockSpec((blocks, NBLOCK, inner), lambda j: (part, 0, 0))
+    made = pl.BlockSpec((piece, tile), lambda j: (0, j))
+    return pl.pallas_call(
+        functools.partial(first_kernel, blocks, inner // HD),
+        grid=(width // tile,),
+        in_specs=[
+            pl.BlockSpec((piece, inner), lambda j: (part, 0)),
+            around,
+            around,
+            around,
+            around,
+            pl.BlockSpec((1, inner, tile), lambda j: (0, 0, j)),
+            pl.BlockSpec((piece, tile), lambda j: (part, j)),
+        ],
+        out_specs=[made, made],
+        out_shape=[
+            jax.ShapeDtypeStruct((piece, width), BF16),
+            jax.ShapeDtypeStruct((piece, width), F32),
+        ],
+        scratch_shapes=[pltpu.VMEM((piece, inner), BF16)],
+        compiler_params=pltpu.CompilerParams(vmem_limit_bytes=40 << 20),
+        cost_estimate=pl.CostEstimate(
+            flops=2 * piece * inner * (width + 512),
+            bytes_accessed=2 * inner * width + 8 * piece * width,
+            transcendentals=piece * 256 * inner // HD,
+        ),
+    )(q, ka, kb, va, vb, wo, state)
+
+
+def second_kernel(
+    blocks, q_steps, away, mp, base, arrived, gain, wq, ka, kb, va, vb, wo, send, home, normed, mid, ctx
+):
+    j = pl.program_id(0)
+    q_tile = wq.shape[2]
+    tile = wo.shape[2]
+
+    @pl.when(j == 0)
+    def _():
+        whole = (base[...] + arrived[...].astype(F32)).astype(BF16)
+        mid[...] = whole
+        normed[...] = rms_scale(whole.astype(F32), gain[...]).astype(BF16)
+
+    @pl.when(j < q_steps)
+    def _():
+        q = (mm(normed[...], wq[0]) * HD ** (-0.5)).astype(BF16)
+        cols = pl.ds(pl.multiple_of(j * q_tile, q_tile), q_tile)
+        for b in range(blocks):
+            rows = slice(b * QBLOCK, (b + 1) * QBLOCK)
+            ctx[rows, cols] = attend_heads(q[rows, :], (ka, kb), (va, vb), b, q_tile // HD)
+
+    @pl.when((j >= q_steps) & (j < q_steps + away))
+    def _():
+        send[...] = mm(ctx[...], wo[0]).astype(BF16)
+
+    @pl.when(j >= q_steps + away)
+    def _():
+        start = pl.multiple_of((mp[0] * away + j - q_steps - away) * tile, tile)
+        home[...] = mid[:, pl.ds(start, tile)].astype(F32) + mm(ctx[...], wo[0])
+
+
+def second_layer(mp, base, arrived, gain, wq, kv, wo, part):
+    ka, kb, va, vb = kv
+    piece, width = base.shape
+    blocks = piece // QBLOCK
+    inner = wo.shape[1]
+    q_tile, tile = 256, 512
+    q_steps = inner // q_tile
+    away = width // 2 // tile
+    around = pl.BlockSpec(
+        (blocks, NBLOCK, q_tile), lambda j, m: (part, 0, jnp.minimum(j, q_steps - 1))
+    )
+    whole = pl.BlockSpec((piece, width), lambda j, m: (0, 0))
+
+    def out_column(j, m):
+        t = jnp.maximum(j - q_steps, 0)
+        return (1, 0, jnp.where(t < away, (1 - m[0]) * away + t, m[0] * away + t - away))
+
+    return pl.pallas_call(
+        functools.partial(second_kernel, blocks, q_steps, away),
+        grid_spec=pltpu.PrefetchScalarGridSpec(
+            num_scalar_prefetch=1,
+            grid=(q_steps + 2 * away,),
+            in_specs=[
+                whole,
+                whole,
+                pl.BlockSpec((1, width), lambda j, m: (0, 0)),
+                pl.BlockSpec(
+                    (1, width, q_tile), lambda j, m: (1, 0, jnp.minimum(j, q_steps - 1))
+                ),
+                around,
+                around,
+                around,
+                around,
+                pl.BlockSpec((1, inner, tile), out_column),
+            ],
+            out_specs=[
+                pl.BlockSpec((piece, tile), lambda j, m: (0, jnp.clip(j - q_steps, 0, away - 1))),
+                pl.BlockSpec(
+                    (piece, tile), lambda j, m: (0, jnp.clip(j - q_steps - away, 0, away - 1))
+                ),
+            ],
+            scratch_shapes=[
+                pltpu.VMEM((piece, width), BF16),
+                pltpu.VMEM((piece, width), BF16),
+                pltpu.VMEM((piece, inner), BF16),
+            ],
+        ),
+        out_shape=[
+            jax.ShapeDtypeStruct((piece, width // 2), BF16),
+            jax.ShapeDtypeStruct((piece, width // 2), F32),
+        ],
+        compiler_params=pltpu.CompilerParams(vmem_limit_bytes=40 << 20),
+        cost_estimate=pl.CostEstimate(
+            flops=4 * piece * inner * width,
+            bytes_accessed=4 * inner * width + 12 * piece * width,
+            transcendentals=piece * 256 * inner // HD,
+        ),
+    )(mp, base, arrived, gain, wq, ka, kb, va, vb, wo)
 
 
 def body(
@@ -102,51 +273,41 @@
     section = lax.axis_index("section")
     mp = lax.axis_index("mp")
     tokens = hidden_in.shape[0] // 2
-    blocks = tokens // QBLOCK
-    width = hidden_in.shape[1]
 
     encoded = encode_half(database, enc_gain, enc_up, enc_down)
     entering = lax.dynamic_slice_in_dim(hidden_in, section * tokens, tokens, 0)
-    state = lax.all_gather(entering, "mp", axis=1, tiled=True)
+    encoded, entering = lax.optimization_barrier((encoded, entering))
+    other = swap(entering, "mp")
+    state = jnp.where(
+        mp == 0,
+        jnp.concatenate([entering, other], axis=1),
+        jnp.concatenate([other, entering], axis=1),
+    )
     gains = lax.all_gather(dec_gain, "section", axis=0, tiled=True)
     wq = lax.all_gather(w_query, "section", axis=0, tiled=True)
     wk = lax.all_gather(w_key, "section", axis=0, tiled=True)
     wv = lax.all_gather(w_value, "section", axis=0, tiled=True)
     wo = lax.all_gather(w_out, "section", axis=0, tiled=True)
 
-    neighbours = fetch(encoded, neighbour_ids).reshape(-1, E)
-
-    def project(layer):
-        k = mm(neighbours, wk[layer]).astype(BF16).reshape(2, blocks, NBLOCK, -1)
-        v = mm(neighbours, wv[layer]).astype(BF16).reshape(2, blocks, NBLOCK, -1)
-        return k, v
-
-    def query(rows, layer):
-        normed = rms_scale(rows.astype(F32), gains[layer]).astype(BF16)
-        return (mm(normed, wq[layer]) * HD ** (-0.5)).astype(BF16)
-
-    q0 = query(state, 0)
-    k0, v0 = project(0)
-    k1, v1 = project(1)
+    normed = rms_scale(state.astype(F32), gains[0]).astype(BF16)
+    q0 = (mm(normed, wq[0]) * HD ** (-0.5)).astype(BF16)
+    rows_a, rows_b, q0 = fetch(encoded, neighbour_ids, q0)
+
+    def around(layer):
+        ka, va = keys_values(rows_a, wk, wv, layer)
+        kb, vb = keys_values(rows_b, wk, wv, layer)
+        return ka, kb, va, vb
+
+    kv0 = around(0)
+    kv1 = around(1)
     piece = tokens // CHUNKS
-    pb = blocks // CHUNKS
+    mp_scalar = mp.astype(jnp.int32).reshape(1)
+    sent = [first_layer(q0, kv0, wo, state, i, piece) for i in range(CHUNKS)]
+    arrived = [swap(send, "mp") for send, _ in sent]
     results = []
     for i in range(CHUNKS):
-        span = slice(i * piece, (i + 1) * piece)
-        bspan = slice(i * pb, (i + 1) * pb)
-        context = attend(q0[span], k0[:, bspan], v0[:, bspan])
-        terms = mm(context, wo[0])
-        arrived = swap(terms.astype(BF16), "mp")
-        mid = (state[span].astype(F32) + terms + arrived.astype(F32)).astype(BF16)
-        q1 = query(mid, 1)
-        context = attend(q1, k1[:, bspan], v1[:, bspan])
-        away = lax.dynamic_slice_in_dim(wo[1], (1 - mp) * width, width, 1)
-        home = lax.dynamic_slice_in_dim(wo[1], mp * width, width, 1)
-        arrived = swap(mm(context, away).astype(BF16), "mp")
-        mine = lax.dynamic_slice_in_dim(mid, mp * width, width, 1)
-        results.append(
-            (mine.astype(F32) + mm(context, home) + arrived.astype(F32)).astype(BF16)
-        )
+        send, home = second_layer(mp_scalar, sent[i][1], arrived[i], gains[1:2], wq, kv1, wo, i)
+        results.append((home + swap(send, "mp").astype(F32)).astype(BF16))
     return jnp.concatenate(results, axis=0)
 
 

time: 260 us -> 217 us (0.83)
  matrix products: 85 us -> 10.1 us
  Pallas kernels: 0 us -> 72.2 us
  local copies, waits for them, and re-layouts: 51.9 us -> 31.1 us
  waiting for transfers between devices: 79.2 us -> 59.1 us
  starting transfers between devices: 14 us -> 16.8 us
    pallas_call x0 -> x8, Pallas kernels: none -> 72.2 us  [the longest x2 34.3 us: second_layer(): pl.pallas_call(functools.partial(second_kernel, blocks, q_steps, away), g...]
    dot_general x14 -> x2, matrix products: 69.1 us -> 10.1 us  [mm(): return jnp.dot(a, b, preferred_element_type=F32)]
    all_to_all x1, waiting for transfers between devices: 40.1 us -> 9.63 us  [fetch(): lax.all_to_all(payload, 'db', split_axis=0, concat_axis=0, tiled=True)]
    squeeze x16 -> x0, local copies, waits for them, and re-layouts: 15.7 us -> none  [the longest x8 8.24 us: attend(): v = jnp.concatenate([v[0], v[1]], axis=1)]
    slice x6 -> x1, local copies, waits for them, and re-layouts: 13 us -> 0.61 us  [body(): gains[1:2]]
    ppermute x7 -> x8, waiting for transfers between devices: 35.8 us -> 46.8 us  [swap(): return lax.ppermute(block, axis, [(0, 1), (1, 0)])]
    sub x4 -> x0, matrix products: 8.44 us -> none  [attend(): probs = jax.nn.softmax(scores, axis=-1).astype(BF16)]
    dot_general x4 -> x0, matrix products: 7.42 us -> none  [attend(): jnp.einsum('chqk,ckhd->cqhd', probs, v, preferred_element_type=F32)]
  transfers between devices with their start and end apart: 13 -> 13, of which waited for: 6 -> 7; matrix products, arithmetic and copies ran while one was open for 46% -> 15% of each run, Pallas kernels for 0% -> 28%
where the time goes in v2:
time: 217 us; the launch traced here: 216 us
  Pallas kernels  72.2 us (33%)
  waiting for transfers between devices  59.1 us (27%)
  local copies, waits for them, and re-layouts  31.1 us (14%)
  starting transfers between devices  16.8 us (8%)
  between operations  13.4 us (6%)
  other arithmetic  11.1 us (5%)
  matrix products  10.1 us (5%)
    ppermute x8, waiting for transfers between devices, swap(): return lax.ppermute(block, axis, [(0, 1), (1, 0)])  46.8 us
    pallas_call x2, Pallas kernels, second_layer(): pl.pallas_call(functools.partial(second_kernel, blocks, q_steps, away), g...  34.3 us
    pallas_call x2, Pallas kernels, first_layer(): pl.pallas_call(functools.partial(first_kernel, blocks, inner // HD), grid...  25.6 us
    unnamed x59, local copies, waits for them, and re-layouts  18.8 us
    pallas_call x4, Pallas kernels, keys_values(): pl.pallas_call(kv_kernel, grid=(count // tile,), in_specs=[pl.BlockSpec((...  12.3 us
    ppermute x8, starting transfers between devices, swap(): return lax.ppermute(block, axis, [(0, 1), (1, 0)])  10.6 us
    dot_general x2, matrix products, mm(): return jnp.dot(a, b, preferred_element_type=F32)  10.1 us
    all_to_all x1, waiting for transfers between devices, fetch(): lax.all_to_all(payload, 'db', split_axis=0, concat_axis=0, tiled=True)  9.63 us
  transfers between devices with their start and end apart: 13, of which 7 were waited for; matrix products, arithmetic and copies ran while one was open for 15% of the time, Pallas kernels for 28%

profile of v2, /device:TPU:0, one launch (start us, length us, event | category | flops | bytes accessed | tf_op | source)
XLA Modules:
  0.0 215.9 jit_solution(16403690627289799643)
XLA Ops:
  6.5 0.7 all-gather.6.cloned.1.call-update
  7.3 0.7 all-gather.8.cloned.1.call-update
  8.1 0.7 all-gather.10.cloned.1.call-update
  8.8 0.5 all-gather.12.cloned.1.call-update
  9.3 0.6 copy-done.22
  9.9 0.3 multiply_reduce_fusion
  10.2 1.2 fusion.8
  11.4 4.4 %fusion.24 = f32[512,896]{1,0:T(8,128)} fusion(bf16[512,896]{1,0:T(8,128)(2,1)} %param.16, bf16[512,896]{1,0:T(8,128)(2,1)} %fusion.8, bf16[896,512]{1,0:T(8,128)(2,1)} %param.15), kind=kOutput, calls=%fused_computation.35 | convolution fusion | flops 941883392 | bytes 4587520 | tf_op jit(solution)/shard_map/dot_general | solution.py:31
  15.8 2.2 %dynamic-slice_bitcast_fusion = f32[4,64,896]{2,1,0:T(8,128)} fusion(f32[4,2,64,896]{3,2,1,0:T(8,128)} %bitcast.87, s32[]{:T(128)S(6)} %select_n.86), kind=kLoop, calls=%fused_computation.34 | loop fusion | bytes 1835012 | tf_op jit(solution)/shard_map/jit(dynamic_index_in_dim)/squeeze | solution.py:42
  17.9 0.5 collective-permute-start
  18.4 0.1 copy.18
  18.6 0.3 convert_reduce_fusion
  18.9 0.1 select_reduce_fusion
  19.0 1.8 collective-permute-done
  20.8 2.2 %fusion.30 = bf16[4,64,896]{2,1,0:T(8,128)(2,1)S(1)} fusion(f32[4,64,896]{2,1,0:T(8,128)} %collective-permute-done, f32[4,2,64,896]{3,2,1,0:T(8,128)} %bitcast.88, s32[]{:T(128)S(6)} %select_n.85), kind=kLoop, calls=%fused_computation.40 | loop fusion | flops 458752 | bytes 2293764 | tf_op jit(solution)/shard_map/convert_element_type | solution.py:44
  23.1 3.0 %collective-permute-start.1 = (bf16[4,64,896]{2,1,0:T(8,128)(2,1)S(1)}, bf16[4,64,896]{2,1,0:T(8,128)(2,1)}, u32[]{:S(2)}, u32[]{:S(2)}) collective-permute-start(bf16[4,64,896]{2,1,0:T(8,128)(2,1)S(1)} %fusion.30), channel_id=1, source_target_pairs={{0,1},{1,0},{2,3},{3,2},{4,5},{5,4},{6,7},{7,6},{8,9},{9,8},{10,11... | collective-permute-start | bytes 1376264 | tf_op jit(solution)/shard_map/ppermute | solution.py:21
  26.2 1.0 constant_dynamic-slice_fusion.4
  27.3 9.7 %collective-permute-done.1 = bf16[4,64,896]{2,1,0:T(8,128)(2,1)} collective-permute-done((bf16[4,64,896]{2,1,0:T(8,128)(2,1)S(1)}, bf16[4,64,896]{2,1,0:T(8,128)(2,1)}, u32[]{:S(2)}, u32[]{:S(2)}) %collective-permute-start.1) | collective-permute-done | bytes 458784 | tf_op jit(solution)/shard_map/ppermute | solution.py:21
  37.0 1.5 fusion.23
  38.5 2.0 gather_fusion
  40.5 6.1 %all-to-all-start = ((bf16[8,2,64,896]{3,2,1,0:T(8,128)(2,1)}), bf16[8,2,64,896]{3,2,1,0:T(8,128)(2,1)}, u32[]{:S(2)}, u32[]{:S(2)}) async-start(bf16[8,2,64,896]{3,2,1,0:T(8,128)(2,1)} %bitcast.9), calls=%async_computation | async-start | bytes 3670016 | tf_op jit(solution)/shard_map/all_to_all | solution.py:74
  46.7 1.5 collective-permute-start.2
  48.2 0.5 fusion.39
  48.7 2.0 all-gather
  50.7 0.6 pad_clamp_fusion
  51.3 0.6 slice_bitcast_fusion.6
  51.9 19.0 %collective-permute-done.2 = bf16[256,2048]{1,0:T(8,128)(2,1)} collective-permute-done((bf16[256,2048]{1,0:T(8,128)(2,1)S(1)}, bf16[256,2048]{1,0:T(8,128)(2,1)}, u32[]{:S(2)}, u32[]{:S(2)}) %collective-permute-start.2) | collective-permute-done | bytes 1048608 | tf_op jit(solution)/shard_map/ppermute | solution.py:21
  70.9 2.4 %fusion.1 = (f32[256]{0:T(256)S(1)}, bf16[256,4096]{1,0:T(8,128)(2,1)S(1)}) fusion(bf16[256,2048]{1,0:T(8,128)(2,1)S(1)} %copy-done.23, bf16[256,2048]{1,0:T(8,128)(2,1)} %collective-permute-done.2, pred[]{:T(512)S(6)} %eq.50), kind=kLoop, calls=%fused_computation.7 | loop fusion | flops 12582656 | bytes 4195329 | tf_op jit(solution)/shard_map/reduce_sum | solution.py:26
  73.4 5.8 %fusion.12.q = bf16[256,1024]{1,0:T(8,128)(2,1)S(1)} fusion(bf16[2,4096,1024]{2,1,0:T(8,128)(2,1)} %all-gather.6.cloned.1.call-done.wq, bf16[256,4096]{1,0:T(8,128)(2,1)S(1)} %get-tuple-element.46.state, f32[4096]{0:T(1024)} %bitcast.91, f32[256]{0:T(256)S(1)} %add_rsqrt_fusion), kind=kOutput, calls=%fused_computation.19 | convolution fusion | flops 2152202240 | bytes 11027456 | tf_op jit(solution)/shard_map/dot_general | solution.py:31
  79.2 9.6 %all-to-all-done = bf16[8,2,64,896]{3,2,1,0:T(8,128)(2,1)} async-done(((bf16[8,2,64,896]{3,2,1,0:T(8,128)(2,1)}), bf16[8,2,64,896]{3,2,1,0:T(8,128)(2,1)}, u32[]{:S(2)}, u32[]{:S(2)}) %all-to-all-start) | async-done | bytes 1835040 | tf_op jit(solution)/shard_map/all_to_all | solution.py:74
  88.8 3.5 %gather_fusion.2 = bf16[8,64,896]{2,1,0:T(8,128)(2,1)} fusion(bf16[16,64,896]{2,1,0:T(8,128)(2,1)} %bitcast.13, s32[1024]{0:T(1024)} %pad_clamp_fusion), kind=kCustom, calls=%fused_computation.2 | custom fusion | bytes 1835040 | tf_op jit(solution)/shard_map/gather | solution.py:77
  92.4 0.6 pad_clamp_fusion.1
  93.0 2.6 %gather_fusion.1 = bf16[8,64,896]{2,1,0:T(8,128)(2,1)S(1)} fusion(bf16[16,64,896]{2,1,0:T(8,128)(2,1)} %bitcast.13, s32[1024]{0:T(1024)} %pad_clamp_fusion.1), kind=kCustom, calls=%fused_computation.1 | custom fusion | bytes 1835040 | tf_op jit(solution)/shard_map/gather | solution.py:78
  95.6 2.9 %copy-done.2 = bf16[2,896,1024]{2,1,0:T(8,128)(2,1)S(1)} copy-done((bf16[2,896,1024]{2,1,0:T(8,128)(2,1)S(1)}, bf16[2,896,1024]{2,1,0:T(8,128)(2,1)}, u32[]{:S(2)}) %copy-start.2) | copy-done | bytes 3670040
  98.5 2.0 copy-done.5
  100.6 2.5 %shard_map.109 = (bf16[512,1024]{1,0:T(8,128)(2,1)S(1)}, bf16[512,1024]{1,0:T(8,128)(2,1)S(1)}) custom-call(bf16[512,896]{1,0:T(8,128)(2,1)S(1)} %bitcast.68, bf16[2,896,1024]{2,1,0:T(8,128)(2,1)S(1)} %copy-done.2, bf16[2,896,1024]{2,1,0:T(8,128)(2,1)S(1)} %copy-done.5), custom_call_target="tpu_custom_call" | custom-call | flops 1879048192 | bytes 6684672 | tf_op jit(solution)/shard_map/pallas_call | solution.py:91
  103.1 1.0 copy-done.8
  104.1 1.0 copy-done.10
  105.1 3.6 %shard_map.110 = (bf16[512,1024]{1,0:T(8,128)(2,1)S(1)}, bf16[512,1024]{1,0:T(8,128)(2,1)S(1)}) custom-call(bf16[512,896]{1,0:T(8,128)(2,1)} %bitcast.20.rows, bf16[2,896,1024]{2,1,0:T(8,128)(2,1)S(1)} %copy-done.3, bf16[2,896,1024]{2,1,0:T(8,128)(2,1)S(1)} %copy-done.6), custom_call_target="tpu_custom_call" | custom-call | flops 1879048192 | bytes 6684672 | tf_op jit(solution)/shard_map/pallas_call | solution.py:91
  108.7 1.0 copy-done.12
  109.7 1.0 copy-done.14
  110.6 1.2 copy-done.9
  111.9 1.2 copy-done.11
  113.1 1.2 copy-done.13
  114.3 1.2 copy-done.15
  115.5 12.2 %shard_map.115 = (bf16[128,4096]{1,0:T(8,128)(2,1)S(1)}, f32[128,4096]{1,0:T(8,128)S(1)}) custom-call(bf16[256,1024]{1,0:T(8,128)(2,1)S(1)} %fusion.12.q, bf16[4,128,1024]{2,1,0:T(8,128)(2,1)S(1)} %bitcast.78, bf16[4,128,1024]{2,1,0:T(8,128)(2,1)S(1)} %bitcast.82, bf16[4,128,1024]{2,1,0:T(8,128)(2,1)S(1)} %bitcast.80, bf16[4,128,1024]{2,1,0:T(8,128)(2,1)S(1)} %bitcast.84, ...), custom_call_target="tpu_custom_call" | custom-call | flops 1207959552 | bytes 12582912 | tf_op jit(solution)/shard_map/pallas_call | solution.py:142
  127.8 1.3 copy-done.18
  129.1 1.8 collective-permute-start.6
  130.9 13.4 %shard_map.111 = (bf16[128,4096]{1,0:T(8,128)(2,1)}, f32[128,4096]{1,0:T(8,128)S(1)}) custom-call(bf16[256,1024]{1,0:T(8,128)(2,1)S(1)} %fusion.12.q, bf16[4,128,1024]{2,1,0:T(8,128)(2,1)S(1)} %bitcast.79, bf16[4,128,1024]{2,1,0:T(8,128)(2,1)S(1)} %bitcast.83, bf16[4,128,1024]{2,1,0:T(8,128)(2,1)S(1)} %bitcast.81, bf16[4,128,1024]{2,1,0:T(8,128)(2,1)S(1)} %bitcast.85, ...), custom_call_target="tpu_custom_call" | custom-call | flops 1207959552 | bytes 12582912 | tf_op jit(solution)/shard_map/pallas_call | solution.py:142
  144.4 2.5 %shard_map.112 = (bf16[512,1024]{1,0:T(8,128)(2,1)S(1)}, bf16[512,1024]{1,0:T(8,128)(2,1)S(1)}) custom-call(bf16[512,896]{1,0:T(8,128)(2,1)S(1)} %bitcast.69, bf16[2,896,1024]{2,1,0:T(8,128)(2,1)S(1)} %copy-done.4, bf16[2,896,1024]{2,1,0:T(8,128)(2,1)S(1)} %copy-done.7), custom_call_target="tpu_custom_call" | custom-call | flops 1879048192 | bytes 6684672 | tf_op jit(solution)/shard_map/pallas_call | solution.py:91
  146.9 3.7 %shard_map.113 = (bf16[512,1024]{1,0:T(8,128)(2,1)S(1)}, bf16[512,1024]{1,0:T(8,128)(2,1)S(1)}) custom-call(bf16[512,896]{1,0:T(8,128)(2,1)} %bitcast.20.rows, bf16[2,896,1024]{2,1,0:T(8,128)(2,1)S(1)} %copy-done.4, bf16[2,896,1024]{2,1,0:T(8,128)(2,1)S(1)} %copy-done.7), custom_call_target="tpu_custom_call" | custom-call | flops 1879048192 | bytes 6684672 | tf_op jit(solution)/shard_map/pallas_call | solution.py:91
  150.7 4.4 %collective-permute-done.6.arrived = bf16[128,4096]{1,0:T(8,128)(2,1)S(1)} collective-permute-done((bf16[128,4096]{1,0:T(8,128)(2,1)S(1)}, bf16[128,4096]{1,0:T(8,128)(2,1)S(1)}, u32[]{:S(2)}, u32[]{:S(2)}) %collective-permute-start.6) | collective-permute-done | bytes 1048608 | tf_op jit(solution)/shard_map/ppermute | solution.py:21
  155.1 1.0 copy-done.20
  156.0 1.2 copy-done.21
  157.3 17.2 %shard_map.116 = (bf16[128,2048]{1,0:T(8,128)(2,1)S(1)}, f32[128,2048]{1,0:T(8,128)S(1)}) custom-call(s32[1]{0:T(128)} %bitcast.mp, f32[128,4096]{1,0:T(8,128)S(1)} %copy-done.19, bf16[128,4096]{1,0:T(8,128)(2,1)S(1)} %copy-done.21, f32[1,4096]{1,0:T(1,128)S(1)} %get-tuple-element.49.gain, bf16[2,4096,1024]{2,1,0:T(8,128)(2,1)} %all-gather.6.cloned.1.call-done.wq, ...), custom_call_target="tpu_custom_call" | custom-call | flops 2147483648 | bytes 23068672 | tf_op jit(solution)/shard_map/pallas_call | solution.py:217
  174.5 1.9 collective-permute-start.7
  176.4 1.1 collective-permute-done.4.arrived
  177.5 17.1 %shard_map.114 = (bf16[128,2048]{1,0:T(8,128)(2,1)S(1)}, f32[128,2048]{1,0:T(8,128)S(1)}) custom-call(s32[1]{0:T(128)} %bitcast.mp, f32[128,4096]{1,0:T(8,128)S(1)} %copy-done.17, bf16[128,4096]{1,0:T(8,128)(2,1)S(1)} %collective-permute-done.4.arrived, f32[1,4096]{1,0:T(1,128)S(1)} %get-tuple-element.49.gain, ...), custom_call_target="tpu_custom_call" | custom-call | flops 2147483648 | bytes 23068672 | tf_op jit(solution)/shard_map/pallas_call | solution.py:217
  194.6 1.9 collective-permute-start.5
  196.6 0.1 add_convert_fusion
  196.7 10.8 %collective-permute-done.5 = bf16[128,2048]{1,0:T(8,128)(2,1)S(1)} collective-permute-done((bf16[128,2048]{1,0:T(8,128)(2,1)S(1)}, bf16[128,2048]{1,0:T(8,128)(2,1)S(1)}, u32[]{:S(2)}, u32[]{:S(2)}) %collective-permute-start.5) | collective-permute-done | bytes 524320 | tf_op jit(solution)/shard_map/ppermute | solution.py:21
  207.4 0.1 add_convert_fusion.1
  207.6 1.0 pad_maximum_fusion
  208.6 0.8 copy-done.1
  (67 shorter events, 0.7 us)
Async XLA Ops:
  6.5 19.7 %copy-start = (bf16[512,2048]{1,0:T(8,128)(2,1)S(1)}, bf16[512,2048]{1,0:T(8,128)(2,1)}, u32[]{:S(2)}) copy-start(bf16[512,2048]{1,0:T(8,128)(2,1)} %param.11) | copy-start | bytes 6291460
  6.5 66.9 %all-gather.6.cloned.1.call-start = ((), (), s32[]{:S(2)}) async-start(), calls=%async_computation.1 | async-start | bytes 25165824 | tf_op jit(solution)/shard_map/all_gather | solution.py:287
  7.3 88.3 %all-gather.8.cloned.1.call-start = ((), (), s32[]{:S(2)}) async-start(), calls=%async_computation.2 | async-start | bytes 5505024 | tf_op jit(solution)/shard_map/all_gather | solution.py:288
  8.0 87.6 %all-gather.10.cloned.1.call-start = ((), (), s32[]{:S(2)}) async-start(), calls=%async_computation.3 | async-start | bytes 5505024 | tf_op jit(solution)/shard_map/all_gather | solution.py:289
  8.7 1.2 copy-start.22
  8.8 1.4 copy-start.26
  8.8 101.9 %all-gather.12.cloned.1.call-start = ((), (), s32[]{:S(2)}) async-start(), calls=%async_computation.4 | async-start | bytes 25165824 | tf_op jit(solution)/shard_map/all_gather | solution.py:290
  11.4 7.0 %copy-start.28 = (s32[64,2]{0,1:T(2,128)S(1)}, s32[64,2]{0,1:T(2,128)}, u32[]{:S(2)}) copy-start(s32[64,2]{0,1:T(2,128)} %param.13) | copy-start | bytes 1540
  17.9 2.9 %collective-permute-start = (f32[4,64,896]{2,1,0:T(8,128)}, f32[4,64,896]{2,1,0:T(8,128)}, u32[]{:S(2)}, u32[]{:S(2)}) collective-permute-start(f32[4,64,896]{2,1,0:T(8,128)} %dynamic-slice_bitcast_fusion), channel_id=1, source_target_pairs={{0,2},{2,0},{1,3},{3,1},{4,6},{6,4},{5,7},{7,5},{8,10},{10,8},{9,1... | collective-permute-start | bytes 2752520 | tf_op jit(solution)/shard_map/ppermute | solution.py:21
  23.1 13.9 %collective-permute-start.1 = (bf16[4,64,896]{2,1,0:T(8,128)(2,1)S(1)}, bf16[4,64,896]{2,1,0:T(8,128)(2,1)}, u32[]{:S(2)}, u32[]{:S(2)}) collective-permute-start(bf16[4,64,896]{2,1,0:T(8,128)(2,1)S(1)} %fusion.30), channel_id=1, source_target_pairs={{0,1},{1,0},{2,3},{3,2},{4,5},{5,4},{6,7},{7,6},{8,9},{9,8},{10,11... | collective-permute-start | bytes 1376264 | tf_op jit(solution)/shard_map/ppermute | solution.py:21
  26.2 10.8 %copy-start.24 = (f32[512,896]{1,0:T(8,128)S(1)}, f32[512,896]{1,0:T(8,128)}, u32[]{:S(2)}) copy-start(f32[512,896]{1,0:T(8,128)} %fusion.24) | copy-start | bytes 5505028
  40.5 6.2 %copy-start.23 = (bf16[256,2048]{1,0:T(8,128)(2,1)S(1)}, bf16[256,2048]{1,0:T(8,128)(2,1)}, u32[]{:S(2)}) copy-start(bf16[256,2048]{1,0:T(8,128)(2,1)} %constant_dynamic-slice_fusion.4) | copy-start | bytes 3145732
  40.5 8.2 %copy-start.25 = (f32[1,4096]{1,0:T(1,128)S(1)}, f32[1,4096]{1,0:T(1,128)}, u32[]{:S(2)}) copy-start(f32[1,4096]{1,0:T(1,128)} %param.17) | copy-start | bytes 49156
  40.5 48.3 %all-to-all-start = ((bf16[8,2,64,896]{3,2,1,0:T(8,128)(2,1)}), bf16[8,2,64,896]{3,2,1,0:T(8,128)(2,1)}, u32[]{:S(2)}, u32[]{:S(2)}) async-start(bf16[8,2,64,896]{3,2,1,0:T(8,128)(2,1)} %bitcast.9), calls=%async_computation | async-start | bytes 3670016 | tf_op jit(solution)/shard_map/all_to_all | solution.py:74
  46.7 24.2 %collective-permute-start.2 = (bf16[256,2048]{1,0:T(8,128)(2,1)S(1)}, bf16[256,2048]{1,0:T(8,128)(2,1)}, u32[]{:S(2)}, u32[]{:S(2)}) collective-permute-start(bf16[256,2048]{1,0:T(8,128)(2,1)S(1)} %copy-done.23), channel_id=1, source_target_pairs={{0,1},{1,0},{2,3},{3,2},{4,5},{5,4},{6,7},{7,6},{8,9},{9,8},{10,11... | collective-permute-start | bytes 3145736 | tf_op jit(solution)/shard_map/ppermute | solution.py:21
  73.4 19.0 %copy-start.27 = (s32[8]{0:T(128)S(1)}, s32[8]{0:T(128)}, u32[]{:S(2)}) copy-start(s32[8]{0:T(128)} %get-tuple-element.52) | copy-start | bytes 100
  92.4 12.7 %collective-permute-start.3 = (bf16[8,64,896]{2,1,0:T(8,128)(2,1)}, bf16[8,64,896]{2,1,0:T(8,128)(2,1)}, u32[]{:S(2)}, u32[]{:S(2)}) collective-permute-start(bf16[8,64,896]{2,1,0:T(8,128)(2,1)} %gather_fusion.2), channel_id=1, source_target_pairs={{0,2},{2,0},{1,3},{3,1},{4,6},{6,4},{5,7},{7,5},{8,10},{10,8},{9,1... | collective-permute-start | bytes 2752520 | tf_op jit(solution)/shard_map/ppermute | solution.py:21
  95.6 2.9 %copy-start.2 = (bf16[2,896,1024]{2,1,0:T(8,128)(2,1)S(1)}, bf16[2,896,1024]{2,1,0:T(8,128)(2,1)}, u32[]{:S(2)}) copy-start(bf16[2,896,1024]{2,1,0:T(8,128)(2,1)} %all-gather.8.cloned.1.call-done.wk) | copy-start | bytes 11010052
  98.5 2.0 copy-start.5
  100.6 4.5 %copy-start.3 = (bf16[2,896,1024]{2,1,0:T(8,128)(2,1)S(1)}, bf16[2,896,1024]{2,1,0:T(8,128)(2,1)}, u32[]{:S(2)}) copy-start(bf16[2,896,1024]{2,1,0:T(8,128)(2,1)} %all-gather.8.cloned.1.call-done.wk) | copy-start | bytes 11010052
  100.6 4.5 %copy-start.6 = (bf16[2,896,1024]{2,1,0:T(8,128)(2,1)S(1)}, bf16[2,896,1024]{2,1,0:T(8,128)(2,1)}, u32[]{:S(2)}) copy-start(bf16[2,896,1024]{2,1,0:T(8,128)(2,1)} %all-gather.10.cloned.1.call-done.wv) | copy-start | bytes 11010052
  103.1 1.0 copy-start.8
  104.1 1.0 copy-start.10
  108.7 1.0 copy-start.12
  109.7 1.0 copy-start.14
  110.6 1.2 copy-start.9
  111.9 1.2 copy-start.11
  113.1 1.2 copy-start.13
  114.3 1.2 copy-start.15
  127.7 1.3 copy-start.18
  129.1 15.3 %copy-start.4 = (bf16[2,896,1024]{2,1,0:T(8,128)(2,1)S(1)}, bf16[2,896,1024]{2,1,0:T(8,128)(2,1)}, u32[]{:S(2)}) copy-start(bf16[2,896,1024]{2,1,0:T(8,128)(2,1)} %all-gather.8.cloned.1.call-done.wk) | copy-start | bytes 11010052
  129.1 15.3 %copy-start.7 = (bf16[2,896,1024]{2,1,0:T(8,128)(2,1)S(1)}, bf16[2,896,1024]{2,1,0:T(8,128)(2,1)}, u32[]{:S(2)}) copy-start(bf16[2,896,1024]{2,1,0:T(8,128)(2,1)} %all-gather.10.cloned.1.call-done.wv) | copy-start | bytes 11010052
  129.1 26.0 %collective-permute-start.6 = (bf16[128,4096]{1,0:T(8,128)(2,1)S(1)}, bf16[128,4096]{1,0:T(8,128)(2,1)S(1)}, u32[]{:S(2)}, u32[]{:S(2)}) collective-permute-start(bf16[128,4096]{1,0:T(8,128)(2,1)S(1)} %get-tuple-element.42), channel_id=1, source_target_pairs={{0,1},{1,0},{2,3},{3,2},{4,5},{5,4},{6,7},{7,6},{8,9},{9,8},{10,11... | collective-permute-start | bytes 3145736 | tf_op jit(solution)/shard_map/ppermute | solution.py:21
  144.4 2.6 %copy-start.16 = (f32[128,4096]{1,0:T(8,128)}, f32[128,4096]{1,0:T(8,128)S(1)}, u32[]{:S(2)}) copy-start(f32[128,4096]{1,0:T(8,128)S(1)} %get-tuple-element.33.base) | copy-start | bytes 6291460
  144.4 33.2 %collective-permute-start.4 = (bf16[128,4096]{1,0:T(8,128)(2,1)}, bf16[128,4096]{1,0:T(8,128)(2,1)S(1)}, u32[]{:S(2)}, u32[]{:S(2)}) collective-permute-start(bf16[128,4096]{1,0:T(8,128)(2,1)} %get-tuple-element.34), channel_id=1, source_target_pairs={{0,1},{1,0},{2,3},{3,2},{4,5},{5,4},{6,7},{7,6},{8,9},{9,8},{10,11... | collective-permute-start | bytes 3145736 | tf_op jit(solution)/shard_map/ppermute | solution.py:21
  146.9 9.1 %copy-start.19 = (f32[128,4096]{1,0:T(8,128)S(1)}, f32[128,4096]{1,0:T(8,128)}, u32[]{:S(2)}) copy-start(f32[128,4096]{1,0:T(8,128)} %copy-done.18) | copy-start | bytes 6291460
  155.1 1.0 copy-start.20
  156.0 1.2 copy-start.21
  157.3 20.3 %copy-start.17 = (f32[128,4096]{1,0:T(8,128)S(1)}, f32[128,4096]{1,0:T(8,128)}, u32[]{:S(2)}) copy-start(f32[128,4096]{1,0:T(8,128)} %copy-done.16) | copy-start | bytes 6291460
  174.5 22.1 %collective-permute-start.7 = (bf16[128,2048]{1,0:T(8,128)(2,1)S(1)}, bf16[128,2048]{1,0:T(8,128)(2,1)S(1)}, u32[]{:S(2)}, u32[]{:S(2)}) collective-permute-start(bf16[128,2048]{1,0:T(8,128)(2,1)S(1)} %get-tuple-element.44), channel_id=1, source_target_pairs={{0,1},{1,0},{2,3},{3,2},{4,5},{5,4},{6,7},{7,6},{8,9},{9,8},{10,11... | collective-permute-start | bytes 1572872 | tf_op jit(solution)/shard_map/ppermute | solution.py:21
  194.6 12.8 %collective-permute-start.5 = (bf16[128,2048]{1,0:T(8,128)(2,1)S(1)}, bf16[128,2048]{1,0:T(8,128)(2,1)S(1)}, u32[]{:S(2)}, u32[]{:S(2)}) collective-permute-start(bf16[128,2048]{1,0:T(8,128)(2,1)S(1)} %get-tuple-element.40), channel_id=1, source_target_pairs={{0,1},{1,0},{2,3},{3,2},{4,5},{5,4},{6,7},{7,6},{8,9},{9,8},{10,11... | collective-permute-start | bytes 1572872 | tf_op jit(solution)/shard_map/ppermute | solution.py:21
  207.4 2.0 copy-start.1
Sparse Core Ops, SparseCore 0:
  8.9 32.7 all-gather.5
  43.3 14.0 all-gather.7
  58.9 14.0 all-gather.9
  74.4 31.7 all-gather.11

commit v3 on v2

--- a/solution.py
+++ b/solution.py
@@ -13,6 +13,7 @@
 QBLOCK = 64
 NBLOCK = 128
 CHUNKS = 2
+VMEM_BYTES = 62 << 20
 F32 = jnp.float32
 BF16 = jnp.bfloat16
 
@@ -31,7 +32,7 @@
     return jnp.dot(a, b, preferred_element_type=F32)
 
 
-def encode_half(database, enc_gain, enc_up, enc_down):
+def encode_half(database, enc_gain, enc_up, enc_down, first):
     section = lax.axis_index("section")
     held = database.shape[0]
     floats = database.reshape(-1, E).astype(F32)
@@ -41,11 +42,12 @@
     mine = lax.dynamic_index_in_dim(terms, section, 1, keepdims=False)
     theirs = lax.dynamic_index_in_dim(terms, 1 - section, 1, keepdims=False)
     mine = mine + swap(theirs, "section")
+    mine, first = lax.optimization_barrier((mine, first))
     mine = mine + swap(mine.astype(BF16), "mp").astype(F32)
     rows = lax.dynamic_index_in_dim(
         database.reshape(held, 2, NBLOCK // 2, E), section, 1, keepdims=False
     )
-    return (rows.astype(F32) + mine).astype(BF16)
+    return (rows.astype(F32) + mine).astype(BF16), first
 
 
 def fetch(encoded, neighbour_ids, fill):
@@ -94,7 +96,7 @@
         in_specs=[pl.BlockSpec((tile, E), lambda i: (i, 0)), weight, weight],
         out_specs=[made, made],
         out_shape=[jax.ShapeDtypeStruct((count, out), BF16)] * 2,
-        compiler_params=pltpu.CompilerParams(vmem_limit_bytes=40 << 20),
+        compiler_params=pltpu.CompilerParams(vmem_limit_bytes=VMEM_BYTES),
         cost_estimate=pl.CostEstimate(
             flops=4 * count * E * out,
             bytes_accessed=4 * E * out + 2 * count * E + 4 * count * out,
@@ -105,27 +107,32 @@
     return k.reshape(shape), v.reshape(shape)
 
 
-def attend_heads(q, ks, vs, block, heads):
+def attend_heads(q, ks, vs, blocks, heads):
+    places = [(b, slice(h * HD, (h + 1) * HD)) for b in range(blocks) for h in range(heads)]
+    scores = []
+    for b, cols in places:
+        k = jnp.concatenate([ref[b, :, cols] for ref in ks], axis=0)
+        rows = slice(b * QBLOCK, (b + 1) * QBLOCK)
+        scores.append(
+            lax.dot_general(
+                q[rows, cols], k, (((1,), (1,)), ((), ())), preferred_element_type=F32
+            )
+        )
+    scores = jnp.concatenate(scores, axis=0)
+    e = jnp.exp(scores - jnp.max(scores, axis=-1, keepdims=True))
+    probs = (e / jnp.sum(e, axis=-1, keepdims=True)).astype(BF16)
     made = []
-    for h in range(heads):
-        cols = slice(h * HD, (h + 1) * HD)
-        k = jnp.concatenate([ref[block, :, cols] for ref in ks], axis=0)
-        v = jnp.concatenate([ref[block, :, cols] for ref in vs], axis=0)
-        scores = lax.dot_general(
-            q[:, cols], k, (((1,), (1,)), ((), ())), preferred_element_type=F32
-        )
-        e = jnp.exp(scores - jnp.max(scores, axis=-1, keepdims=True))
-        probs = (e / jnp.sum(e, axis=-1, keepdims=True)).astype(BF16)
-        made.append(mm(probs, v).astype(BF16))
-    return jnp.concatenate(made, axis=1)
+    for i, (b, cols) in enumerate(places):
+        v = jnp.concatenate([ref[b, :, cols] for ref in vs], axis=0)
+        made.append(mm(probs[i * QBLOCK : (i + 1) * QBLOCK], v).astype(BF16))
+    rows = [jnp.concatenate(made[b * heads : (b + 1) * heads], axis=1) for b in range(blocks)]
+    return jnp.concatenate(rows, axis=0)
 
 
 def first_kernel(blocks, heads, q, ka, kb, va, vb, wo, state, send, base, ctx):
     @pl.when(pl.program_id(0) == 0)
     def _():
-        for b in range(blocks):
-            rows = slice(b * QBLOCK, (b + 1) * QBLOCK)
-            ctx[rows, :] = attend_heads(q[rows, :], (ka, kb), (va, vb), b, heads)
+        ctx[...] = attend_heads(q[...], (ka, kb), (va, vb), blocks, heads)
 
     terms = mm(ctx[...], wo[0])
     send[...] = terms.astype(BF16)
@@ -157,7 +164,7 @@
             jax.ShapeDtypeStruct((piece, width), F32),
         ],
         scratch_shapes=[pltpu.VMEM((piece, inner), BF16)],
-        compiler_params=pltpu.CompilerParams(vmem_limit_bytes=40 << 20),
+        compiler_params=pltpu.CompilerParams(vmem_limit_bytes=VMEM_BYTES),
         cost_estimate=pl.CostEstimate(
             flops=2 * piece * inner * (width + 512),
             bytes_accessed=2 * inner * width + 8 * piece * width,
@@ -183,9 +190,7 @@
     def _():
         q = (mm(normed[...], wq[0]) * HD ** (-0.5)).astype(BF16)
         cols = pl.ds(pl.multiple_of(j * q_tile, q_tile), q_tile)
-        for b in range(blocks):
-            rows = slice(b * QBLOCK, (b + 1) * QBLOCK)
-            ctx[rows, cols] = attend_heads(q[rows, :], (ka, kb), (va, vb), b, q_tile // HD)
+        ctx[:, cols] = attend_heads(q, (ka, kb), (va, vb), blocks, q_tile // HD)
 
     @pl.when((j >= q_steps) & (j < q_steps + away))
     def _():
@@ -248,7 +253,7 @@
             jax.ShapeDtypeStruct((piece, width // 2), BF16),
             jax.ShapeDtypeStruct((piece, width // 2), F32),
         ],
-        compiler_params=pltpu.CompilerParams(vmem_limit_bytes=40 << 20),
+        compiler_params=pltpu.CompilerParams(vmem_limit_bytes=VMEM_BYTES),
         cost_estimate=pl.CostEstimate(
             flops=4 * piece * inner * width,
             bytes_accessed=4 * inner * width + 12 * piece * width,
@@ -274,10 +279,9 @@
     mp = lax.axis_index("mp")
     tokens = hidden_in.shape[0] // 2
 
-    encoded = encode_half(database, enc_gain, enc_up, enc_down)
     entering = lax.dynamic_slice_in_dim(hidden_in, section * tokens, tokens, 0)
-    encoded, entering = lax.optimization_barrier((encoded, entering))
     other = swap(entering, "mp")
+    encoded, other = encode_half(database, enc_gain, enc_up, enc_down, other)
     state = jnp.where(
         mp == 0,
         jnp.concatenate([entering, other], axis=1),

time: 217 us -> 224 us (1.032)
  waiting for transfers between devices: 59.1 us -> 80.9 us
  local copies, waits for them, and re-layouts: 31.1 us -> 14.5 us
  Pallas kernels: 72.2 us -> 75 us
    all_to_all x1, waiting for transfers between devices: 9.63 us -> 28.5 us  [fetch(): lax.all_to_all(payload, 'db', split_axis=0, concat_axis=0, tiled=True)]
    unnamed x59 -> x23, local copies, waits for them, and re-layouts: 18.8 us -> 2.68 us
    pallas_call x4, Pallas kernels: 12.3 us -> 22.2 us  [keys_values(): pl.pallas_call(kv_kernel, grid=(count // tile,), in_specs=[pl.BlockSpec((...]
    pallas_call x2, Pallas kernels: 25.6 us -> 20 us  [first_layer(): pl.pallas_call(functools.partial(first_kernel, blocks, inner // HD), grid...]
    ppermute x8, waiting for transfers between devices: 46.8 us -> 49.8 us  [swap(): return lax.ppermute(block, axis, [(0, 1), (1, 0)])]
    add x0 -> x1, other arithmetic: none -> 2.26 us  [encode_half(): mine = mine + swap(theirs, 'section')]
  transfers between devices with their start and end apart: 13 -> 13, of which waited for: 7 -> 6; matrix products, arithmetic and copies ran while one was open for 15% -> 14% of each run, Pallas kernels for 28% -> 29%
where the time goes in v3:
time: 224 us; the launch traced here: 223 us
  waiting for transfers between devices  80.9 us (36%)
  Pallas kernels  75 us (33%)
  starting transfers between devices  16.3 us (7%)
  local copies, waits for them, and re-layouts  14.5 us (6%)
  between operations  13.3 us (6%)
  matrix products  11.1 us (5%)
  other arithmetic  10.1 us (5%)
    ppermute x8, waiting for transfers between devices, swap(): return lax.ppermute(block, axis, [(0, 1), (1, 0)])  49.8 us
    pallas_call x2, Pallas kernels, second_layer(): pl.pallas_call(functools.partial(second_kernel, blocks, q_steps, away), g...  32.8 us
    all_to_all x1, waiting for transfers between devices, fetch(): lax.all_to_all(payload, 'db', split_axis=0, concat_axis=0, tiled=True)  28.5 us
    pallas_call x4, Pallas kernels, keys_values(): pl.pallas_call(kv_kernel, grid=(count // tile,), in_specs=[pl.BlockSpec((...  22.2 us
    pallas_call x2, Pallas kernels, first_layer(): pl.pallas_call(functools.partial(first_kernel, blocks, inner // HD), grid...  20 us
    dot_general x2, matrix products, mm(): return jnp.dot(a, b, preferred_element_type=F32)  11.1 us
    ppermute x8, starting transfers between devices, swap(): return lax.ppermute(block, axis, [(0, 1), (1, 0)])  10.2 us
    all_to_all x1, starting transfers between devices, fetch(): lax.all_to_all(payload, 'db', split_axis=0, concat_axis=0, tiled=True)  6.02 us
  transfers between devices with their start and end apart: 13, of which 6 were waited for; matrix products, arithmetic and copies ran while one was open for 14% of the time, Pallas kernels for 29%

profile of v3, /device:TPU:0, one launch (start us, length us, event | category | flops | bytes accessed | tf_op | source)
XLA Modules:
  0.0 223.2 jit_solution(2619275667800330795)
XLA Ops:
  6.5 0.7 all-gather.6.cloned.1.call-update
  7.3 0.0 all-gather.8.cloned.1.call-start
  7.3 0.7 all-gather.8.cloned.1.call-update
  8.0 0.0 all-gather.10.cloned.1.call-start
  8.1 0.7 all-gather.10.cloned.1.call-update
  8.8 0.0 all-gather.12.cloned.1.call-start
  8.8 0.5 all-gather.12.cloned.1.call-update
  9.3 0.6 copy-done.3
  9.9 0.3 multiply_reduce_fusion
  10.2 0.3 fusion.8
  10.5 3.8 %fusion.24 = f32[512,896]{1,0:T(8,128)} fusion(bf16[512,896]{1,0:T(8,128)(2,1)S(1)} %copy-done, bf16[512,896]{1,0:T(8,128)(2,1)S(1)} %fusion.8, bf16[896,512]{1,0:T(8,128)(2,1)} %param.15), kind=kOutput, calls=%fused_computation.35 | convolution fusion | flops 941883392 | bytes 4587520 | tf_op jit(solution)/shard_map/dot_general | solution.py:32
  14.3 1.3 dynamic-slice_bitcast_fusion
  15.6 0.5 collective-permute-start
  16.1 2.3 %constant_dynamic-slice_fusion.4 = bf16[256,2048]{1,0:T(8,128)(2,1)} fusion(bf16[512,2048]{1,0:T(8,128)(2,1)} %param.11, s32[]{:T(128)S(6)} %select_n.87), kind=kLoop, calls=%fused_computation.66 | loop fusion | bytes 2097156 | tf_op jit(solution)/shard_map/dynamic_slice | solution.py:282
  18.4 2.8 %collective-permute-start.1 = (bf16[256,2048]{1,0:T(8,128)(2,1)}, bf16[256,2048]{1,0:T(8,128)(2,1)S(1)}, u32[]{:S(2)}, u32[]{:S(2)}) collective-permute-start(bf16[256,2048]{1,0:T(8,128)(2,1)} %constant_dynamic-slice_fusion.4), channel_id=1, source_target_pairs={{0,1},{1,0},{2,3},{3,2},{4,5},{5,4},{6,7},{7,6},{8,9},{9,8},{10,11... | collective-permute-start | bytes 3145736 | tf_op jit(solution)/shard_map/ppermute | solution.py:22
  21.1 0.1 copy.18
  21.2 0.1 reshape.258
  21.3 0.0 collective-permute-done
  21.4 2.3 %bitcast_add_fusion = f32[4,64,896]{2,1,0:T(8,128)S(1)} fusion(f32[4,64,896]{2,1,0:T(8,128)} %collective-permute-done, f32[4,2,64,896]{3,2,1,0:T(8,128)} %bitcast.86, s32[]{:T(128)S(6)} %select_n.85), kind=kLoop, calls=%fused_computation.33 | loop fusion | flops 229376 | bytes 2752516 | tf_op jit(solution)/shard_map/add | solution.py:44
  23.6 21.5 %collective-permute-done.1 = bf16[256,2048]{1,0:T(8,128)(2,1)S(1)} collective-permute-done((bf16[256,2048]{1,0:T(8,128)(2,1)}, bf16[256,2048]{1,0:T(8,128)(2,1)S(1)}, u32[]{:S(2)}, u32[]{:S(2)}) %collective-permute-start.1) | collective-permute-done | bytes 1048608 | tf_op jit(solution)/shard_map/ppermute | solution.py:22
  45.1 0.9 convert_element_type.62
  46.1 1.7 collective-permute-start.2
  47.8 0.3 convert_reduce_fusion
  48.1 0.2 select_reduce_fusion
  48.3 0.1 copy.19
  48.3 0.1 reshape.274
  48.4 10.2 %collective-permute-done.2 = bf16[4,64,896]{2,1,0:T(8,128)(2,1)S(1)} collective-permute-done((bf16[4,64,896]{2,1,0:T(8,128)(2,1)}, bf16[4,64,896]{2,1,0:T(8,128)(2,1)S(1)}, u32[]{:S(2)}, u32[]{:S(2)}) %collective-permute-start.2) | collective-permute-done | bytes 458784 | tf_op jit(solution)/shard_map/ppermute | solution.py:22
  58.6 0.2 fusion.23
  58.8 2.0 gather_fusion
  60.8 6.0 %all-to-all-start = ((bf16[8,2,64,896]{3,2,1,0:T(8,128)(2,1)}), bf16[8,2,64,896]{3,2,1,0:T(8,128)(2,1)}, u32[]{:S(2)}, u32[]{:S(2)}) async-start(bf16[8,2,64,896]{3,2,1,0:T(8,128)(2,1)} %bitcast.9), calls=%async_computation | async-start | bytes 3670016 | tf_op jit(solution)/shard_map/all_to_all | solution.py:76
  66.8 0.1 add.144
  66.9 2.0 all-gather
  68.9 0.6 slice_bitcast_fusion.6
  69.5 3.2 %fusion.1 = (f32[256]{0:T(256)S(1)}, bf16[256,4096]{1,0:T(8,128)(2,1)S(1)}) fusion(bf16[256,2048]{1,0:T(8,128)(2,1)} %constant_dynamic-slice_fusion.4, bf16[256,2048]{1,0:T(8,128)(2,1)} %copy-done.5, pred[]{:T(512)S(6)} %eq.50), kind=kLoop, calls=%fused_computation.7 | loop fusion | flops 12582656 | bytes 4195329 | tf_op jit(solution)/shard_map/reduce_sum | solution.py:27
  72.7 0.0 copy-start.2
  72.7 0.0 all-gather.6.cloned.1.call-done.wq
  72.7 7.3 %fusion.12.q = bf16[256,1024]{1,0:T(8,128)(2,1)} fusion(bf16[2,4096,1024]{2,1,0:T(8,128)(2,1)} %all-gather.6.cloned.1.call-done.wq, bf16[256,4096]{1,0:T(8,128)(2,1)S(1)} %get-tuple-element.46.state, f32[4096]{0:T(1024)S(1)} %bitcast.88, f32[256]{0:T(256)S(1)} %add_rsqrt_fusion), kind=kOutput, calls=%fused_computation.19 | convolution fusion | flops 2152202240 | bytes 11027456 | tf_op jit(solution)/shard_map/dot_general | solution.py:32
  80.0 28.5 %all-to-all-done = bf16[8,2,64,896]{3,2,1,0:T(8,128)(2,1)} async-done(((bf16[8,2,64,896]{3,2,1,0:T(8,128)(2,1)}), bf16[8,2,64,896]{3,2,1,0:T(8,128)(2,1)}, u32[]{:S(2)}, u32[]{:S(2)}) %all-to-all-start) | async-done | bytes 1835040 | tf_op jit(solution)/shard_map/all_to_all | solution.py:76
  108.5 2.2 gather_fusion.2
  110.7 0.1 collective-permute-start.3
  110.8 3.1 %gather_fusion.1 = bf16[8,64,896]{2,1,0:T(8,128)(2,1)} fusion(bf16[16,64,896]{2,1,0:T(8,128)(2,1)} %bitcast.13, s32[1024]{0:T(1024)S(1)} %pad_clamp_fusion.1), kind=kCustom, calls=%fused_computation.1 | custom fusion | bytes 1835040 | tf_op jit(solution)/shard_map/gather | solution.py:80
  113.9 5.6 %shard_map.109 = (bf16[512,1024]{1,0:T(8,128)(2,1)}, bf16[512,1024]{1,0:T(8,128)(2,1)}) custom-call(bf16[512,896]{1,0:T(8,128)(2,1)} %bitcast.64, bf16[2,896,1024]{2,1,0:T(8,128)(2,1)} %all-gather.8.cloned.1.call-done.wk, bf16[2,896,1024]{2,1,0:T(8,128)(2,1)} %all-gather.10.cloned.1.call-done.wv), custom_call_target="tpu_custom_call" | custom-call | flops 1879048192 | bytes 6684672 | tf_op jit(solution)/shard_map/pallas_call | solution.py:93
  119.4 0.0 collective-permute-done.3
  119.5 1.0 copy-done.4
  120.4 5.5 %shard_map.110 = (bf16[512,1024]{1,0:T(8,128)(2,1)}, bf16[512,1024]{1,0:T(8,128)(2,1)}) custom-call(bf16[512,896]{1,0:T(8,128)(2,1)} %bitcast.83, bf16[2,896,1024]{2,1,0:T(8,128)(2,1)} %all-gather.8.cloned.1.call-done.wk, bf16[2,896,1024]{2,1,0:T(8,128)(2,1)} %all-gather.10.cloned.1.call-done.wv), custom_call_target="tpu_custom_call" | custom-call | flops 1879048192 | bytes 6684672 | tf_op jit(solution)/shard_map/pallas_call | solution.py:93
  125.9 10.0 %shard_map.115 = (bf16[128,4096]{1,0:T(8,128)(2,1)}, f32[128,4096]{1,0:T(8,128)}) custom-call(bf16[256,1024]{1,0:T(8,128)(2,1)} %fusion.12.q, bf16[4,128,1024]{2,1,0:T(8,128)(2,1)} %bitcast.75, bf16[4,128,1024]{2,1,0:T(8,128)(2,1)} %bitcast.79, bf16[4,128,1024]{2,1,0:T(8,128)(2,1)} %bitcast.77, bf16[4,128,1024]{2,1,0:T(8,128)(2,1)} %bitcast.81, ...), custom_call_target="tpu_custom_call" | custom-call | flops 1207959552 | bytes 12582912 | tf_op jit(solution)/shard_map/pallas_call | solution.py:149
  135.9 1.5 collective-permute-start.6
  137.5 10.0 %shard_map.111 = (bf16[128,4096]{1,0:T(8,128)(2,1)}, f32[128,4096]{1,0:T(8,128)}) custom-call(bf16[256,1024]{1,0:T(8,128)(2,1)} %fusion.12.q, bf16[4,128,1024]{2,1,0:T(8,128)(2,1)} %bitcast.76, bf16[4,128,1024]{2,1,0:T(8,128)(2,1)} %bitcast.80, bf16[4,128,1024]{2,1,0:T(8,128)(2,1)} %bitcast.78, bf16[4,128,1024]{2,1,0:T(8,128)(2,1)} %bitcast.82, ...), custom_call_target="tpu_custom_call" | custom-call | flops 1207959552 | bytes 12582912 | tf_op jit(solution)/shard_map/pallas_call | solution.py:149
  147.5 0.5 collective-permute-start.4
  148.0 5.5 %shard_map.112 = (bf16[512,1024]{1,0:T(8,128)(2,1)}, bf16[512,1024]{1,0:T(8,128)(2,1)}) custom-call(bf16[512,896]{1,0:T(8,128)(2,1)} %bitcast.65, bf16[2,896,1024]{2,1,0:T(8,128)(2,1)} %all-gather.8.cloned.1.call-done.wk, bf16[2,896,1024]{2,1,0:T(8,128)(2,1)} %all-gather.10.cloned.1.call-done.wv), custom_call_target="tpu_custom_call" | custom-call | flops 1879048192 | bytes 6684672 | tf_op jit(solution)/shard_map/pallas_call | solution.py:93
  153.5 5.5 %shard_map.113 = (bf16[512,1024]{1,0:T(8,128)(2,1)}, bf16[512,1024]{1,0:T(8,128)(2,1)}) custom-call(bf16[512,896]{1,0:T(8,128)(2,1)} %bitcast.84, bf16[2,896,1024]{2,1,0:T(8,128)(2,1)} %all-gather.8.cloned.1.call-done.wk, bf16[2,896,1024]{2,1,0:T(8,128)(2,1)} %all-gather.10.cloned.1.call-done.wv), custom_call_target="tpu_custom_call" | custom-call | flops 1879048192 | bytes 6684672 | tf_op jit(solution)/shard_map/pallas_call | solution.py:93
  159.1 3.1 %collective-permute-done.6.arrived = bf16[128,4096]{1,0:T(8,128)(2,1)} collective-permute-done((bf16[128,4096]{1,0:T(8,128)(2,1)}, bf16[128,4096]{1,0:T(8,128)(2,1)}, u32[]{:S(2)}, u32[]{:S(2)}) %collective-permute-start.6) | collective-permute-done | bytes 1048608 | tf_op jit(solution)/shard_map/ppermute | solution.py:22
  162.2 16.4 %shard_map.116 = (bf16[128,2048]{1,0:T(8,128)(2,1)}, f32[128,2048]{1,0:T(8,128)}) custom-call(s32[1]{0:T(128)} %bitcast.mp, f32[128,4096]{1,0:T(8,128)} %get-tuple-element.41.base, bf16[128,4096]{1,0:T(8,128)(2,1)} %collective-permute-done.6.arrived, f32[1,4096]{1,0:T(1,128)} %get-tuple-element.49.gain, ...), custom_call_target="tpu_custom_call" | custom-call | flops 2147483648 | bytes 23068672 | tf_op jit(solution)/shard_map/pallas_call | solution.py:222
  178.6 1.5 collective-permute-start.7
  180.1 4.4 %collective-permute-done.4.arrived = bf16[128,4096]{1,0:T(8,128)(2,1)S(1)} collective-permute-done((bf16[128,4096]{1,0:T(8,128)(2,1)}, bf16[128,4096]{1,0:T(8,128)(2,1)S(1)}, u32[]{:S(2)}, u32[]{:S(2)}) %collective-permute-start.4) | collective-permute-done | bytes 1048608 | tf_op jit(solution)/shard_map/ppermute | solution.py:22
  184.6 1.0 copy-done.6
  185.5 16.4 %shard_map.114 = (bf16[128,2048]{1,0:T(8,128)(2,1)}, f32[128,2048]{1,0:T(8,128)}) custom-call(s32[1]{0:T(128)} %bitcast.mp, f32[128,4096]{1,0:T(8,128)} %get-tuple-element.33.base, bf16[128,4096]{1,0:T(8,128)(2,1)} %copy-done.6, f32[1,4096]{1,0:T(1,128)} %get-tuple-element.49.gain, bf16[2,4096,1024]{2,1,0:T(8,128)(2,1)} %all-gather.6.cloned.1.call-done.wq, ...), custom_call_target="tpu_custom_call" | custom-call | flops 2147483648 | bytes 23068672 | tf_op jit(solution)/shard_map/pallas_call | solution.py:222
  202.0 1.6 collective-permute-start.5
  203.5 0.0 collective-permute-done.7
  203.6 1.3 add_convert_fusion
  204.9 10.5 %collective-permute-done.5 = bf16[128,2048]{1,0:T(8,128)(2,1)S(1)} collective-permute-done((bf16[128,2048]{1,0:T(8,128)(2,1)}, bf16[128,2048]{1,0:T(8,128)(2,1)S(1)}, u32[]{:S(2)}, u32[]{:S(2)}) %collective-permute-start.5) | collective-permute-done | bytes 524320 | tf_op jit(solution)/shard_map/ppermute | solution.py:22
  215.4 0.1 add_convert_fusion.1
  215.5 1.1 pad_maximum_fusion
  216.6 0.1 copy-done.1
  (32 shorter events, 0.1 us)
Async XLA Ops:
  6.5 3.9 %copy-start = (bf16[512,896]{1,0:T(8,128)(2,1)S(1)}, bf16[512,896]{1,0:T(8,128)(2,1)}, u32[]{:S(2)}) copy-start(bf16[512,896]{1,0:T(8,128)(2,1)} %param.16) | copy-start | bytes 2752516
  6.5 66.2 %all-gather.6.cloned.1.call-start = ((), (), s32[]{:S(2)}) async-start(), calls=%async_computation.1 | async-start | bytes 25165824 | tf_op jit(solution)/shard_map/all_gather | solution.py:291
  7.3 106.6 %all-gather.8.cloned.1.call-start = ((), (), s32[]{:S(2)}) async-start(), calls=%async_computation.2 | async-start | bytes 5505024 | tf_op jit(solution)/shard_map/all_gather | solution.py:292
  8.0 105.9 %all-gather.10.cloned.1.call-start = ((), (), s32[]{:S(2)}) async-start(), calls=%async_computation.3 | async-start | bytes 5505024 | tf_op jit(solution)/shard_map/all_gather | solution.py:293
  8.7 1.2 copy-start.3
  8.8 1.4 copy-start.9
  8.8 117.2 %all-gather.12.cloned.1.call-start = ((), (), s32[]{:S(2)}) async-start(), calls=%async_computation.4 | async-start | bytes 25165824 | tf_op jit(solution)/shard_map/all_gather | solution.py:294
  14.3 6.8 %copy-start.10 = (s32[64,2]{0,1:T(2,128)S(1)}, s32[64,2]{0,1:T(2,128)}, u32[]{:S(2)}) copy-start(s32[64,2]{0,1:T(2,128)} %param.13) | copy-start | bytes 1540
  15.6 5.8 %collective-permute-start = (f32[4,64,896]{2,1,0:T(8,128)S(1)}, f32[4,64,896]{2,1,0:T(8,128)}, u32[]{:S(2)}, u32[]{:S(2)}) collective-permute-start(f32[4,64,896]{2,1,0:T(8,128)S(1)} %dynamic-slice_bitcast_fusion), channel_id=1, source_target_pairs={{0,2},{2,0},{1,3},{3,1},{4,6},{6,4},{5,7},{7,5},{8,10},{10,8},{9,1... | collective-permute-start | bytes 2752520 | tf_op jit(solution)/shard_map/ppermute | solution.py:22
  18.4 26.8 %collective-permute-start.1 = (bf16[256,2048]{1,0:T(8,128)(2,1)}, bf16[256,2048]{1,0:T(8,128)(2,1)S(1)}, u32[]{:S(2)}, u32[]{:S(2)}) collective-permute-start(bf16[256,2048]{1,0:T(8,128)(2,1)} %constant_dynamic-slice_fusion.4), channel_id=1, source_target_pairs={{0,1},{1,0},{2,3},{3,2},{4,5},{5,4},{6,7},{7,6},{8,9},{9,8},{10,11... | collective-permute-start | bytes 3145736 | tf_op jit(solution)/shard_map/ppermute | solution.py:22
  45.1 13.5 %copy-start.5 = (bf16[256,2048]{1,0:T(8,128)(2,1)}, bf16[256,2048]{1,0:T(8,128)(2,1)S(1)}, u32[]{:S(2)}) copy-start(bf16[256,2048]{1,0:T(8,128)(2,1)S(1)} %collective-permute-done.1) | copy-start | bytes 3145732
  46.1 12.5 %collective-permute-start.2 = (bf16[4,64,896]{2,1,0:T(8,128)(2,1)}, bf16[4,64,896]{2,1,0:T(8,128)(2,1)S(1)}, u32[]{:S(2)}, u32[]{:S(2)}) collective-permute-start(bf16[4,64,896]{2,1,0:T(8,128)(2,1)} %convert_element_type.62), channel_id=1, source_target_pairs={{0,1},{1,0},{2,3},{3,2},{4,5},{5,4},{6,7},{7,6},{8,9},{9,8},{10,11... | collective-permute-start | bytes 1376264 | tf_op jit(solution)/shard_map/ppermute | solution.py:22
  60.8 6.1 %copy-start.8 = (f32[1,4096]{1,0:T(1,128)S(1)}, f32[1,4096]{1,0:T(1,128)}, u32[]{:S(2)}) copy-start(f32[1,4096]{1,0:T(1,128)} %param.17) | copy-start | bytes 49156
  60.8 47.7 %all-to-all-start = ((bf16[8,2,64,896]{3,2,1,0:T(8,128)(2,1)}), bf16[8,2,64,896]{3,2,1,0:T(8,128)(2,1)}, u32[]{:S(2)}, u32[]{:S(2)}) async-start(bf16[8,2,64,896]{3,2,1,0:T(8,128)(2,1)} %bitcast.9), calls=%async_computation | async-start | bytes 3670016 | tf_op jit(solution)/shard_map/all_to_all | solution.py:76
  72.7 7.3 %copy-start.2 = (bf16[256,4096]{1,0:T(8,128)(2,1)}, bf16[256,4096]{1,0:T(8,128)(2,1)S(1)}, u32[]{:S(2)}) copy-start(bf16[256,4096]{1,0:T(8,128)(2,1)S(1)} %get-tuple-element.46.state) | copy-start | bytes 6291460
  110.7 8.7 %collective-permute-start.3 = (bf16[8,64,896]{2,1,0:T(8,128)(2,1)S(1)}, bf16[8,64,896]{2,1,0:T(8,128)(2,1)S(1)}, u32[]{:S(2)}, u32[]{:S(2)}) collective-permute-start(bf16[8,64,896]{2,1,0:T(8,128)(2,1)S(1)} %gather_fusion.2), channel_id=1, source_target_pairs={{0,2},{2,0},{1,3},{3,1},{4,6},{6,4},{5,7},{7,5},{8,10},{10,8},{9,1... | collective-permute-start | bytes 2752520 | tf_op jit(solution)/shard_map/ppermute | solution.py:22
  119.4 1.0 copy-start.4
  135.9 26.3 %collective-permute-start.6 = (bf16[128,4096]{1,0:T(8,128)(2,1)}, bf16[128,4096]{1,0:T(8,128)(2,1)}, u32[]{:S(2)}, u32[]{:S(2)}) collective-permute-start(bf16[128,4096]{1,0:T(8,128)(2,1)} %get-tuple-element.42), channel_id=1, source_target_pairs={{0,1},{1,0},{2,3},{3,2},{4,5},{5,4},{6,7},{7,6},{8,9},{9,8},{10,11... | collective-permute-start | bytes 3145736 | tf_op jit(solution)/shard_map/ppermute | solution.py:22
  147.5 37.1 %collective-permute-start.4 = (bf16[128,4096]{1,0:T(8,128)(2,1)}, bf16[128,4096]{1,0:T(8,128)(2,1)S(1)}, u32[]{:S(2)}, u32[]{:S(2)}) collective-permute-start(bf16[128,4096]{1,0:T(8,128)(2,1)} %get-tuple-element.34), channel_id=1, source_target_pairs={{0,1},{1,0},{2,3},{3,2},{4,5},{5,4},{6,7},{7,6},{8,9},{9,8},{10,11... | collective-permute-start | bytes 3145736 | tf_op jit(solution)/shard_map/ppermute | solution.py:22
  178.6 24.9 %collective-permute-start.7 = (bf16[128,2048]{1,0:T(8,128)(2,1)}, bf16[128,2048]{1,0:T(8,128)(2,1)S(1)}, u32[]{:S(2)}, u32[]{:S(2)}) collective-permute-start(bf16[128,2048]{1,0:T(8,128)(2,1)} %get-tuple-element.44), channel_id=1, source_target_pairs={{0,1},{1,0},{2,3},{3,2},{4,5},{5,4},{6,7},{7,6},{8,9},{9,8},{10,11... | collective-permute-start | bytes 1572872 | tf_op jit(solution)/shard_map/ppermute | solution.py:22
  184.6 1.0 copy-start.6
  202.0 13.4 %copy-start.7 = (f32[128,2048]{1,0:T(8,128)S(1)}, f32[128,2048]{1,0:T(8,128)}, u32[]{:S(2)}) copy-start(f32[128,2048]{1,0:T(8,128)} %get-tuple-element.39) | copy-start | bytes 3145732
  202.0 13.4 %collective-permute-start.5 = (bf16[128,2048]{1,0:T(8,128)(2,1)}, bf16[128,2048]{1,0:T(8,128)(2,1)S(1)}, u32[]{:S(2)}, u32[]{:S(2)}) collective-permute-start(bf16[128,2048]{1,0:T(8,128)(2,1)} %get-tuple-element.40), channel_id=1, source_target_pairs={{0,1},{1,0},{2,3},{3,2},{4,5},{5,4},{6,7},{7,6},{8,9},{9,8},{10,11... | collective-permute-start | bytes 1572872 | tf_op jit(solution)/shard_map/ppermute | solution.py:22
  215.4 1.3 copy-start.1
Sparse Core Ops, SparseCore 0:
  8.9 32.7 all-gather.5
  43.3 14.0 all-gather.7
  58.9 14.0 all-gather.9
  74.4 31.2 all-gather.11

commit v4 on v3

--- a/solution.py
+++ b/solution.py
@@ -32,8 +32,9 @@
     return jnp.dot(a, b, preferred_element_type=F32)
 
 
-def encode_half(database, enc_gain, enc_up, enc_down, first):
+def encode_quarter(database, enc_gain, enc_up, enc_down):
     section = lax.axis_index("section")
+    mp = lax.axis_index("mp")
     held = database.shape[0]
     floats = database.reshape(-1, E).astype(F32)
     normed = rms_scale(floats, enc_gain).astype(BF16)
@@ -41,13 +42,14 @@
     terms = mm(inner, enc_down).reshape(held, 2, NBLOCK // 2, E)
     mine = lax.dynamic_index_in_dim(terms, section, 1, keepdims=False)
     theirs = lax.dynamic_index_in_dim(terms, 1 - section, 1, keepdims=False)
-    mine = mine + swap(theirs, "section")
-    mine, first = lax.optimization_barrier((mine, first))
-    mine = mine + swap(mine.astype(BF16), "mp").astype(F32)
+    mine = (mine + swap(theirs, "section")).reshape(held, 2, NBLOCK // 4, E)
+    away = lax.dynamic_index_in_dim(mine, 1 - mp, 1, keepdims=False)
+    home = lax.dynamic_index_in_dim(mine, mp, 1, keepdims=False)
+    home = home + swap(away.astype(BF16), "mp").astype(F32)
     rows = lax.dynamic_index_in_dim(
-        database.reshape(held, 2, NBLOCK // 2, E), section, 1, keepdims=False
-    )
-    return (rows.astype(F32) + mine).astype(BF16), first
+        database.reshape(held, 4, NBLOCK // 4, E), section * 2 + mp, 1, keepdims=False
+    )
+    return (rows.astype(F32) + home).astype(BF16)
 
 
 def fetch(encoded, neighbour_ids, fill):
@@ -75,9 +77,13 @@
     payload = encoded[send_local]
     received = lax.all_to_all(payload, "db", split_axis=0, concat_axis=0, tiled=True)
     received, fill = lax.optimization_barrier((received, fill))
-    received = received.reshape(db_count * capacity, NBLOCK // 2, E)
+    received = received.reshape(db_count * capacity, NBLOCK // 4, E)
     moved = swap(received[theirs], "section")
-    return received[mine].reshape(-1, E), moved.reshape(-1, E), fill
+    groups = request // 2 // NEIGH
+    near = jnp.concatenate(
+        [received[mine].reshape(groups, -1, E), moved.reshape(groups, -1, E)], axis=1
+    ).reshape(-1, E)
+    return near, swap(near, "mp"), fill
 
 
 def kv_kernel(rows, wk, wv, k, v):
@@ -143,7 +149,7 @@
     ka, kb, va, vb = kv
     blocks = piece // QBLOCK
     inner, width = wo.shape[1], wo.shape[2]
-    tile = 512
+    tile = 1024
     around = pl.BlockSpec((blocks, NBLOCK, inner), lambda j: (part, 0, 0))
     made = pl.BlockSpec((piece, tile), lambda j: (0, j))
     return pl.pallas_call(
@@ -207,7 +213,7 @@
     piece, width = base.shape
     blocks = piece // QBLOCK
     inner = wo.shape[1]
-    q_tile, tile = 256, 512
+    q_tile, tile = 256, 1024
     q_steps = inner // q_tile
     away = width // 2 // tile
     around = pl.BlockSpec(
@@ -280,8 +286,9 @@
     tokens = hidden_in.shape[0] // 2
 
     entering = lax.dynamic_slice_in_dim(hidden_in, section * tokens, tokens, 0)
+    encoded = encode_quarter(database, enc_gain, enc_up, enc_down)
+    encoded, entering = lax.optimization_barrier((encoded, entering))
     other = swap(entering, "mp")
-    encoded, other = encode_half(database, enc_gain, enc_up, enc_down, other)
     state = jnp.where(
         mp == 0,
         jnp.concatenate([entering, other], axis=1),

time: 224 us -> 200 us (0.89)
  waiting for transfers between devices: 80.9 us -> 69.6 us
  Pallas kernels: 75 us -> 67.3 us
  local copies, waits for them, and re-layouts: 14.5 us -> 7.8 us
  starting transfers between devices: 16.3 us -> 18.6 us
    all_to_all x1, waiting for transfers between devices: 28.5 us -> 0.01 us  [fetch(): lax.all_to_all(payload, 'db', split_axis=0, concat_axis=0, tiled=True)]
    ppermute x8 -> x9, waiting for transfers between devices: 49.8 us -> 65.6 us  [swap(): return lax.ppermute(block, axis, [(0, 1), (1, 0)])]
    pallas_call x2, Pallas kernels: 20 us -> 16 us  [first_layer(): pl.pallas_call(functools.partial(first_kernel, blocks, inner // HD), grid...]
    pallas_call x2, Pallas kernels: 32.8 us -> 29.1 us  [second_layer(): pl.pallas_call(functools.partial(second_kernel, blocks, q_steps, away), g...]
    gather x1, local copies, waits for them, and re-layouts: 3.09 us -> 0.62 us  [fetch(): received[mine].reshape(groups, -1, E)]
    ppermute x8 -> x9, starting transfers between devices: 10.2 us -> 12.4 us  [swap(): return lax.ppermute(block, axis, [(0, 1), (1, 0)])]
  transfers between devices with their start and end apart: 13 -> 14, of which waited for: 6 -> 8; matrix products, arithmetic and copies ran while one was open for 14% -> 12% of each run, Pallas kernels for 29% -> 30%
where the time goes in v4:
time: 200 us; the launch traced here: 199 us
  waiting for transfers between devices  69.6 us (35%)
  Pallas kernels  67.3 us (34%)
  starting transfers between devices  18.6 us (9%)
  between operations  13.4 us (7%)
  matrix products  12 us (6%)
  other arithmetic  8.28 us (4%)
  local copies, waits for them, and re-layouts  7.8 us (4%)
    ppermute x9, waiting for transfers between devices, swap(): return lax.ppermute(block, axis, [(0, 1), (1, 0)])  65.6 us
    pallas_call x2, Pallas kernels, second_layer(): pl.pallas_call(functools.partial(second_kernel, blocks, q_steps, away), g...  29.1 us
    pallas_call x4, Pallas kernels, keys_values(): pl.pallas_call(kv_kernel, grid=(count // tile,), in_specs=[pl.BlockSpec((...  22.2 us
    pallas_call x2, Pallas kernels, first_layer(): pl.pallas_call(functools.partial(first_kernel, blocks, inner // HD), grid...  16 us
    ppermute x9, starting transfers between devices, swap(): return lax.ppermute(block, axis, [(0, 1), (1, 0)])  12.4 us
    dot_general x2, matrix products, mm(): return jnp.dot(a, b, preferred_element_type=F32)  12 us
    all_to_all x1, starting transfers between devices, fetch(): lax.all_to_all(payload, 'db', split_axis=0, concat_axis=0, tiled=True)  6.09 us
  transfers between devices with their start and end apart: 14, of which 8 were waited for; matrix products, arithmetic and copies ran while one was open for 12% of the time, Pallas kernels for 30%

profile of v4, /device:TPU:0, one launch (start us, length us, event | category | flops | bytes accessed | tf_op | source)
XLA Modules:
  0.0 198.9 jit_solution(2583756714033477710)
XLA Ops:
  6.5 0.7 all-gather.6.cloned.1.call-update
  7.3 0.0 all-gather.8.cloned.1.call-start
  7.3 0.7 all-gather.8.cloned.1.call-update
  8.0 0.0 all-gather.10.cloned.1.call-start
  8.1 0.7 all-gather.10.cloned.1.call-update
  8.8 0.0 all-gather.12.cloned.1.call-start
  8.8 0.5 all-gather.12.cloned.1.call-update
  9.3 0.6 copy-done.4
  9.9 0.3 multiply_reduce_fusion
  10.2 0.3 fusion.8
  10.5 0.0 copy-start.12
  10.5 3.8 %fusion.23 = f32[512,896]{1,0:T(8,128)} fusion(bf16[512,896]{1,0:T(8,128)(2,1)S(1)} %copy-done, bf16[512,896]{1,0:T(8,128)(2,1)S(1)} %fusion.8, bf16[896,512]{1,0:T(8,128)(2,1)} %param.15), kind=kOutput, calls=%fused_computation.34 | convolution fusion | flops 941883392 | bytes 4587520 | tf_op jit(solution)/shard_map/dot_general | solution.py:32
  14.3 1.2 dynamic-slice_bitcast_fusion
  15.6 0.5 collective-permute-start
  16.1 0.1 copy.23
  16.2 0.1 reshape.266
  16.3 0.3 convert_reduce_fusion
  16.6 0.1 select_reduce_fusion
  16.8 0.1 copy.24
  16.8 0.1 reshape.283
  16.9 2.0 all-gather
  18.9 1.5 bitcast_add_fusion
  20.5 2.9 %collective-permute-start.1 = (bf16[4,32,896]{2,1,0:T(8,128)(2,1)S(1)}, bf16[4,32,896]{2,1,0:T(8,128)(2,1)S(1)}, u32[]{:S(2)}, u32[]{:S(2)}) collective-permute-start(bf16[4,32,896]{2,1,0:T(8,128)(2,1)S(1)} %fusion.30), channel_id=1, source_target_pairs={{0,1},{1,0},{2,3},{3,2},{4,5},{5,4},{6,7},{7,6},{8,9},{9,8},{10,11... | collective-permute-start | bytes 688136 | tf_op jit(solution)/shard_map/ppermute | solution.py:22
  23.3 0.1 constant_dynamic-slice_fusion.4
  23.4 6.0 %collective-permute-done.1 = bf16[4,32,896]{2,1,0:T(8,128)(2,1)S(1)} collective-permute-done((bf16[4,32,896]{2,1,0:T(8,128)(2,1)S(1)}, bf16[4,32,896]{2,1,0:T(8,128)(2,1)S(1)}, u32[]{:S(2)}, u32[]{:S(2)}) %collective-permute-start.1) | collective-permute-done | bytes 229408 | tf_op jit(solution)/shard_map/ppermute | solution.py:22
  29.4 0.1 fusion.29
  29.5 1.6 gather_fusion
  31.1 6.1 %all-to-all-start = ((bf16[8,2,32,896]{3,2,1,0:T(8,128)(2,1)}), bf16[8,2,32,896]{3,2,1,0:T(8,128)(2,1)S(1)}, u32[]{:S(2)}, u32[]{:S(2)}) async-start(bf16[8,2,32,896]{3,2,1,0:T(8,128)(2,1)} %bitcast.12), calls=%async_computation | async-start | bytes 1835008 | tf_op jit(solution)/shard_map/all_to_all | solution.py:78
  37.2 1.6 collective-permute-start.2
  38.7 0.6 slice_bitcast_fusion.6
  39.4 0.1 add.161
  39.5 22.2 %collective-permute-done.2 = bf16[256,2048]{1,0:T(8,128)(2,1)} collective-permute-done((bf16[256,2048]{1,0:T(8,128)(2,1)S(1)}, bf16[256,2048]{1,0:T(8,128)(2,1)}, u32[]{:S(2)}, u32[]{:S(2)}) %collective-permute-start.2) | collective-permute-done | bytes 1048608 | tf_op jit(solution)/shard_map/ppermute | solution.py:22
  61.7 3.0 %fusion.1 = (f32[256]{0:T(256)S(1)}, bf16[256,4096]{1,0:T(8,128)(2,1)S(1)}) fusion(bf16[256,2048]{1,0:T(8,128)(2,1)} %copy-done.5, bf16[256,2048]{1,0:T(8,128)(2,1)} %collective-permute-done.2, pred[]{:T(512)S(6)} %eq.50), kind=kLoop, calls=%fused_computation.7 | loop fusion | flops 12582656 | bytes 4195329 | tf_op jit(solution)/shard_map/reduce_sum | solution.py:27
  64.7 0.0 all-gather.6.cloned.1.call-done.wq
  64.8 8.2 %fusion.12.q = bf16[256,1024]{1,0:T(8,128)(2,1)} fusion(bf16[2,4096,1024]{2,1,0:T(8,128)(2,1)} %all-gather.6.cloned.1.call-done.wq, bf16[256,4096]{1,0:T(8,128)(2,1)S(1)} %get-tuple-element.46.state, f32[4096]{0:T(1024)S(1)} %bitcast.105, f32[256]{0:T(256)S(1)} %add_rsqrt_fusion), kind=kOutput, calls=%fused_computation.19 | convolution fusion | flops 2152202240 | bytes 11027456 | tf_op jit(solution)/shard_map/dot_general | solution.py:32
  73.0 0.6 gather_fusion.2
  73.6 0.1 collective-permute-start.3
  73.7 0.6 gather_fusion.1
  74.3 1.2 collective-permute-done.3
  75.5 0.1 pad_maximum_fusion.1
  75.6 1.6 collective-permute-start.4
  77.2 5.6 %shard_map.109 = (bf16[512,1024]{1,0:T(8,128)(2,1)}, bf16[512,1024]{1,0:T(8,128)(2,1)}) custom-call(bf16[512,896]{1,0:T(8,128)(2,1)} %bitcast.77, bf16[2,896,1024]{2,1,0:T(8,128)(2,1)} %all-gather.8.cloned.1.call-done.wk, bf16[2,896,1024]{2,1,0:T(8,128)(2,1)} %all-gather.10.cloned.1.call-done.wv), custom_call_target="tpu_custom_call" | custom-call | flops 1879048192 | bytes 6684672 | tf_op jit(solution)/shard_map/pallas_call | solution.py:99
  82.7 15.3 %collective-permute-done.4.rows = bf16[512,896]{1,0:T(8,128)(2,1)S(1)} collective-permute-done((bf16[512,896]{1,0:T(8,128)(2,1)S(1)}, bf16[512,896]{1,0:T(8,128)(2,1)S(1)}, u32[]{:S(2)}, u32[]{:S(2)}) %collective-permute-start.4) | collective-permute-done | bytes 917536 | tf_op jit(solution)/shard_map/ppermute | solution.py:22
  98.0 1.0 copy-done.6
  99.0 5.5 %shard_map.110 = (bf16[512,1024]{1,0:T(8,128)(2,1)}, bf16[512,1024]{1,0:T(8,128)(2,1)}) custom-call(bf16[512,896]{1,0:T(8,128)(2,1)} %copy-done.6, bf16[2,896,1024]{2,1,0:T(8,128)(2,1)} %all-gather.8.cloned.1.call-done.wk, bf16[2,896,1024]{2,1,0:T(8,128)(2,1)} %all-gather.10.cloned.1.call-done.wv), custom_call_target="tpu_custom_call" | custom-call | flops 1879048192 | bytes 6684672 | tf_op jit(solution)/shard_map/pallas_call | solution.py:99
  104.5 1.4 all-gather.12.cloned.1.call-done.wo
  105.9 8.0 %shard_map.115 = (bf16[128,4096]{1,0:T(8,128)(2,1)}, f32[128,4096]{1,0:T(8,128)}) custom-call(bf16[256,1024]{1,0:T(8,128)(2,1)} %fusion.12.q, bf16[4,128,1024]{2,1,0:T(8,128)(2,1)} %bitcast.88, bf16[4,128,1024]{2,1,0:T(8,128)(2,1)} %bitcast.92, bf16[4,128,1024]{2,1,0:T(8,128)(2,1)} %bitcast.90, bf16[4,128,1024]{2,1,0:T(8,128)(2,1)} %bitcast.94, ...), custom_call_target="tpu_custom_call" | custom-call | flops 1207959552 | bytes 12582912 | tf_op jit(solution)/shard_map/pallas_call | solution.py:155
  114.0 1.8 collective-permute-start.7
  115.8 8.0 %shard_map.111 = (bf16[128,4096]{1,0:T(8,128)(2,1)}, f32[128,4096]{1,0:T(8,128)}) custom-call(bf16[256,1024]{1,0:T(8,128)(2,1)} %fusion.12.q, bf16[4,128,1024]{2,1,0:T(8,128)(2,1)} %bitcast.89, bf16[4,128,1024]{2,1,0:T(8,128)(2,1)} %bitcast.93, bf16[4,128,1024]{2,1,0:T(8,128)(2,1)} %bitcast.91, bf16[4,128,1024]{2,1,0:T(8,128)(2,1)} %bitcast.95, ...), custom_call_target="tpu_custom_call" | custom-call | flops 1207959552 | bytes 12582912 | tf_op jit(solution)/shard_map/pallas_call | solution.py:155
  123.8 0.2 collective-permute-start.5
  124.0 5.5 %shard_map.112 = (bf16[512,1024]{1,0:T(8,128)(2,1)}, bf16[512,1024]{1,0:T(8,128)(2,1)}) custom-call(bf16[512,896]{1,0:T(8,128)(2,1)} %bitcast.78, bf16[2,896,1024]{2,1,0:T(8,128)(2,1)} %all-gather.8.cloned.1.call-done.wk, bf16[2,896,1024]{2,1,0:T(8,128)(2,1)} %all-gather.10.cloned.1.call-done.wv), custom_call_target="tpu_custom_call" | custom-call | flops 1879048192 | bytes 6684672 | tf_op jit(solution)/shard_map/pallas_call | solution.py:99
  129.5 5.6 %shard_map.113 = (bf16[512,1024]{1,0:T(8,128)(2,1)}, bf16[512,1024]{1,0:T(8,128)(2,1)}) custom-call(bf16[512,896]{1,0:T(8,128)(2,1)} %copy-done.6, bf16[2,896,1024]{2,1,0:T(8,128)(2,1)} %all-gather.8.cloned.1.call-done.wk, bf16[2,896,1024]{2,1,0:T(8,128)(2,1)} %all-gather.10.cloned.1.call-done.wv), custom_call_target="tpu_custom_call" | custom-call | flops 1879048192 | bytes 6684672 | tf_op jit(solution)/shard_map/pallas_call | solution.py:99
  135.1 5.2 %collective-permute-done.7.arrived = bf16[128,4096]{1,0:T(8,128)(2,1)} collective-permute-done((bf16[128,4096]{1,0:T(8,128)(2,1)}, bf16[128,4096]{1,0:T(8,128)(2,1)}, u32[]{:S(2)}, u32[]{:S(2)}) %collective-permute-start.7) | collective-permute-done | bytes 1048608 | tf_op jit(solution)/shard_map/ppermute | solution.py:22
  140.3 14.6 %shard_map.116 = (bf16[128,2048]{1,0:T(8,128)(2,1)}, f32[128,2048]{1,0:T(8,128)}) custom-call(s32[1]{0:T(128)} %bitcast.mp, f32[128,4096]{1,0:T(8,128)} %get-tuple-element.41.base, bf16[128,4096]{1,0:T(8,128)(2,1)} %collective-permute-done.7.arrived, f32[1,4096]{1,0:T(1,128)} %get-tuple-element.49.gain, ...), custom_call_target="tpu_custom_call" | custom-call | flops 2147483648 | bytes 23068672 | tf_op jit(solution)/shard_map/pallas_call | solution.py:228
  154.9 1.9 collective-permute-start.8
  156.7 5.9 %collective-permute-done.5.arrived = bf16[128,4096]{1,0:T(8,128)(2,1)S(1)} collective-permute-done((bf16[128,4096]{1,0:T(8,128)(2,1)}, bf16[128,4096]{1,0:T(8,128)(2,1)S(1)}, u32[]{:S(2)}, u32[]{:S(2)}) %collective-permute-start.5) | collective-permute-done | bytes 1048608 | tf_op jit(solution)/shard_map/ppermute | solution.py:22
  162.7 0.9 copy-done.7
  163.6 14.5 %shard_map.114 = (bf16[128,2048]{1,0:T(8,128)(2,1)}, f32[128,2048]{1,0:T(8,128)}) custom-call(s32[1]{0:T(128)} %bitcast.mp, f32[128,4096]{1,0:T(8,128)} %get-tuple-element.33.base, bf16[128,4096]{1,0:T(8,128)(2,1)} %copy-done.7, f32[1,4096]{1,0:T(1,128)} %get-tuple-element.49.gain, bf16[2,4096,1024]{2,1,0:T(8,128)(2,1)} %all-gather.6.cloned.1.call-done.wq, ...), custom_call_target="tpu_custom_call" | custom-call | flops 2147483648 | bytes 23068672 | tf_op jit(solution)/shard_map/pallas_call | solution.py:228
  178.2 1.9 collective-permute-start.6
  180.1 1.3 add_convert_fusion
  181.4 9.7 %collective-permute-done.6 = bf16[128,2048]{1,0:T(8,128)(2,1)S(1)} collective-permute-done((bf16[128,2048]{1,0:T(8,128)(2,1)}, bf16[128,2048]{1,0:T(8,128)(2,1)S(1)}, u32[]{:S(2)}, u32[]{:S(2)}) %collective-permute-start.6) | collective-permute-done | bytes 524320 | tf_op jit(solution)/shard_map/ppermute | solution.py:22
  191.2 0.1 add_convert_fusion.1
  191.3 1.1 pad_maximum_fusion
  192.3 0.1 copy-done.1
  (39 shorter events, 0.2 us)
Async XLA Ops:
  6.5 3.9 %copy-start = (bf16[512,896]{1,0:T(8,128)(2,1)S(1)}, bf16[512,896]{1,0:T(8,128)(2,1)}, u32[]{:S(2)}) copy-start(bf16[512,896]{1,0:T(8,128)(2,1)} %param.16) | copy-start | bytes 2752516
  6.5 58.2 %all-gather.6.cloned.1.call-start = ((), (), s32[]{:S(2)}) async-start(), calls=%async_computation.1 | async-start | bytes 25165824 | tf_op jit(solution)/shard_map/all_gather | solution.py:298
  7.3 69.9 %all-gather.8.cloned.1.call-start = ((), (), s32[]{:S(2)}) async-start(), calls=%async_computation.2 | async-start | bytes 5505024 | tf_op jit(solution)/shard_map/all_gather | solution.py:299
  8.0 69.2 %all-gather.10.cloned.1.call-start = ((), (), s32[]{:S(2)}) async-start(), calls=%async_computation.3 | async-start | bytes 5505024 | tf_op jit(solution)/shard_map/all_gather | solution.py:300
  8.7 1.2 copy-start.4
  8.8 1.4 copy-start.11
  8.8 97.2 %all-gather.12.cloned.1.call-start = ((), (), s32[]{:S(2)}) async-start(), calls=%async_computation.4 | async-start | bytes 25165824 | tf_op jit(solution)/shard_map/all_gather | solution.py:301
  10.5 5.6 %copy-start.12 = (s32[64,2]{0,1:T(2,128)S(1)}, s32[64,2]{0,1:T(2,128)}, u32[]{:S(2)}) copy-start(s32[64,2]{0,1:T(2,128)} %param.13) | copy-start | bytes 1540
  10.5 6.4 %copy-start.10 = (f32[1,4096]{1,0:T(1,128)S(1)}, f32[1,4096]{1,0:T(1,128)}, u32[]{:S(2)}) copy-start(f32[1,4096]{1,0:T(1,128)} %param.17) | copy-start | bytes 49156
  15.6 3.3 %collective-permute-start = (f32[4,64,896]{2,1,0:T(8,128)S(1)}, f32[4,64,896]{2,1,0:T(8,128)S(1)}, u32[]{:S(2)}, u32[]{:S(2)}) collective-permute-start(f32[4,64,896]{2,1,0:T(8,128)S(1)} %dynamic-slice_bitcast_fusion), channel_id=1, source_target_pairs={{0,2},{2,0},{1,3},{3,1},{4,6},{6,4},{5,7},{7,5},{8,10},{10,8},{9,1... | collective-permute-start | bytes 2752520 | tf_op jit(solution)/shard_map/ppermute | solution.py:22
  16.9 6.4 %copy-start.9 = (bf16[512,2048]{1,0:T(8,128)(2,1)S(1)}, bf16[512,2048]{1,0:T(8,128)(2,1)}, u32[]{:S(2)}) copy-start(bf16[512,2048]{1,0:T(8,128)(2,1)} %param.11) | copy-start | bytes 6291460
  20.5 9.0 %collective-permute-start.1 = (bf16[4,32,896]{2,1,0:T(8,128)(2,1)S(1)}, bf16[4,32,896]{2,1,0:T(8,128)(2,1)S(1)}, u32[]{:S(2)}, u32[]{:S(2)}) collective-permute-start(bf16[4,32,896]{2,1,0:T(8,128)(2,1)S(1)} %fusion.30), channel_id=1, source_target_pairs={{0,1},{1,0},{2,3},{3,2},{4,5},{5,4},{6,7},{7,6},{8,9},{9,8},{10,11... | collective-permute-start | bytes 688136 | tf_op jit(solution)/shard_map/ppermute | solution.py:22
  23.4 13.7 %copy-start.5 = (bf16[256,2048]{1,0:T(8,128)(2,1)}, bf16[256,2048]{1,0:T(8,128)(2,1)S(1)}, u32[]{:S(2)}) copy-start(bf16[256,2048]{1,0:T(8,128)(2,1)S(1)} %constant_dynamic-slice_fusion.4) | copy-start | bytes 3145732
  31.1 41.9 %all-to-all-start = ((bf16[8,2,32,896]{3,2,1,0:T(8,128)(2,1)}), bf16[8,2,32,896]{3,2,1,0:T(8,128)(2,1)S(1)}, u32[]{:S(2)}, u32[]{:S(2)}) async-start(bf16[8,2,32,896]{3,2,1,0:T(8,128)(2,1)} %bitcast.12), calls=%async_computation | async-start | bytes 1835008 | tf_op jit(solution)/shard_map/all_to_all | solution.py:78
  37.2 24.5 %collective-permute-start.2 = (bf16[256,2048]{1,0:T(8,128)(2,1)S(1)}, bf16[256,2048]{1,0:T(8,128)(2,1)}, u32[]{:S(2)}, u32[]{:S(2)}) collective-permute-start(bf16[256,2048]{1,0:T(8,128)(2,1)S(1)} %constant_dynamic-slice_fusion.4), channel_id=1, source_target_pairs={{0,1},{1,0},{2,3},{3,2},{4,5},{5,4},{6,7},{7,6},{8,9},{9,8},{10,11... | collective-permute-start | bytes 3145736 | tf_op jit(solution)/shard_map/ppermute | solution.py:22
  64.7 8.3 %copy-start.2 = (bf16[256,4096]{1,0:T(8,128)(2,1)}, bf16[256,4096]{1,0:T(8,128)(2,1)S(1)}, u32[]{:S(2)}) copy-start(bf16[256,4096]{1,0:T(8,128)(2,1)S(1)} %get-tuple-element.46.state) | copy-start | bytes 6291460
  73.6 1.9 collective-permute-start.3
  75.6 1.6 copy-start.3
  75.6 22.5 %collective-permute-start.4 = (bf16[512,896]{1,0:T(8,128)(2,1)S(1)}, bf16[512,896]{1,0:T(8,128)(2,1)S(1)}, u32[]{:S(2)}, u32[]{:S(2)}) collective-permute-start(bf16[512,896]{1,0:T(8,128)(2,1)S(1)} %bitcast.76), channel_id=1, source_target_pairs={{0,1},{1,0},{2,3},{3,2},{4,5},{5,4},{6,7},{7,6},{8,9},{9,8},{10,11... | collective-permute-start | bytes 2752520 | tf_op jit(solution)/shard_map/ppermute | solution.py:22
  98.0 1.0 copy-start.6
  114.0 26.3 %collective-permute-start.7 = (bf16[128,4096]{1,0:T(8,128)(2,1)}, bf16[128,4096]{1,0:T(8,128)(2,1)}, u32[]{:S(2)}, u32[]{:S(2)}) collective-permute-start(bf16[128,4096]{1,0:T(8,128)(2,1)} %get-tuple-element.42), channel_id=1, source_target_pairs={{0,1},{1,0},{2,3},{3,2},{4,5},{5,4},{6,7},{7,6},{8,9},{9,8},{10,11... | collective-permute-start | bytes 3145736 | tf_op jit(solution)/shard_map/ppermute | solution.py:22
  123.8 38.9 %collective-permute-start.5 = (bf16[128,4096]{1,0:T(8,128)(2,1)}, bf16[128,4096]{1,0:T(8,128)(2,1)S(1)}, u32[]{:S(2)}, u32[]{:S(2)}) collective-permute-start(bf16[128,4096]{1,0:T(8,128)(2,1)} %get-tuple-element.34), channel_id=1, source_target_pairs={{0,1},{1,0},{2,3},{3,2},{4,5},{5,4},{6,7},{7,6},{8,9},{9,8},{10,11... | collective-permute-start | bytes 3145736 | tf_op jit(solution)/shard_map/ppermute | solution.py:22
  154.9 25.2 %collective-permute-start.8 = (bf16[128,2048]{1,0:T(8,128)(2,1)}, bf16[128,2048]{1,0:T(8,128)(2,1)S(1)}, u32[]{:S(2)}, u32[]{:S(2)}) collective-permute-start(bf16[128,2048]{1,0:T(8,128)(2,1)} %get-tuple-element.44), channel_id=1, source_target_pairs={{0,1},{1,0},{2,3},{3,2},{4,5},{5,4},{6,7},{7,6},{8,9},{9,8},{10,11... | collective-permute-start | bytes 1572872 | tf_op jit(solution)/shard_map/ppermute | solution.py:22
  162.7 1.0 copy-start.7
  178.2 13.0 %copy-start.8 = (f32[128,2048]{1,0:T(8,128)S(1)}, f32[128,2048]{1,0:T(8,128)}, u32[]{:S(2)}) copy-start(f32[128,2048]{1,0:T(8,128)} %get-tuple-element.39) | copy-start | bytes 3145732
  178.2 13.0 %collective-permute-start.6 = (bf16[128,2048]{1,0:T(8,128)(2,1)}, bf16[128,2048]{1,0:T(8,128)(2,1)S(1)}, u32[]{:S(2)}, u32[]{:S(2)}) collective-permute-start(bf16[128,2048]{1,0:T(8,128)(2,1)} %get-tuple-element.40), channel_id=1, source_target_pairs={{0,1},{1,0},{2,3},{3,2},{4,5},{5,4},{6,7},{7,6},{8,9},{9,8},{10,11... | collective-permute-start | bytes 1572872 | tf_op jit(solution)/shard_map/ppermute | solution.py:22
  191.2 1.3 copy-start.1
Sparse Core Ops, SparseCore 0:
  8.9 32.9 all-gather.5
  43.4 14.0 all-gather.7
  59.1 14.0 all-gather.9
  74.6 31.3 all-gather.11

commit v5 on v4

--- a/solution.py
+++ b/solution.py
@@ -20,6 +20,12 @@
 
 def swap(block, axis):
     return lax.ppermute(block, axis, [(0, 1), (1, 0)])
+
+
+def both_layers(own):
+    other = swap(own, "section")
+    first = lax.axis_index("section") == 0
+    return jnp.where(first, own, other), jnp.where(first, other, own)
 
 
 def rms_scale(rows_in, gain_vec):
@@ -76,13 +82,13 @@
     theirs = lax.dynamic_index_in_dim(slot_pick, 1 - section, 0, keepdims=False)
     payload = encoded[send_local]
     received = lax.all_to_all(payload, "db", split_axis=0, concat_axis=0, tiled=True)
-    received, fill = lax.optimization_barrier((received, fill))
     received = received.reshape(db_count * capacity, NBLOCK // 4, E)
     moved = swap(received[theirs], "section")
     groups = request // 2 // NEIGH
     near = jnp.concatenate(
         [received[mine].reshape(groups, -1, E), moved.reshape(groups, -1, E)], axis=1
     ).reshape(-1, E)
+    near, fill = lax.optimization_barrier((near, fill))
     return near, swap(near, "mp"), fill
 
 
@@ -91,10 +97,10 @@
     v[...] = mm(rows[...], wv[0]).astype(BF16)
 
 
-def keys_values(rows, wk, wv, layer):
+def keys_values(rows, wk, wv):
     count, out = rows.shape[0], wk.shape[2]
     tile = 256
-    weight = pl.BlockSpec((1, E, out), lambda i: (layer, 0, 0))
+    weight = pl.BlockSpec((1, E, out), lambda i: (0, 0, 0))
     made = pl.BlockSpec((tile, out), lambda i: (i, 0))
     k, v = pl.pallas_call(
         kv_kernel,
@@ -287,7 +293,9 @@
 
     entering = lax.dynamic_slice_in_dim(hidden_in, section * tokens, tokens, 0)
     encoded = encode_quarter(database, enc_gain, enc_up, enc_down)
-    encoded, entering = lax.optimization_barrier((encoded, entering))
+    encoded, entering, w_key, w_value = lax.optimization_barrier(
+        (encoded, entering, w_key, w_value)
+    )
     other = swap(entering, "mp")
     state = jnp.where(
         mp == 0,
@@ -296,17 +304,18 @@
     )
     gains = lax.all_gather(dec_gain, "section", axis=0, tiled=True)
     wq = lax.all_gather(w_query, "section", axis=0, tiled=True)
-    wk = lax.all_gather(w_key, "section", axis=0, tiled=True)
-    wv = lax.all_gather(w_value, "section", axis=0, tiled=True)
+    wk = both_layers(w_key)
+    wv = both_layers(w_value)
     wo = lax.all_gather(w_out, "section", axis=0, tiled=True)
 
+    rows_a, rows_b, state = fetch(encoded, neighbour_ids, state)
     normed = rms_scale(state.astype(F32), gains[0]).astype(BF16)
     q0 = (mm(normed, wq[0]) * HD ** (-0.5)).astype(BF16)
-    rows_a, rows_b, q0 = fetch(encoded, neighbour_ids, q0)
+    rows_b, q0 = lax.optimization_barrier((rows_b, q0))
 
     def around(layer):
-        ka, va = keys_values(rows_a, wk, wv, layer)
-        kb, vb = keys_values(rows_b, wk, wv, layer)
+        ka, va = keys_values(rows_a, wk[layer], wv[layer])
+        kb, vb = keys_values(rows_b, wk[layer], wv[layer])
         return ka, kb, va, vb
 
     kv0 = around(0)

time: 200 us -> 195 us (0.975)
  waiting for transfers between devices: 69.6 us -> 55.6 us
  other arithmetic: 8.28 us -> 18.7 us
    select_n x0 -> x3, other arithmetic: none -> 12.9 us  [the longest x2 8.99 us: both_layers(): return (jnp.where(first, own, other), jnp.where(first, other, own))]
    ppermute x9 -> x11, waiting for transfers between devices: 65.6 us -> 54.2 us  [swap(): return lax.ppermute(block, axis, [(0, 1), (1, 0)])]
    reduce_sum x2, other arithmetic: 3.3 us -> 0.75 us  [rms_scale(): jnp.mean(rows_in * rows_in, axis=-1, keepdims=True) + 1e-06]
    ppermute x9 -> x11, starting transfers between devices: 12.4 us -> 12.2 us  [swap(): return lax.ppermute(block, axis, [(0, 1), (1, 0)])]
  transfers between devices with their start and end apart: 14 -> 14, of which waited for: 8 -> 7; matrix products, arithmetic and copies ran while one was open for 12% -> 18% of each run, Pallas kernels for 30% -> 31%
where the time goes in v5:
time: 195 us; the launch traced here: 194 us
  Pallas kernels  67.4 us (35%)
  waiting for transfers between devices  55.6 us (29%)
  other arithmetic  18.7 us (10%)
  starting transfers between devices  18.3 us (9%)
  between operations  13.7 us (7%)
  matrix products  11 us (6%)
  local copies, waits for them, and re-layouts  7.56 us (4%)
  blocking collectives  1.98 us (1%)
    ppermute x11, waiting for transfers between devices, swap(): return lax.ppermute(block, axis, [(0, 1), (1, 0)])  54.2 us
    pallas_call x2, Pallas kernels, second_layer(): pl.pallas_call(functools.partial(second_kernel, blocks, q_steps, away), g...  29.1 us
    pallas_call x4, Pallas kernels, keys_values(): pl.pallas_call(kv_kernel, grid=(count // tile,), in_specs=[pl.BlockSpec((...  22.3 us
    pallas_call x2, Pallas kernels, first_layer(): pl.pallas_call(functools.partial(first_kernel, blocks, inner // HD), grid...  16 us
    ppermute x11, starting transfers between devices, swap(): return lax.ppermute(block, axis, [(0, 1), (1, 0)])  12.2 us
    dot_general x2, matrix products, mm(): return jnp.dot(a, b, preferred_element_type=F32)  11 us
    select_n x2, other arithmetic, both_layers(): return (jnp.where(first, own, other), jnp.where(first, other, own))  8.99 us
    all_to_all x1, starting transfers between devices, fetch(): lax.all_to_all(payload, 'db', split_axis=0, concat_axis=0, tiled=True)  6.08 us
  transfers between devices with their start and end apart: 14, of which 7 were waited for; matrix products, arithmetic and copies ran while one was open for 18% of the time, Pallas kernels for 31%

profile of v5, /device:TPU:0, one launch (start us, length us, event | category | flops | bytes accessed | tf_op | source)
XLA Modules:
  0.0 194.2 jit_solution(7579616862992561806)
XLA Ops:
  6.5 0.7 all-gather.4.cloned.1.call-update
  7.3 0.0 all-gather.6.cloned.1.call-start
  7.3 0.7 all-gather.6.cloned.1.call-update
  8.0 0.4 copy-done.3
  8.4 0.3 multiply_reduce_fusion
  8.7 0.3 fusion.8
  9.0 0.0 copy-start.12
  9.0 3.8 %fusion.23 = f32[512,896]{1,0:T(8,128)} fusion(bf16[512,896]{1,0:T(8,128)(2,1)S(1)} %copy-done, bf16[512,896]{1,0:T(8,128)(2,1)S(1)} %fusion.8, bf16[896,512]{1,0:T(8,128)(2,1)} %param.15), kind=kOutput, calls=%fused_computation.38 | convolution fusion | flops 941883392 | bytes 4587520 | tf_op jit(solution)/shard_map/dot_general | solution.py:38
  12.8 1.2 dynamic-slice_bitcast_fusion
  14.1 0.5 collective-permute-start
  14.6 0.1 copy.23
  14.7 0.1 reshape.266
  14.8 0.3 convert_reduce_fusion
  15.1 0.1 add.159
  15.2 0.2 select_reduce_fusion
  15.4 0.1 copy.24
  15.4 0.1 reshape.283
  15.5 1.2 collective-permute-done
  16.7 1.5 bitcast_add_fusion
  18.2 2.9 %collective-permute-start.1 = (bf16[4,32,896]{2,1,0:T(8,128)(2,1)S(1)}, bf16[4,32,896]{2,1,0:T(8,128)(2,1)S(1)}, u32[]{:S(2)}, u32[]{:S(2)}) collective-permute-start(bf16[4,32,896]{2,1,0:T(8,128)(2,1)S(1)} %fusion.30), channel_id=1, source_target_pairs={{0,1},{1,0},{2,3},{3,2},{4,5},{5,4},{6,7},{7,6},{8,9},{9,8},{10,11... | collective-permute-start | bytes 688136 | tf_op jit(solution)/shard_map/ppermute | solution.py:22
  21.1 0.1 constant_dynamic-slice_fusion.4
  21.2 0.0 copy-start.4
  21.3 5.8 %collective-permute-done.1 = bf16[4,32,896]{2,1,0:T(8,128)(2,1)S(1)} collective-permute-done((bf16[4,32,896]{2,1,0:T(8,128)(2,1)S(1)}, bf16[4,32,896]{2,1,0:T(8,128)(2,1)S(1)}, u32[]{:S(2)}, u32[]{:S(2)}) %collective-permute-start.1) | collective-permute-done | bytes 229408 | tf_op jit(solution)/shard_map/ppermute | solution.py:22
  27.0 0.1 fusion.29
  27.1 0.0 copy-start.10
  27.1 0.1 collective-permute-start.5
  27.3 1.6 gather_fusion
  28.9 6.1 %all-to-all-start = ((bf16[8,2,32,896]{3,2,1,0:T(8,128)(2,1)}), bf16[8,2,32,896]{3,2,1,0:T(8,128)(2,1)S(1)}, u32[]{:S(2)}, u32[]{:S(2)}) async-start(bf16[8,2,32,896]{3,2,1,0:T(8,128)(2,1)} %bitcast.12), calls=%async_computation | async-start | bytes 1835008 | tf_op jit(solution)/shard_map/all_to_all | solution.py:84
  35.0 1.6 collective-permute-start.3
  36.6 2.0 %all-gather = f32[2,1,4096]{2,1,0:T(1,128)S(1)} all-gather(f32[1,1,4096]{2,1,0:T(1,128)S(1)} %bitcast.104), channel_id=1, replica_groups=mesh['db'=8,'section'=2,'mp'=2] {'section'}, dimensions={0}, use_global_device_ids=true | all-gather | bytes 49152 | tf_op jit(solution)/shard_map/all_gather | solution.py:305
  38.6 0.6 slice_bitcast_fusion.6
  39.2 21.2 %collective-permute-done.3 = bf16[256,2048]{1,0:T(8,128)(2,1)} collective-permute-done((bf16[256,2048]{1,0:T(8,128)(2,1)S(1)}, bf16[256,2048]{1,0:T(8,128)(2,1)}, u32[]{:S(2)}, u32[]{:S(2)}) %collective-permute-start.3) | collective-permute-done | bytes 1048608 | tf_op jit(solution)/shard_map/ppermute | solution.py:22
  60.4 3.9 %maximum_select_fusion.state = bf16[256,4096]{1,0:T(8,128)(2,1)S(1)} fusion(bf16[256,2048]{1,0:T(8,128)(2,1)} %collective-permute-done.3, bf16[256,2048]{1,0:T(8,128)(2,1)} %copy-done.4, pred[]{:T(512)S(6)} %eq.54), kind=kLoop, calls=%fused_computation.10 | loop fusion | flops 9437184 | bytes 4194305 | tf_op jit(solution)/shard_map/jit(_where)/select_n | solution.py:300
  64.3 1.4 gather_fusion.2
  65.8 0.6 gather_fusion.1
  66.4 0.0 copy-start.5
  66.4 0.1 collective-permute-start.2
  66.5 5.4 %broadcast_select_fusion.1 = (bf16[1,896,1024]{2,1,0:T(8,128)(2,1)}, bf16[1,896,1024]{2,1,0:T(8,128)(2,1)}) fusion(bf16[1,896,1024]{2,1,0:T(8,128)(2,1)} %collective-permute-done.5, bf16[1,896,1024]{2,1,0:T(8,128)(2,1)} %param.19, pred[]{:T(512)S(6)} %eq.55), kind=kLoop, calls=%fused_computation.18 | loop fusion | flops 1835008 | bytes 7340033 | tf_op jit(solution)/shard_map/jit(_where)/select_n | solution.py:28
  71.9 3.6 %broadcast_select_fusion = (bf16[1,896,1024]{2,1,0:T(8,128)(2,1)}, bf16[1,896,1024]{2,1,0:T(8,128)(2,1)}) fusion(bf16[1,896,1024]{2,1,0:T(8,128)(2,1)} %collective-permute-done.6, bf16[1,896,1024]{2,1,0:T(8,128)(2,1)S(1)} %copy-done.5, pred[]{:T(512)S(6)} %eq.55), kind=kLoop, calls=%fused_computation.17 | loop fusion | flops 1835008 | bytes 7340033 | tf_op jit(solution)/shard_map/jit(_where)/select_n | solution.py:28
  75.5 0.1 pad_maximum_fusion.1
  75.6 1.7 collective-permute-start.4
  77.4 0.5 fusion.1
  77.9 5.7 %shard_map.109 = (bf16[512,1024]{1,0:T(8,128)(2,1)}, bf16[512,1024]{1,0:T(8,128)(2,1)}) custom-call(bf16[512,896]{1,0:T(8,128)(2,1)} %bitcast.101, bf16[1,896,1024]{2,1,0:T(8,128)(2,1)} %get-tuple-element.58.wk, bf16[1,896,1024]{2,1,0:T(8,128)(2,1)} %get-tuple-element.56.wv), custom_call_target="tpu_custom_call" | custom-call | flops 1879048192 | bytes 6684672 | tf_op jit(solution)/shard_map/pallas_call | solution.py:105
  83.6 7.2 %fusion.12.q = bf16[256,1024]{1,0:T(8,128)(2,1)} fusion(bf16[2,4096,1024]{2,1,0:T(8,128)(2,1)} %all-gather.4.cloned.1.call-done.wq, bf16[256,4096]{1,0:T(8,128)(2,1)} %copy-done.2, f32[4096]{0:T(1024)S(1)} %bitcast.105, f32[256]{0:T(256)S(1)} %add_rsqrt_fusion), kind=kOutput, calls=%fused_computation.23 | convolution fusion | flops 2152202240 | bytes 11027456 | tf_op jit(solution)/shard_map/dot_general | solution.py:38
  90.8 7.2 %collective-permute-done.4.rows = bf16[512,896]{1,0:T(8,128)(2,1)} collective-permute-done((bf16[512,896]{1,0:T(8,128)(2,1)S(1)}, bf16[512,896]{1,0:T(8,128)(2,1)}, u32[]{:S(2)}, u32[]{:S(2)}) %collective-permute-start.4) | collective-permute-done | bytes 917536 | tf_op jit(solution)/shard_map/ppermute | solution.py:22
  98.0 5.5 %shard_map.110 = (bf16[512,1024]{1,0:T(8,128)(2,1)}, bf16[512,1024]{1,0:T(8,128)(2,1)}) custom-call(bf16[512,896]{1,0:T(8,128)(2,1)} %collective-permute-done.4.rows, bf16[1,896,1024]{2,1,0:T(8,128)(2,1)} %get-tuple-element.58.wk, bf16[1,896,1024]{2,1,0:T(8,128)(2,1)} %get-tuple-element.56.wv), custom_call_target="tpu_custom_call" | custom-call | flops 1879048192 | bytes 6684672 | tf_op jit(solution)/shard_map/pallas_call | solution.py:105
  103.5 8.0 %shard_map.115 = (bf16[128,4096]{1,0:T(8,128)(2,1)}, f32[128,4096]{1,0:T(8,128)}) custom-call(bf16[256,1024]{1,0:T(8,128)(2,1)} %fusion.12.q, bf16[4,128,1024]{2,1,0:T(8,128)(2,1)} %bitcast.85, bf16[4,128,1024]{2,1,0:T(8,128)(2,1)} %bitcast.89, bf16[4,128,1024]{2,1,0:T(8,128)(2,1)} %bitcast.87, bf16[4,128,1024]{2,1,0:T(8,128)(2,1)} %bitcast.91, ...), custom_call_target="tpu_custom_call" | custom-call | flops 1207959552 | bytes 12582912 | tf_op jit(solution)/shard_map/pallas_call | solution.py:161
  111.5 1.6 collective-permute-start.9
  113.1 8.0 %shard_map.111 = (bf16[128,4096]{1,0:T(8,128)(2,1)}, f32[128,4096]{1,0:T(8,128)}) custom-call(bf16[256,1024]{1,0:T(8,128)(2,1)} %fusion.12.q, bf16[4,128,1024]{2,1,0:T(8,128)(2,1)} %bitcast.86, bf16[4,128,1024]{2,1,0:T(8,128)(2,1)} %bitcast.90, bf16[4,128,1024]{2,1,0:T(8,128)(2,1)} %bitcast.88, bf16[4,128,1024]{2,1,0:T(8,128)(2,1)} %bitcast.92, ...), custom_call_target="tpu_custom_call" | custom-call | flops 1207959552 | bytes 12582912 | tf_op jit(solution)/shard_map/pallas_call | solution.py:161
  121.1 0.4 collective-permute-start.7
  121.5 5.5 %shard_map.112 = (bf16[512,1024]{1,0:T(8,128)(2,1)}, bf16[512,1024]{1,0:T(8,128)(2,1)}) custom-call(bf16[512,896]{1,0:T(8,128)(2,1)} %bitcast.102, bf16[1,896,1024]{2,1,0:T(8,128)(2,1)} %get-tuple-element.57.wk, bf16[1,896,1024]{2,1,0:T(8,128)(2,1)} %get-tuple-element.55.wv), custom_call_target="tpu_custom_call" | custom-call | flops 1879048192 | bytes 6684672 | tf_op jit(solution)/shard_map/pallas_call | solution.py:105
  127.1 5.5 %shard_map.113 = (bf16[512,1024]{1,0:T(8,128)(2,1)}, bf16[512,1024]{1,0:T(8,128)(2,1)}) custom-call(bf16[512,896]{1,0:T(8,128)(2,1)} %collective-permute-done.4.rows, bf16[1,896,1024]{2,1,0:T(8,128)(2,1)} %get-tuple-element.57.wk, bf16[1,896,1024]{2,1,0:T(8,128)(2,1)} %get-tuple-element.55.wv), custom_call_target="tpu_custom_call" | custom-call | flops 1879048192 | bytes 6684672 | tf_op jit(solution)/shard_map/pallas_call | solution.py:105
  132.6 5.3 %collective-permute-done.9.arrived = bf16[128,4096]{1,0:T(8,128)(2,1)} collective-permute-done((bf16[128,4096]{1,0:T(8,128)(2,1)}, bf16[128,4096]{1,0:T(8,128)(2,1)}, u32[]{:S(2)}, u32[]{:S(2)}) %collective-permute-start.9) | collective-permute-done | bytes 1048608 | tf_op jit(solution)/shard_map/ppermute | solution.py:22
  137.9 14.6 %shard_map.116 = (bf16[128,2048]{1,0:T(8,128)(2,1)}, f32[128,2048]{1,0:T(8,128)}) custom-call(s32[1]{0:T(128)} %bitcast.mp, f32[128,4096]{1,0:T(8,128)} %get-tuple-element.49.base, bf16[128,4096]{1,0:T(8,128)(2,1)} %collective-permute-done.9.arrived, f32[1,4096]{1,0:T(1,128)} %get-tuple-element.59.gain, ...), custom_call_target="tpu_custom_call" | custom-call | flops 2147483648 | bytes 23068672 | tf_op jit(solution)/shard_map/pallas_call | solution.py:234
  152.5 1.6 collective-permute-start.10
  154.1 6.2 %collective-permute-done.7.arrived = bf16[128,4096]{1,0:T(8,128)(2,1)S(1)} collective-permute-done((bf16[128,4096]{1,0:T(8,128)(2,1)}, bf16[128,4096]{1,0:T(8,128)(2,1)S(1)}, u32[]{:S(2)}, u32[]{:S(2)}) %collective-permute-start.7) | collective-permute-done | bytes 1048608 | tf_op jit(solution)/shard_map/ppermute | solution.py:22
  160.3 1.0 copy-done.6
  161.3 14.5 %shard_map.114 = (bf16[128,2048]{1,0:T(8,128)(2,1)}, f32[128,2048]{1,0:T(8,128)}) custom-call(s32[1]{0:T(128)} %bitcast.mp, f32[128,4096]{1,0:T(8,128)} %get-tuple-element.41.base, bf16[128,4096]{1,0:T(8,128)(2,1)} %copy-done.6, f32[1,4096]{1,0:T(1,128)} %get-tuple-element.59.gain, bf16[2,4096,1024]{2,1,0:T(8,128)(2,1)} %all-gather.4.cloned.1.call-done.wq, ...), custom_call_target="tpu_custom_call" | custom-call | flops 2147483648 | bytes 23068672 | tf_op jit(solution)/shard_map/pallas_call | solution.py:234
  175.8 1.7 collective-permute-start.8
  177.5 1.3 add_convert_fusion
  178.8 7.3 %collective-permute-done.8 = bf16[128,2048]{1,0:T(8,128)(2,1)S(1)} collective-permute-done((bf16[128,2048]{1,0:T(8,128)(2,1)}, bf16[128,2048]{1,0:T(8,128)(2,1)S(1)}, u32[]{:S(2)}, u32[]{:S(2)}) %collective-permute-start.8) | collective-permute-done | bytes 524320 | tf_op jit(solution)/shard_map/ppermute | solution.py:22
  186.1 0.1 add_convert_fusion.1
  186.2 1.1 pad_maximum_fusion
  187.3 0.1 copy-done.1
  (40 shorter events, 0.2 us)
Async XLA Ops:
  6.5 2.5 %copy-start = (bf16[512,896]{1,0:T(8,128)(2,1)S(1)}, bf16[512,896]{1,0:T(8,128)(2,1)}, u32[]{:S(2)}) copy-start(bf16[512,896]{1,0:T(8,128)(2,1)} %param.16) | copy-start | bytes 2752516
  6.5 77.1 %all-gather.4.cloned.1.call-start = ((), (), s32[]{:S(2)}) async-start(), calls=%async_computation.1 | async-start | bytes 25165824 | tf_op jit(solution)/shard_map/all_gather | solution.py:306
  7.3 1.2 copy-start.3
  7.3 1.4 copy-start.11
  7.3 96.2 %all-gather.6.cloned.1.call-start = ((), (), s32[]{:S(2)}) async-start(), calls=%async_computation.2 | async-start | bytes 25165824 | tf_op jit(solution)/shard_map/all_gather | solution.py:309
  9.0 5.6 %copy-start.12 = (s32[64,2]{0,1:T(2,128)S(1)}, s32[64,2]{0,1:T(2,128)}, u32[]{:S(2)}) copy-start(s32[64,2]{0,1:T(2,128)} %param.13) | copy-start | bytes 1540
  14.1 2.6 %collective-permute-start = (f32[4,64,896]{2,1,0:T(8,128)S(1)}, f32[4,64,896]{2,1,0:T(8,128)S(1)}, u32[]{:S(2)}, u32[]{:S(2)}) collective-permute-start(f32[4,64,896]{2,1,0:T(8,128)S(1)} %dynamic-slice_bitcast_fusion), channel_id=1, source_target_pairs={{0,2},{2,0},{1,3},{3,1},{4,6},{6,4},{5,7},{7,5},{8,10},{10,8},{9,1... | collective-permute-start | bytes 2752520 | tf_op jit(solution)/shard_map/ppermute | solution.py:22
  15.5 5.6 %copy-start.9 = (bf16[512,2048]{1,0:T(8,128)(2,1)S(1)}, bf16[512,2048]{1,0:T(8,128)(2,1)}, u32[]{:S(2)}) copy-start(bf16[512,2048]{1,0:T(8,128)(2,1)} %param.11) | copy-start | bytes 6291460
  18.2 8.8 %collective-permute-start.1 = (bf16[4,32,896]{2,1,0:T(8,128)(2,1)S(1)}, bf16[4,32,896]{2,1,0:T(8,128)(2,1)S(1)}, u32[]{:S(2)}, u32[]{:S(2)}) collective-permute-start(bf16[4,32,896]{2,1,0:T(8,128)(2,1)S(1)} %fusion.30), channel_id=1, source_target_pairs={{0,1},{1,0},{2,3},{3,2},{4,5},{5,4},{6,7},{7,6},{8,9},{9,8},{10,11... | collective-permute-start | bytes 688136 | tf_op jit(solution)/shard_map/ppermute | solution.py:22
  21.2 13.7 %copy-start.4 = (bf16[256,2048]{1,0:T(8,128)(2,1)}, bf16[256,2048]{1,0:T(8,128)(2,1)S(1)}, u32[]{:S(2)}) copy-start(bf16[256,2048]{1,0:T(8,128)(2,1)S(1)} %constant_dynamic-slice_fusion.4) | copy-start | bytes 3145732
  27.1 9.4 %copy-start.10 = (f32[1,4096]{1,0:T(1,128)S(1)}, f32[1,4096]{1,0:T(1,128)}, u32[]{:S(2)}) copy-start(f32[1,4096]{1,0:T(1,128)} %param.17) | copy-start | bytes 49156
  27.1 39.4 %collective-permute-start.5 = (bf16[1,896,1024]{2,1,0:T(8,128)(2,1)}, bf16[1,896,1024]{2,1,0:T(8,128)(2,1)}, u32[]{:S(2)}, u32[]{:S(2)}) collective-permute-start(bf16[1,896,1024]{2,1,0:T(8,128)(2,1)} %param.19), channel_id=1, source_target_pairs={{0,2},{2,0},{1,3},{3,1},{4,6},{6,4},{5,7},{7,5},{8,10},{10,8},{9,1... | collective-permute-start | bytes 5505032 | tf_op jit(solution)/shard_map/ppermute | solution.py:22
  28.9 35.5 %all-to-all-start = ((bf16[8,2,32,896]{3,2,1,0:T(8,128)(2,1)}), bf16[8,2,32,896]{3,2,1,0:T(8,128)(2,1)S(1)}, u32[]{:S(2)}, u32[]{:S(2)}) async-start(bf16[8,2,32,896]{3,2,1,0:T(8,128)(2,1)} %bitcast.12), calls=%async_computation | async-start | bytes 1835008 | tf_op jit(solution)/shard_map/all_to_all | solution.py:84
  35.0 25.4 %collective-permute-start.3 = (bf16[256,2048]{1,0:T(8,128)(2,1)S(1)}, bf16[256,2048]{1,0:T(8,128)(2,1)}, u32[]{:S(2)}, u32[]{:S(2)}) collective-permute-start(bf16[256,2048]{1,0:T(8,128)(2,1)S(1)} %constant_dynamic-slice_fusion.4), channel_id=1, source_target_pairs={{0,1},{1,0},{2,3},{3,2},{4,5},{5,4},{6,7},{7,6},{8,9},{9,8},{10,11... | collective-permute-start | bytes 3145736 | tf_op jit(solution)/shard_map/ppermute | solution.py:22
  36.5 35.4 %collective-permute-start.6 = (bf16[1,896,1024]{2,1,0:T(8,128)(2,1)}, bf16[1,896,1024]{2,1,0:T(8,128)(2,1)}, u32[]{:S(2)}, u32[]{:S(2)}) collective-permute-start(bf16[1,896,1024]{2,1,0:T(8,128)(2,1)} %param.20), channel_id=1, source_target_pairs={{0,2},{2,0},{1,3},{3,1},{4,6},{6,4},{5,7},{7,5},{8,10},{10,8},{9,1... | collective-permute-start | bytes 5505032 | tf_op jit(solution)/shard_map/ppermute | solution.py:22
  64.3 13.0 %copy-start.2 = (bf16[256,4096]{1,0:T(8,128)(2,1)}, bf16[256,4096]{1,0:T(8,128)(2,1)S(1)}, u32[]{:S(2)}) copy-start(bf16[256,4096]{1,0:T(8,128)(2,1)S(1)} %maximum_select_fusion.state) | copy-start | bytes 6291460
  66.4 5.5 %copy-start.5 = (bf16[1,896,1024]{2,1,0:T(8,128)(2,1)S(1)}, bf16[1,896,1024]{2,1,0:T(8,128)(2,1)}, u32[]{:S(2)}) copy-start(bf16[1,896,1024]{2,1,0:T(8,128)(2,1)} %param.20) | copy-start | bytes 5505028
  66.4 9.1 %collective-permute-start.2 = (bf16[8,32,896]{2,1,0:T(8,128)(2,1)}, bf16[8,32,896]{2,1,0:T(8,128)(2,1)S(1)}, u32[]{:S(2)}, u32[]{:S(2)}) collective-permute-start(bf16[8,32,896]{2,1,0:T(8,128)(2,1)} %gather_fusion.2), channel_id=1, source_target_pairs={{0,2},{2,0},{1,3},{3,1},{4,6},{6,4},{5,7},{7,5},{8,10},{10,8},{9,1... | collective-permute-start | bytes 1376264 | tf_op jit(solution)/shard_map/ppermute | solution.py:22
  75.6 2.3 %copy-start.8 = (bf16[4,128,896]{2,1,0:T(8,128)(2,1)}, bf16[4,128,896]{2,1,0:T(8,128)(2,1)S(1)}, u32[]{:S(2)}) copy-start(bf16[4,128,896]{2,1,0:T(8,128)(2,1)S(1)} %pad_maximum_fusion.1) | copy-start | bytes 2752516
  75.6 22.4 %collective-permute-start.4 = (bf16[512,896]{1,0:T(8,128)(2,1)S(1)}, bf16[512,896]{1,0:T(8,128)(2,1)}, u32[]{:S(2)}, u32[]{:S(2)}) collective-permute-start(bf16[512,896]{1,0:T(8,128)(2,1)S(1)} %bitcast.100), channel_id=1, source_target_pairs={{0,1},{1,0},{2,3},{3,2},{4,5},{5,4},{6,7},{7,6},{8,9},{9,8},{10,11... | collective-permute-start | bytes 2752520 | tf_op jit(solution)/shard_map/ppermute | solution.py:22
  111.5 26.4 %collective-permute-start.9 = (bf16[128,4096]{1,0:T(8,128)(2,1)}, bf16[128,4096]{1,0:T(8,128)(2,1)}, u32[]{:S(2)}, u32[]{:S(2)}) collective-permute-start(bf16[128,4096]{1,0:T(8,128)(2,1)} %get-tuple-element.50), channel_id=1, source_target_pairs={{0,1},{1,0},{2,3},{3,2},{4,5},{5,4},{6,7},{7,6},{8,9},{9,8},{10,11... | collective-permute-start | bytes 3145736 | tf_op jit(solution)/shard_map/ppermute | solution.py:22
  121.1 39.2 %collective-permute-start.7 = (bf16[128,4096]{1,0:T(8,128)(2,1)}, bf16[128,4096]{1,0:T(8,128)(2,1)S(1)}, u32[]{:S(2)}, u32[]{:S(2)}) collective-permute-start(bf16[128,4096]{1,0:T(8,128)(2,1)} %get-tuple-element.42), channel_id=1, source_target_pairs={{0,1},{1,0},{2,3},{3,2},{4,5},{5,4},{6,7},{7,6},{8,9},{9,8},{10,11... | collective-permute-start | bytes 3145736 | tf_op jit(solution)/shard_map/ppermute | solution.py:22
  152.5 25.0 %collective-permute-start.10 = (bf16[128,2048]{1,0:T(8,128)(2,1)}, bf16[128,2048]{1,0:T(8,128)(2,1)S(1)}, u32[]{:S(2)}, u32[]{:S(2)}) collective-permute-start(bf16[128,2048]{1,0:T(8,128)(2,1)} %get-tuple-element.52), channel_id=1, source_target_pairs={{0,1},{1,0},{2,3},{3,2},{4,5},{5,4},{6,7},{7,6},{8,9},{9,8},{10,11... | collective-permute-start | bytes 1572872 | tf_op jit(solution)/shard_map/ppermute | solution.py:22
  160.3 1.0 copy-start.6
  175.8 10.3 %copy-start.7 = (f32[128,2048]{1,0:T(8,128)S(1)}, f32[128,2048]{1,0:T(8,128)}, u32[]{:S(2)}) copy-start(f32[128,2048]{1,0:T(8,128)} %get-tuple-element.47) | copy-start | bytes 3145732
  175.8 10.3 %collective-permute-start.8 = (bf16[128,2048]{1,0:T(8,128)(2,1)}, bf16[128,2048]{1,0:T(8,128)(2,1)S(1)}, u32[]{:S(2)}, u32[]{:S(2)}) collective-permute-start(bf16[128,2048]{1,0:T(8,128)(2,1)} %get-tuple-element.48), channel_id=1, source_target_pairs={{0,1},{1,0},{2,3},{3,2},{4,5},{5,4},{6,7},{7,6},{8,9},{9,8},{10,11... | collective-permute-start | bytes 1572872 | tf_op jit(solution)/shard_map/ppermute | solution.py:22
  186.1 1.3 copy-start.1
Sparse Core Ops, SparseCore 0:
  8.9 36.8 all-gather.3
  47.3 31.5 all-gather.5
